TPU v7x, 512 devices: a whole 4x8x8 slice. The times are simulated.
512 devices in a mesh: dp: 32 (over x, y), seq: 16 (over z, core).
Axes of the slice: x: 4, y: 8, z: 8, core: 2. Of those that a mesh axis runs over, the one named last changes fastest.
Arguments:
- volume: bfloat16 [32, 3072, 1024], P('dp', 'seq')
- cotangent: bfloat16 [32, 3072, 1024], P('dp', 'seq'), may hold values from -6 to 6
- weights: bfloat16 [1024, 3, 1024], P('dp')
- pairs: int32 [32, 16, 24, 4], P('dp', 'seq'), may hold values from 0 to 23, as said below
- valid: int32 [32, 16, 24, 4], P('dp', 'seq'), may hold values from 0 to 1, as said below
Outputs:
- attended: bfloat16 [32, 3072, 1024], P('dp', 'seq')
- weight_grad: float32 [1024, 3, 1024], P('dp', None, 'seq')
Inputs may be any that keep to these rules, and one draw needn't show every extreme that they name: `pairs`: slot 0 of query block b holds b; the key blocks of one query block's slots are distinct. `valid`: slot 0 is always 1.
All inputs are finite; a program needn't handle non-finite values.
Results may differ from a plain program's by a relative error of at most 0.03.
Values may be sent and summed in bfloat16 or wider, within the bound.
No kernel may reach another device: no remote copies, remote signals or barrier semaphores. Data moves between devices by JAX's collectives and lax.ppermute only.
A program may use at most 64 MiB of HBM per device.

v0:
```python
import math

import jax
import jax.numpy as jnp
from jax import lax
from jax.sharding import PartitionSpec as P

HD = 64


def head_pass(queries, keys_all, values_all, upstream, pair_list, pair_live):
    block_count, slot_count = pair_list.shape
    all_rows, head_size = queries.shape
    block_rows = all_rows // block_count
    per_step = math.gcd(block_count, max(1, 512 // block_rows))
    steps_n = block_count // per_step
    scaling = head_size ** (-0.5)
    key_blocks = keys_all.reshape(block_count, block_rows, head_size)
    value_blocks = values_all.reshape(block_count, block_rows, head_size)
    block_index = jnp.arange(block_count, dtype=jnp.int32)

    def step(totals, sliced):
        key_total, value_total = totals
        query_rows, grad_rows, slot_blocks, slot_live = sliced
        key_rows = key_blocks[slot_blocks].reshape(per_step, slot_count * block_rows, head_size)
        value_rows = value_blocks[slot_blocks].reshape(per_step, slot_count * block_rows, head_size)
        live_cols = jnp.repeat(slot_live > 0, block_rows, axis=1)[:, None, :]
        scores = (
            jnp.einsum("nqd,nkd->nqk", query_rows, key_rows, preferred_element_type=jnp.float32)
            * scaling
        )
        row_max = jnp.max(jnp.where(live_cols, scores, -1e30), axis=-1, keepdims=True)
        exponent = jnp.where(live_cols, jnp.exp(scores - row_max), 0.0)
        prob_full = exponent / jnp.sum(exponent, axis=-1, keepdims=True)
        rounded = prob_full.astype(jnp.bfloat16)
        result = jnp.einsum(
            "nqk,nkd->nqd", rounded, value_rows, preferred_element_type=jnp.float32
        ).astype(jnp.bfloat16)
        value_grad = jnp.einsum(
            "nqk,nqd->nkd", rounded, grad_rows, preferred_element_type=jnp.float32
        )
        prob_grad = jnp.einsum(
            "nqd,nkd->nqk", grad_rows, value_rows, preferred_element_type=jnp.float32
        )
        row_dot = jnp.sum(
            grad_rows.astype(jnp.float32) * result.astype(jnp.float32), axis=-1, keepdims=True
        )
        score_grad = (prob_full * (prob_grad - row_dot) * scaling).astype(jnp.bfloat16)
        query_grad = jnp.einsum(
            "nqk,nkd->nqd", score_grad, key_rows, preferred_element_type=jnp.float32
        ).astype(jnp.bfloat16)
        key_grad = jnp.einsum(
            "nqk,nqd->nkd", score_grad, query_rows, preferred_element_type=jnp.float32
        )
        one_hot = (
            (slot_blocks.reshape(-1)[:, None] == block_index[None, :])
            & (slot_live.reshape(-1)[:, None] > 0)
        ).astype(jnp.float32)
        key_total = key_total + jnp.einsum(
            "jb,jrd->brd",
            one_hot,
            key_grad.reshape(per_step * slot_count, block_rows, head_size),
            precision=lax.Precision.HIGHEST,
        )
        value_total = value_total + jnp.einsum(
            "jb,jrd->brd",
            one_hot,
            value_grad.reshape(per_step * slot_count, block_rows, head_size),
            precision=lax.Precision.HIGHEST,
        )
        return ((key_total, value_total), (result, query_grad))

    empty_acc = jnp.zeros((block_count, block_rows, head_size), jnp.float32)
    sliced_all = (
        queries.reshape(steps_n, per_step, block_rows, head_size),
        upstream.reshape(steps_n, per_step, block_rows, head_size),
        pair_list.reshape(steps_n, per_step, slot_count),
        pair_live.reshape(steps_n, per_step, slot_count),
    )
    (key_total, value_total), (results, query_grads) = lax.scan(
        step, (empty_acc, empty_acc), sliced_all
    )
    return (
        results.reshape(all_rows, head_size),
        query_grads.reshape(all_rows, head_size),
        key_total.astype(jnp.bfloat16).reshape(all_rows, head_size),
        value_total.astype(jnp.bfloat16).reshape(all_rows, head_size),
    )


def local(volume, cotangent, weights, pairs, valid):
    seq_devices = lax.axis_size("seq")
    local_volume = volume[0]
    local_grad = cotangent[0]
    tok_count = local_volume.shape[0]
    width_all = local_grad.shape[1]
    local_cols = width_all // seq_devices
    all_rows = tok_count * seq_devices
    projected = jnp.einsum(
        "td,djc->tjc",
        local_volume,
        lax.all_gather(weights, "dp", axis=0, tiled=True),
        preferred_element_type=jnp.float32,
    )
    projected = projected.astype(jnp.bfloat16)
    head_inputs, head_grad = (
        lax.all_to_all(projected, "seq", split_axis=2, concat_axis=0, tiled=True),
        lax.all_to_all(
            local_grad.reshape(tok_count, 1, width_all),
            "seq",
            split_axis=2,
            concat_axis=0,
            tiled=True,
        ),
    )
    head_grad = head_grad.reshape(all_rows, local_cols)
    upper = HD
    result, query_grad, key_grad, value_grad = head_pass(
        head_inputs[:, 0, 0:upper],
        head_inputs[:, 1, 0:upper],
        head_inputs[:, 2, 0:upper],
        head_grad,
        pairs[0, 0],
        valid[0, 0],
    )
    grad_flat = jnp.stack([query_grad, key_grad, value_grad], axis=1).reshape(
        all_rows, 3 * local_cols
    )
    attended = lax.all_to_all(result, "seq", split_axis=0, concat_axis=1, tiled=True)
    local_sum = lax.dot_general(
        lax.all_gather(local_volume, "seq", axis=0, tiled=True),
        grad_flat,
        (((0,), (0,)), ((), ())),
        preferred_element_type=jnp.float32,
    )
    weight_part = (
        lax.psum_scatter(local_sum.astype(jnp.bfloat16), "dp", scatter_dimension=0, tiled=True)
        .astype(jnp.float32)
        .reshape(-1, 3, local_cols)
    )
    return (attended[None], weight_part)


def solution(mesh):
    return jax.shard_map(
        local,
        mesh=mesh,
        in_specs=(
            P("dp", "seq", None),
            P("dp", "seq", None),
            P("dp", None, None),
            P("dp", "seq", None, None),
            P("dp", "seq", None, None),
        ),
        out_specs=(P("dp", "seq", None), P("dp", None, "seq")),
        check_vma=False,
    )
```

profile of v0, /device:TPU:1, one launch (start us, length us, event | category | flops | bytes accessed | tf_op | source)
XLA Modules:
  0.0 504.7 jit_solution(6228003603930186872)
XLA Ops:
  8.7 2.4 copy.66
  11.6 4.1 reduce
  15.7 1.3 reshape.121
  17.1 11.8 %all-to-all-start.1 = ((bf16[16,2,6144]{2,1,0:T(2,128)(2,1)}), bf16[16,2,6144]{2,1,0:T(2,128)(2,1)S(1)}, u32[]{:S(2)}, u32[]{:S(2)}) async-start(bf16[16,2,6144]{2,1,0:T(2,128)(2,1)} %reshape.121), calls=%async_computation.1 | async-start | bytes 786432 | tf_op jit(solution)/shard_map/all_to_all | solution.py:108
  28.9 81.8 %all-gather.4.cloned.1.call-done = bf16[1024,3,1024]{2,0,1:T(8,128)(2,1)} async-done(((bf16[32,3,1024]{2,0,1:T(8,128)(2,1)}), bf16[1024,3,1024]{2,0,1:T(8,128)(2,1)}) %all-gather.4.cloned.1.call-update) | async-done | bytes 6291472 | tf_op jit(solution)/shard_map/all_gather | solution.py:102
  110.7 4.2 convolution_convert_fusion.2
  114.9 2.6 copy.63
  117.4 8.8 %all-to-all-start = ((bf16[192,3,1024]{0,1,2:T(4,128)(2,1)}), bf16[192,3,1024]{0,1,2:T(4,128)(2,1)S(1)}, u32[]{:S(2)}, u32[]{:S(2)}) async-start(bf16[192,3,1024]{0,1,2:T(4,128)(2,1)} %copy.63), calls=%async_computation | async-start | bytes 4194304 | tf_op jit(solution)/shard_map/all_to_all | solution.py:107
  127.9 2.0 reshape.122
  129.9 1.3 copy.95
  131.5 1.4 reshape_reshape.3
  132.9 58.4 %all-to-all-done = bf16[192,3,1024]{0,1,2:T(4,128)(2,1)S(1)} async-done(((bf16[192,3,1024]{0,1,2:T(4,128)(2,1)}), bf16[192,3,1024]{0,1,2:T(4,128)(2,1)S(1)}, u32[]{:S(2)}, u32[]{:S(2)}) %all-to-all-start) | async-done | bytes 1179680 | tf_op jit(solution)/shard_map/all_to_all | solution.py:107
  192.4 1.7 all_to_all.39
  194.1 1.2 copy.85
  195.3 1.2 copy.86
  196.5 1.1 reshape_squeeze.20
  197.6 83.3 %while.17 = (s32[]{:T(128)}, f32[24,128,64]{1,0,2:T(8,128)S(1)}, f32[24,128,64]{1,0,2:T(8,128)}, bf16[6,4,128,64]{2,1,0,3:T(4,128)(2,1)}, bf16[6,4,128,64]{2,1,0...) while((s32[]{:T(128)}, f32[24,128,64]{1,0,2:T(8,128)S(1)}, ...), condition=%wide.region_4.5_spmd.clone, body=%wide.region_0.4_spmd.clone.sunk | while | flops 280955456 | bytes 27224828 | solution.py:80
  198.3 1.8 gather_fusion.1
  202.5 1.8 gather_fusion
  212.3 1.8 gather_fusion.1
  216.4 1.8 gather_fusion
  226.1 1.8 gather_fusion.1
  230.3 1.8 gather_fusion
  240.0 1.8 gather_fusion.1
  244.1 1.8 gather_fusion
  253.9 1.8 gather_fusion.1
  258.0 1.8 gather_fusion
  267.7 1.8 gather_fusion.1
  271.9 1.8 gather_fusion
  282.6 4.2 fusion.34
  288.4 23.2 %all_to_all.49 = bf16[16,192,64]{1,2,0:T(8,128)(2,1)S(1)} all-to-all(bf16[16,192,64]{1,2,0:T(8,128)(2,1)S(1)} %copy.75), channel_id=1, replica_groups=mesh['dp'=32,'seq'=16] {'seq'}, dimensions={0} | all-to-all | bytes 786432 | tf_op jit(solution)/shard_map/all_to_all | solution.py:129
  312.5 183.2 %reduce-scatter.4.cloned.1.call-done = bf16[32,192]{1,0:T(8,128)(2,1)} async-done(((bf16[1024,192]{1,0:T(8,128)(2,1)}), bf16[32,192]{1,0:T(8,128)(2,1)}) %reduce-scatter.4.cloned.1.call-update) | async-done | bytes 12304
  (247 shorter events, 71.0 us)
Async XLA Ops:
  8.0 102.7 %all-gather.4.cloned.1.call-start = ((), (), s32[]{:S(2)}) async-start(), calls=%async_computation.4 | async-start | bytes 6488064 | tf_op jit(solution)/shard_map/all_gather | solution.py:102
  11.6 99.0 %copy-start.3 = (bf16[1,192,1024]{2,1,0:T(8,128)(2,1)S(1)}, bf16[1,192,1024]{2,1,0:T(8,128)(2,1)}, u32[]{:S(2)}) copy-start(bf16[1,192,1024]{2,1,0:T(8,128)(2,1)} %param.7) | copy-start | bytes 1179652
  17.1 100.4 %all-to-all-start.1 = ((bf16[16,2,6144]{2,1,0:T(2,128)(2,1)}), bf16[16,2,6144]{2,1,0:T(2,128)(2,1)S(1)}, u32[]{:S(2)}, u32[]{:S(2)}) async-start(bf16[16,2,6144]{2,1,0:T(2,128)(2,1)} %reshape.121), calls=%async_computation.1 | async-start | bytes 786432 | tf_op jit(solution)/shard_map/all_to_all | solution.py:108
  117.4 9.7 %copy-start.8 = (s32[1,1,24,4]{2,3,1,0:T(4,128)S(1)}, s32[1,1,24,4]{2,3,1,0:T(4,128)}, u32[]{:S(2)}) copy-start(s32[1,1,24,4]{2,3,1,0:T(4,128)} %param.10) | copy-start | bytes 1156
  117.4 10.4 %copy-start.9 = (s32[1,1,24,4]{2,3,1,0:T(4,128)S(1)}, s32[1,1,24,4]{2,3,1,0:T(4,128)}, u32[]{:S(2)}) copy-start(s32[1,1,24,4]{2,3,1,0:T(4,128)} %param.11) | copy-start | bytes 1156
  117.4 73.8 %all-to-all-start = ((bf16[192,3,1024]{0,1,2:T(4,128)(2,1)}), bf16[192,3,1024]{0,1,2:T(4,128)(2,1)S(1)}, u32[]{:S(2)}, u32[]{:S(2)}) async-start(bf16[192,3,1024]{0,1,2:T(4,128)(2,1)} %copy.63), calls=%async_computation | async-start | bytes 4194304 | tf_op jit(solution)/shard_map/all_to_all | solution.py:107
  126.3 156.4 %all-gather.6.cloned.1.call-start = ((), (), s32[]{:S(2)}) async-start(), calls=%async_computation.5 | async-start | bytes 6684672 | tf_op jit(solution)/shard_map/all_gather | solution.py:131
  126.8 368.9 %reduce-scatter.4.cloned.1.call-start = ((), (), s32[]{:S(2)}) async-start(), calls=%async_computation.6 | async-start | bytes 540672
  197.6 4.0 copy-start.6
  208.7 1.1 copy-start
  210.6 0.9 copy-start.1
  211.5 3.9 copy-start.6
  220.9 0.9 copy-start.7
  222.6 1.1 copy-start
  224.4 0.9 copy-start.1
  225.4 3.9 copy-start.6
  236.5 1.1 copy-start
  238.3 0.9 copy-start.1
  239.2 3.9 copy-start.6
  250.3 1.1 copy-start
  252.2 0.9 copy-start.1
  253.1 3.9 copy-start.6
  262.5 0.9 copy-start.7
  264.2 1.1 copy-start
  266.0 0.9 copy-start.1
  266.9 3.9 copy-start.6
  276.4 0.9 copy-start.7
  278.1 1.1 copy-start
  279.9 0.9 copy-start.1
  280.8 1.1 copy-start.2
  280.9 1.3 copy-start.5
  286.8 1.0 copy-start.4
  (3 other events, 2.6 us)
Sparse Core Ops, SparseCore 0:
  12.0 98.6 all-gather.3
  288.0 207.7 reduce-scatter.3
Sparse Core Ops, SparseCore 1:
  128.9 77.7 all-gather.5
where the time goes:
time: 511 us; the launch traced here: 505 us
  waiting for transfers between devices  325 us (64%)
  local copies, waits for them, and re-layouts  76.9 us (15%)
  matrix products  27.8 us (5%)
  blocking collectives  23.2 us (5%)
  starting transfers between devices  21 us (4%)
  between operations  15.7 us (3%)
  other arithmetic  14.6 us (3%)
    unnamed x4, waiting for transfers between devices  184 us
    all_gather x1, waiting for transfers between devices, local(): lax.all_gather(weights, 'dp', axis=0, tiled=True)  81.8 us
    all_to_all x1, waiting for transfers between devices, local(): lax.all_to_all(projected, 'seq', split_axis=2, concat_axis=0, tiled=True)  58.4 us
    all_to_all x1, blocking collectives, local(): lax.all_to_all(result, 'seq', split_axis=0, concat_axis=1, tiled=True)  23.2 us
    unnamed x24, local copies, waits for them, and re-layouts  12.6 us
    all_to_all x1, starting transfers between devices, local(): lax.all_to_all(local_grad.reshape(tok_count, 1, width_all), 'seq', split_...  11.8 us
    gather x6, local copies, waits for them, and re-layouts, step(): key_blocks[slot_blocks]  10.7 us
    gather x6, local copies, waits for them, and re-layouts, step(): value_blocks[slot_blocks]  10.7 us
  transfers between devices with their start and end apart: 5, of which 3 were waited for; matrix products, arithmetic and copies ran while one was open for 20% of the time, Pallas kernels for 0%

commit v1 on v0

v1 whole, which is shorter than its diff:
```python
import functools

import jax
import jax.numpy as jnp
from jax import lax
from jax.experimental import pallas as pl
from jax.experimental.pallas import tpu as pltpu
from jax.sharding import PartitionSpec as P

HD = 64
BLOCK = 128
LOG2E = 1.4426950408889634
CHUNKS = 8
UNROLL = 2

NN = (((1,), (0,)), ((), ()))
NT = (((1,), (1,)), ((), ()))


def mm(a, b, dims=NN):
    return lax.dot_general(a, b, dims, preferred_element_type=jnp.float32)


def head_kernel(
    pairs_ref, valid_ref, vol_hbm, w_ref, cot_ref, att_ref, wg_ref,
    vol_ref, kv_ref, kvt_ref, q_ref, do_ref, acc_ref, dt_ref, o_ref, sems,
):
    rows, width = vol_ref.shape
    n_blocks, slots = pairs_ref.shape
    peers, half, _ = cot_ref.shape
    chunk = rows // CHUNKS
    blocks_per = chunk // BLOCK
    scale = HD ** -0.5

    copies = [
        pltpu.make_async_copy(
            vol_hbm.at[pl.ds(c * chunk, chunk)], vol_ref.at[pl.ds(c * chunk, chunk)], sems.at[c]
        )
        for c in range(CHUNKS)
    ]
    for copy in copies:
        copy.start()

    acc_ref[...] = jnp.zeros_like(acc_ref)
    blank = jnp.zeros((half, HD), jnp.bfloat16)
    for s in range(peers):
        both = cot_ref[s]
        do_ref[pl.ds(2 * half * s, half), :] = jnp.concatenate([blank, both[:, :HD]], axis=1)
        do_ref[pl.ds(2 * half * s + half, half), :] = jnp.concatenate([blank, both[:, HD:]], axis=1)

    for c in range(CHUNKS):
        copies[c].wait()
        got = mm(vol_ref[pl.ds(c * chunk, chunk), :], w_ref[...])
        q_ref[pl.ds(c * chunk, chunk), :] = got[:, BLOCK:].astype(jnp.bfloat16)
        keys = got[:, :BLOCK].astype(jnp.bfloat16)
        for b in range(blocks_per):
            one = keys[b * BLOCK:(b + 1) * BLOCK]
            kv_ref[c * blocks_per + b] = one
            kvt_ref[c * blocks_per + b] = one.T

    def block(b):
        at = pl.ds(pl.multiple_of(b * BLOCK, BLOCK), BLOCK)
        names = [pairs_ref[b, j] for j in range(slots)]
        kv = jnp.concatenate([kv_ref[n] for n in names], axis=0)
        kvt = jnp.concatenate([kvt_ref[n] for n in names], axis=1)
        d_out = do_ref[at, :]
        rhs = jnp.concatenate([q_ref[at, :], d_out], axis=0)
        both = mm(kv, rhs, NT)
        scores = both[:, :BLOCK] * (scale * LOG2E)
        prob_grad = both[:, BLOCK:]
        masked = jnp.concatenate(
            [
                jnp.where(valid_ref[b, j] > 0, scores[j * BLOCK:(j + 1) * BLOCK], -jnp.inf)
                for j in range(slots)
            ],
            axis=0,
        )
        top = jnp.max(masked, axis=0, keepdims=True)
        exponent = jnp.exp2(masked - top)
        probs = exponent * (1.0 / jnp.sum(exponent, axis=0, keepdims=True))
        rounded = probs.astype(jnp.bfloat16)
        out_t = mm(kvt[HD:], rounded).astype(jnp.bfloat16)
        out = out_t.astype(jnp.float32).T
        o_ref[at, :] = out.astype(jnp.bfloat16)
        grad_t = d_out.astype(jnp.float32).T[HD:]
        row_dot = jnp.sum(grad_t * out_t.astype(jnp.float32), axis=0, keepdims=True)
        score_grad = (probs * (prob_grad - row_dot)).astype(jnp.bfloat16)
        query_grad = mm(kvt[:HD], score_grad) * scale
        dt_ref[BLOCK:, at] = query_grad.astype(jnp.bfloat16)
        back = mm(jnp.concatenate([score_grad, rounded], axis=1), rhs)
        for j in range(slots):
            acc_ref[names[j]] += back[j * BLOCK:(j + 1) * BLOCK]

    def body(i, carry):
        for u in range(UNROLL):
            block(i * UNROLL + u)
        return carry

    lax.fori_loop(0, n_blocks // UNROLL, body, 0)

    for s in range(peers):
        att_ref[s] = jnp.concatenate(
            [
                o_ref[pl.ds(2 * half * s, half), :],
                o_ref[pl.ds(2 * half * s + half, half), :],
            ],
            axis=1,
        )
    lane = lax.broadcasted_iota(jnp.int32, (BLOCK, BLOCK), 1)
    factor = jnp.where(lane < HD, scale, 1.0)
    for b in range(n_blocks):
        dt_ref[:BLOCK, b * BLOCK:(b + 1) * BLOCK] = (acc_ref[b] * factor).T.astype(jnp.bfloat16)

    owners = wg_ref.shape[0]
    mine = width // owners
    part = 256
    for n in range(width // part):
        got = mm(dt_ref[...], vol_ref[:, n * part:(n + 1) * part])
        kv_part = got[:BLOCK].T.astype(jnp.bfloat16)
        q_part = got[BLOCK:].T.astype(jnp.bfloat16)
        for k in range(part // mine):
            owner = n * (part // mine) + k
            wg_ref[owner, :mine] = kv_part[k * mine:(k + 1) * mine]
            q_rows = q_part[k * mine:(k + 1) * mine]
            wg_ref[owner, mine:] = jnp.concatenate([q_rows[:mine // 2], q_rows[mine // 2:]], axis=1)


def head_call(pairs, valid, vol, w, cot, owners):
    rows, width = vol.shape
    n_blocks = rows // BLOCK
    mine = width // owners
    vmem = functools.partial(pl.BlockSpec, memory_space=pltpu.VMEM)
    smem = functools.partial(pl.BlockSpec, memory_space=pltpu.SMEM)
    return pl.pallas_call(
        head_kernel,
        out_shape=(
            jax.ShapeDtypeStruct(cot.shape, jnp.bfloat16),
            jax.ShapeDtypeStruct((owners, mine + mine // 2, BLOCK), jnp.bfloat16),
        ),
        in_specs=[smem(), smem(), pl.BlockSpec(memory_space=pl.ANY), vmem(), vmem()],
        out_specs=(vmem(), vmem()),
        scratch_shapes=[
            pltpu.VMEM((rows, width), jnp.bfloat16),
            pltpu.VMEM((n_blocks, BLOCK, BLOCK), jnp.bfloat16),
            pltpu.VMEM((n_blocks, BLOCK, BLOCK), jnp.bfloat16),
            pltpu.VMEM((rows, BLOCK), jnp.bfloat16),
            pltpu.VMEM((rows, BLOCK), jnp.bfloat16),
            pltpu.VMEM((n_blocks, BLOCK, BLOCK), jnp.float32),
            pltpu.VMEM((BLOCK + HD, rows), jnp.bfloat16),
            pltpu.VMEM((rows, HD), jnp.bfloat16),
            pltpu.SemaphoreType.DMA((CHUNKS,)),
        ],
        compiler_params=pltpu.CompilerParams(vmem_limit_bytes=40 * 2**20),
        name="head",
    )(pairs, valid, vol, w, cot)


def local(volume, cotangent, weights, pairs, valid):
    peers = lax.axis_size("seq")
    owners = lax.axis_size("dp")
    vol, cot = volume[0], cotangent[0]
    toks, width = vol.shape
    w_rows = weights.shape[0]
    half = toks // 2

    gathered = lax.all_gather(vol, "seq", axis=0, tiled=True)

    column = lax.axis_index("seq") * HD
    mine = lax.dynamic_slice_in_dim(weights, column, HD, axis=2)
    mine = jnp.stack([mine[:, 1], mine[:, 2], mine[:, 0]], axis=1).reshape(-1, BLOCK)
    sent = jnp.broadcast_to(mine[None], (owners, *mine.shape))
    w = lax.all_to_all(sent, "dp", split_axis=0, concat_axis=0, tiled=True)
    w = w.reshape(owners * w_rows, 3 * HD)
    w = jnp.pad(w, ((0, 0), (0, HD)))

    cot = cot.reshape(2, half, peers, HD).transpose(2, 1, 0, 3).reshape(peers, half, 2 * HD)
    cot = lax.all_to_all(cot, "seq", split_axis=0, concat_axis=0, tiled=True)

    att, wg = head_call(pairs[0, 0], valid[0, 0], gathered, w, cot, owners)

    wg = lax.all_to_all(wg, "dp", split_axis=0, concat_axis=0, tiled=True)
    att = lax.all_to_all(att, "seq", split_axis=0, concat_axis=0, tiled=True)
    att = att.reshape(peers, half, 2, HD).transpose(2, 1, 0, 3).reshape(1, toks, peers * HD)
    total = jnp.sum(wg.astype(jnp.float32), axis=0)
    kv = total[:w_rows].reshape(w_rows, 2, HD)
    q = total[w_rows:].reshape(w_rows // 2, 2, HD).transpose(1, 0, 2).reshape(w_rows, 1, HD)
    return att, jnp.concatenate([q, kv], axis=1)


def solution(mesh):
    return jax.shard_map(
        local,
        mesh=mesh,
        in_specs=(
            P("dp", "seq", None),
            P("dp", "seq", None),
            P("dp", None, None),
            P("dp", "seq", None, None),
            P("dp", "seq", None, None),
        ),
        out_specs=(P("dp", "seq", None), P("dp", None, "seq")),
        check_vma=False,
    )
```

time: 511 us -> 155 us (0.30); the launches traced: 505 us -> 155 us
  waiting for transfers between devices: 325 us -> 50.3 us
  local copies, waits for them, and re-layouts: 76.9 us -> 10.2 us
  matrix products: 27.8 us -> 0 us
  Pallas kernels: 0 us -> 27.3 us
  other arithmetic: 14.6 us -> 0.12 us
  starting transfers between devices: 21 us -> 34.1 us
    unnamed x4 -> x1, waiting for transfers between devices: 184 us -> 0.68 us
    all_gather x2 -> x1, waiting for transfers between devices: 81.8 us -> 10.2 us  [local(): gathered = lax.all_gather(vol, 'seq', axis=0, tiled=True)]
    dot_general x50 -> x0, matrix products: 27.8 us -> none  [the longest x6 4.26 us: step(): jnp.einsum('jb,jrd->brd', one_hot, key_grad.reshape(per_step * slot_count...]
    pallas_call x0 -> x1, Pallas kernels: none -> 27.3 us  [head_call(): pl.pallas_call(head_kernel, out_shape=(jax.ShapeDtypeStruct(cot.shape, jn...]
    gather x12 -> x0, local copies, waits for them, and re-layouts: 21.4 us -> none  [the longest x6 10.7 us: step(): key_blocks[slot_blocks]]
    all_to_all x2 -> x3, waiting for transfers between devices: 58.4 us -> 39.4 us  [the longest x1 17.7 us: local(): cot = lax.all_to_all(cot, 'seq', split_axis=0, concat_axis=0, tiled=True)]
    all_to_all x2 -> x3, starting transfers between devices: 20.7 us -> 34 us  [the longest x1 14.2 us: local(): cot = lax.all_to_all(cot, 'seq', split_axis=0, concat_axis=0, tiled=True)]
    dynamic_slice x12 -> x0, local copies, waits for them, and re-layouts: 10.5 us -> none  [head_pass(): lax.scan(step, (empty_acc, empty_acc), sliced_all)]
  transfers between devices with their start and end apart: 5 -> 4, of which waited for: 3 -> 4; matrix products, arithmetic and copies ran while one was open for 20% -> 4% of each run, Pallas kernels for 0% -> 0%
where the time goes in v1:
time: 155 us
  waiting for transfers between devices  50.3 us (32%)
  starting transfers between devices  34.1 us (22%)
  Pallas kernels  27.3 us (18%)
  blocking collectives  18.7 us (12%)
  between operations  14.2 us (9%)
  local copies, waits for them, and re-layouts  10.2 us (7%)
    pallas_call x1, Pallas kernels, head_call(): pl.pallas_call(head_kernel, out_shape=(jax.ShapeDtypeStruct(cot.shape, jn...  27.3 us
    all_to_all x1, blocking collectives, local(): att = lax.all_to_all(att, 'seq', split_axis=0, concat_axis=0, tiled=True)  18.7 us
    all_to_all x1, waiting for transfers between devices, local(): cot = lax.all_to_all(cot, 'seq', split_axis=0, concat_axis=0, tiled=True)  17.7 us
    all_to_all x1, starting transfers between devices, local(): cot = lax.all_to_all(cot, 'seq', split_axis=0, concat_axis=0, tiled=True)  14.2 us
    all_to_all x1, waiting for transfers between devices, local(): wg = lax.all_to_all(wg, 'dp', split_axis=0, concat_axis=0, tiled=True)  12.7 us
    all_to_all x1, starting transfers between devices, local(): w = lax.all_to_all(sent, 'dp', split_axis=0, concat_axis=0, tiled=True)  10.5 us
    all_gather x1, waiting for transfers between devices, local(): gathered = lax.all_gather(vol, 'seq', axis=0, tiled=True)  10.2 us
    all_to_all x1, starting transfers between devices, local(): wg = lax.all_to_all(wg, 'dp', split_axis=0, concat_axis=0, tiled=True)  9.35 us
  transfers between devices with their start and end apart: 4, of which 4 were waited for; matrix products, arithmetic and copies ran while one was open for 4% of the time, Pallas kernels for 0%

profile of v1, /device:TPU:1, one launch (start us, length us, event | category | flops | bytes accessed | tf_op | source)
XLA Modules:
  0.0 154.9 jit_solution(13805155374558216788)
XLA Ops:
  7.2 0.0 all-gather.3.cloned.1.call-start
  7.2 0.7 all-gather.3.cloned.1.call-update
  7.9 0.2 copy-done
  8.1 0.1 constant_dynamic-slice_fusion.1
  8.2 0.1 constant_dynamic-slice_fusion
  8.3 0.1 broadcast_in_dim.7
  8.4 0.8 broadcast_in_dim.8
  9.2 10.5 %all-to-all-start = ((bf16[32,48,128]{2,1,0:T(8,128)(2,1)}), bf16[32,48,128]{2,1,0:T(8,128)(2,1)S(1)}, u32[]{:S(2)}, u32[]{:S(2)}) async-start(bf16[32,48,128]{2,1,0:T(8,128)(2,1)} %broadcast_in_dim.8), calls=%async_computation | async-start | bytes 786432 | tf_op jit(solution)/shard_map/all_to_all | solution.py:172
  19.7 1.2 copy.22
  20.9 0.3 reshape_squeeze.3
  21.2 0.1 copy.23
  21.3 1.0 copy.24
  22.3 9.1 %all-to-all-done = bf16[32,48,128]{2,1,0:T(8,128)(2,1)S(1)} async-done(((bf16[32,48,128]{2,1,0:T(8,128)(2,1)}), bf16[32,48,128]{2,1,0:T(8,128)(2,1)S(1)}, u32[]{:S(2)}, u32[]{:S(2)}) %all-to-all-start) | async-done | bytes 393248 | tf_op jit(solution)/shard_map/all_to_all | solution.py:172
  31.3 14.2 %all-to-all-start.1 = ((bf16[16,96,128]{2,1,0:T(8,128)(2,1)}), bf16[16,96,128]{2,1,0:T(8,128)(2,1)S(1)}, u32[]{:S(2)}, u32[]{:S(2)}) async-start(bf16[16,96,128]{2,1,0:T(8,128)(2,1)} %copy.24), calls=%async_computation.1 | async-start | bytes 786432 | tf_op jit(solution)/shard_map/all_to_all | solution.py:177
  45.5 0.1 copy.25.pairs_ref
  45.6 0.1 copy.26.valid_ref
  45.7 0.4 reshape.26
  46.1 0.1 pad.4.w_ref
  46.2 17.7 %all-to-all-done.1.cot_ref = bf16[16,96,128]{2,1,0:T(8,128)(2,1)S(1)} async-done(((bf16[16,96,128]{2,1,0:T(8,128)(2,1)}), bf16[16,96,128]{2,1,0:T(8,128)(2,1)S(1)}, u32[]{:S(2)}, u32[]{:S(2)}) %all-to-all-start.1) | async-done | bytes 393248 | tf_op jit(solution)/shard_map/all_to_all | solution.py:177
  63.8 10.2 %all-gather.3.cloned.1.call-done = bf16[1,3072,1024]{2,1,0:T(8,128)(2,1)} async-done(((bf16[1,192,1024]{2,1,0:T(8,128)(2,1)}), bf16[1,3072,1024]{2,1,0:T(8,128)(2,1)}) %all-gather.3.cloned.1.call-update) | async-done | bytes 6291472 | tf_op jit(solution)/shard_map/all_gather | solution.py:166
  74.0 2.8 %copy-done.1 = bf16[1,3072,1024]{2,1,0:T(8,128)(2,1)S(1)} copy-done((bf16[1,3072,1024]{2,1,0:T(8,128)(2,1)S(1)}, bf16[1,3072,1024]{2,1,0:T(8,128)(2,1)}, u32[]{:S(2)}) %copy-start.1) | copy-done | bytes 6291480
  76.8 27.3 %head.1 = (bf16[16,96,128]{2,1,0:T(8,128)(2,1)S(1)}, bf16[32,48,128]{2,1,0:T(8,128)(2,1)}) custom-call(s32[24,4]{1,0:T(8,128)S(1)} %copy.25.pairs_ref, s32[24,4]{1,0:T(8,128)S(1)} %copy.26.valid_ref, bf16[3072,1024]{1,0:T(8,128)(2,1)S(1)} %bitcast.16, bf16[1024,256]{1,0:T(8,128)(2,1)S(1)} %pad.4.w_ref, bf16[16,96,128]{2,1,0:T(8,128)(2,1)S(1)} %all-to-all-done.1.cot_ref), custom_call_target="tpu_custom_call" | custom-call | tf_op jit(solution)/shard_map/head/pallas_call | solution.py:134
  104.1 18.7 %all_to_all.20 = bf16[16,96,128]{2,1,0:T(8,128)(2,1)S(1)} all-to-all(bf16[16,96,128]{2,1,0:T(8,128)(2,1)S(1)} %get-tuple-element.4), channel_id=1, replica_groups=mesh['dp'=32,'seq'=16] {'seq'}, dimensions={0} | all-to-all | bytes 786432 | tf_op jit(solution)/shard_map/all_to_all | solution.py:182
  122.9 9.4 %all-to-all-start.3 = ((bf16[32,48,128]{2,1,0:T(8,128)(2,1)}), bf16[32,48,128]{2,1,0:T(8,128)(2,1)S(1)}, u32[]{:S(2)}, u32[]{:S(2)}) async-start(bf16[32,48,128]{2,1,0:T(8,128)(2,1)} %get-tuple-element.5), calls=%async_computation.3 | async-start | bytes 786432 | tf_op jit(solution)/shard_map/all_to_all | solution.py:181
  132.2 0.3 copy.27
  132.5 0.6 copy.33
  133.1 1.3 reshape.34
  134.4 12.7 %all-to-all-done.3 = bf16[32,48,128]{2,1,0:T(8,128)(2,1)S(1)} async-done(((bf16[32,48,128]{2,1,0:T(8,128)(2,1)}), bf16[32,48,128]{2,1,0:T(8,128)(2,1)S(1)}, u32[]{:S(2)}, u32[]{:S(2)}) %all-to-all-start.3) | async-done | bytes 393248 | tf_op jit(solution)/shard_map/all_to_all | solution.py:181
  147.1 0.1 convert_reduce_fusion
  147.2 0.1 reshape.30
  147.3 0.1 reshape.32
  147.4 0.6 copy.32
  (12 shorter events, 0.1 us)
Async XLA Ops:
  7.2 0.9 copy-start
  7.2 38.3 %copy-start.2 = (s32[1,1,24,4]{2,3,1,0:T(4,128)S(1)}, s32[1,1,24,4]{2,3,1,0:T(4,128)}, u32[]{:S(2)}) copy-start(s32[1,1,24,4]{2,3,1,0:T(4,128)} %param.8) | copy-start | bytes 1156
  7.2 38.4 %copy-start.3 = (s32[1,1,24,4]{2,3,1,0:T(4,128)S(1)}, s32[1,1,24,4]{2,3,1,0:T(4,128)}, u32[]{:S(2)}) copy-start(s32[1,1,24,4]{2,3,1,0:T(4,128)} %param.9) | copy-start | bytes 1156
  7.2 66.8 %all-gather.3.cloned.1.call-start = ((), (), s32[]{:S(2)}) async-start(), calls=%async_computation.4 | async-start | bytes 6684672 | tf_op jit(solution)/shard_map/all_gather | solution.py:166
  9.2 22.2 %all-to-all-start = ((bf16[32,48,128]{2,1,0:T(8,128)(2,1)}), bf16[32,48,128]{2,1,0:T(8,128)(2,1)S(1)}, u32[]{:S(2)}, u32[]{:S(2)}) async-start(bf16[32,48,128]{2,1,0:T(8,128)(2,1)} %broadcast_in_dim.8), calls=%async_computation | async-start | bytes 786432 | tf_op jit(solution)/shard_map/all_to_all | solution.py:172
  31.3 32.5 %all-to-all-start.1 = ((bf16[16,96,128]{2,1,0:T(8,128)(2,1)}), bf16[16,96,128]{2,1,0:T(8,128)(2,1)S(1)}, u32[]{:S(2)}, u32[]{:S(2)}) async-start(bf16[16,96,128]{2,1,0:T(8,128)(2,1)} %copy.24), calls=%async_computation.1 | async-start | bytes 786432 | tf_op jit(solution)/shard_map/all_to_all | solution.py:177
  74.0 2.8 %copy-start.1 = (bf16[1,3072,1024]{2,1,0:T(8,128)(2,1)S(1)}, bf16[1,3072,1024]{2,1,0:T(8,128)(2,1)}, u32[]{:S(2)}) copy-start(bf16[1,3072,1024]{2,1,0:T(8,128)(2,1)} %all-gather.3.cloned.1.call-done) | copy-start | bytes 18874372
  122.9 24.3 %all-to-all-start.3 = ((bf16[32,48,128]{2,1,0:T(8,128)(2,1)}), bf16[32,48,128]{2,1,0:T(8,128)(2,1)S(1)}, u32[]{:S(2)}, u32[]{:S(2)}) async-start(bf16[32,48,128]{2,1,0:T(8,128)(2,1)} %get-tuple-element.5), calls=%async_computation.3 | async-start | bytes 786432 | tf_op jit(solution)/shard_map/all_to_all | solution.py:181
Sparse Core Ops, SparseCore 0:
  10.2 63.7 all-gather.2

commit v2 on v1

v2 whole, which is shorter than its diff:
```python
import functools

import jax
import jax.numpy as jnp
from jax import lax
from jax.experimental import pallas as pl
from jax.experimental.pallas import tpu as pltpu
from jax.sharding import PartitionSpec as P

HD = 64
BLOCK = 128
LOG2E = 1.4426950408889634
UNROLL = 4

NN = (((1,), (0,)), ((), ()))
NT = (((1,), (1,)), ((), ()))


def mm(a, b, dims=NN):
    return lax.dot_general(a, b, dims, preferred_element_type=jnp.float32)


def attend(n_blocks, slots, pairs_ref, valid_ref, kv_ref, kvt_ref, q_ref, do_ref, acc_ref, dt_ref, o_ref):
    scale = HD ** -0.5

    def row(b):
        return pl.ds(pl.multiple_of(b * BLOCK, BLOCK), BLOCK)

    def group(blocks):
        names = [[pairs_ref[b, j] for j in range(slots)] for b in blocks]
        rhs = [jnp.concatenate([q_ref[row(b), :], do_ref[row(b), :]], axis=0) for b in blocks]
        both = [
            mm(jnp.concatenate([kv_ref[row(n), :] for n in some], axis=0), r, NT)
            for some, r in zip(names, rhs)
        ]
        sent = []
        for b, pair in zip(blocks, both):
            parts = [pair[j * BLOCK:(j + 1) * BLOCK, :BLOCK] * (scale * LOG2E) for j in range(slots)]
            live = [valid_ref[b, j] > 0 for j in range(slots)]
            tops = [
                jnp.where(ok, jnp.max(part, axis=0, keepdims=True), -jnp.inf)
                for ok, part in zip(live, parts)
            ]
            top = functools.reduce(jnp.maximum, tops)
            exponents = [
                jnp.exp2(part - jnp.where(ok, top, jnp.inf)) for ok, part in zip(live, parts)
            ]
            exponent = jnp.concatenate(exponents, axis=0)
            probs = exponent * (1.0 / jnp.sum(exponent, axis=0, keepdims=True))
            weighted = probs * pair[:, BLOCK:]
            row_dot = jnp.sum(weighted, axis=0, keepdims=True)
            score_grad = (weighted - probs * row_dot).astype(jnp.bfloat16)
            sent.append(jnp.concatenate([score_grad, probs.astype(jnp.bfloat16)], axis=1))
        for b, some, pair in zip(blocks, names, sent):
            kvt = jnp.concatenate([kvt_ref[n] for n in some], axis=1)
            mixed = mm(kvt, pair)
            dt_ref[BLOCK:, row(b)] = (mixed[:HD, :BLOCK] * scale).astype(jnp.bfloat16)
            o_ref[row(b), :] = mixed[HD:, BLOCK:].T.astype(jnp.bfloat16)
        for some, pair, r in zip(names, sent, rhs):
            back = mm(pair, r)
            for j in range(slots):
                acc_ref[some[j]] += back[j * BLOCK:(j + 1) * BLOCK]

    def body(i, carry):
        group([i * UNROLL + u for u in range(UNROLL)])
        return carry

    lax.fori_loop(0, n_blocks // UNROLL, body, 0)


def block_places(me, peers):
    core = lax.rem(me, 2)
    chip = lax.div(me, 2)
    chips = peers // 2
    ahead = 1 - 2 * core
    places = [me, me + ahead]
    for k in range(1, chips // 2 + 1):
        back = lax.rem(chip - k * ahead + chips, chips)
        forth = lax.rem(chip + k * ahead + chips, chips)
        places += [2 * back + core, 2 * forth + 1 - core]
        if k < chips // 2:
            places += [2 * back + 1 - core, 2 * forth + core]
    return places


def head_kernel(*refs):
    me_ref, pairs_ref, valid_ref, w_ref, cot_ref = refs[:5]
    (
        att_ref, wg_ref, vol_ref, kv_ref, kvt_ref, q_ref, do_ref, acc_ref, dt_ref, o_ref,
    ) = refs[-10:]
    blocks = refs[5:-10]
    rows, width = vol_ref.shape
    toks = blocks[0].shape[0]
    n_blocks, slots = pairs_ref.shape
    peers, half, _ = cot_ref.shape
    scale = HD ** -0.5

    acc_ref[...] = jnp.zeros_like(acc_ref)
    blank = jnp.zeros((half, HD), jnp.bfloat16)
    for s in range(peers):
        both = cot_ref[s]
        do_ref[pl.ds(2 * half * s, half), :] = jnp.concatenate([blank, both[:, :HD]], axis=1)
        do_ref[pl.ds(2 * half * s + half, half), :] = jnp.concatenate([blank, both[:, HD:]], axis=1)

    for place, block_ref in zip(block_places(me_ref[0], peers), blocks):
        at = pl.ds(pl.multiple_of(place * toks, HD), toks)
        vol_ref[at, :] = block_ref[...]
        got = mm(block_ref[...], w_ref[...])
        q_ref[at, :] = got[:, BLOCK:].astype(jnp.bfloat16)
        kv_ref[at, :] = got[:, :BLOCK].astype(jnp.bfloat16)
    for b in range(n_blocks):
        kvt_ref[b] = kv_ref[b * BLOCK:(b + 1) * BLOCK, :].T

    attend(n_blocks, slots, pairs_ref, valid_ref, kv_ref, kvt_ref, q_ref, do_ref, acc_ref, dt_ref, o_ref)

    for s in range(peers):
        att_ref[s] = jnp.concatenate(
            [
                o_ref[pl.ds(2 * half * s, half), :],
                o_ref[pl.ds(2 * half * s + half, half), :],
            ],
            axis=1,
        )
    lane = lax.broadcasted_iota(jnp.int32, (BLOCK, BLOCK), 1)
    factor = jnp.where(lane < HD, scale, 1.0)
    for b in range(n_blocks):
        dt_ref[:BLOCK, b * BLOCK:(b + 1) * BLOCK] = (acc_ref[b] * factor).T.astype(jnp.bfloat16)

    owners = wg_ref.shape[0]
    mine = width // owners
    part = 256
    for n in range(width // part):
        got = mm(dt_ref[...], vol_ref[:, n * part:(n + 1) * part])
        kv_part = got[:BLOCK].T.astype(jnp.bfloat16)
        q_part = got[BLOCK:].T.astype(jnp.bfloat16)
        for k in range(part // mine):
            owner = n * (part // mine) + k
            wg_ref[owner, :mine] = kv_part[k * mine:(k + 1) * mine]
            q_rows = q_part[k * mine:(k + 1) * mine]
            wg_ref[owner, mine:] = jnp.concatenate([q_rows[:mine // 2], q_rows[mine // 2:]], axis=1)


def head_call(me, pairs, valid, w, cot, blocks, owners):
    toks, width = blocks[0].shape
    rows = toks * len(blocks)
    n_blocks = rows // BLOCK
    mine = width // owners
    vmem = pl.BlockSpec(memory_space=pltpu.VMEM)
    smem = pl.BlockSpec(memory_space=pltpu.SMEM)
    return pl.pallas_call(
        head_kernel,
        out_shape=(
            jax.ShapeDtypeStruct(cot.shape, jnp.bfloat16),
            jax.ShapeDtypeStruct((owners, mine + mine // 2, BLOCK), jnp.bfloat16),
        ),
        in_specs=[smem] * 3 + [vmem] * (2 + len(blocks)),
        out_specs=(vmem, vmem),
        scratch_shapes=[
            pltpu.VMEM((rows, width), jnp.bfloat16),
            pltpu.VMEM((rows, BLOCK), jnp.bfloat16),
            pltpu.VMEM((n_blocks, BLOCK, BLOCK), jnp.bfloat16),
            pltpu.VMEM((rows, BLOCK), jnp.bfloat16),
            pltpu.VMEM((rows, BLOCK), jnp.bfloat16),
            pltpu.VMEM((n_blocks, BLOCK, BLOCK), jnp.float32),
            pltpu.VMEM((BLOCK + HD, rows), jnp.bfloat16),
            pltpu.VMEM((rows, HD), jnp.bfloat16),
        ],
        compiler_params=pltpu.CompilerParams(vmem_limit_bytes=32 * 2**20),
        name="head",
    )(me, pairs, valid, w, cot, *blocks)


def gather(vol):
    peers = lax.axis_size("seq")
    chips = peers // 2
    onward = [
        (2 * z + c, 2 * ((z + 1) % chips) if c == 0 else 2 * ((z - 1) % chips) + 1)
        for z in range(chips)
        for c in range(2)
    ]
    twin = [(i, i ^ 1) for i in range(peers)]

    def swap(x):
        return lax.ppermute(x, "seq", twin)

    own, other = vol, swap(vol)
    blocks = [own, other]
    for k in range(1, chips // 2 + 1):
        own = lax.ppermute(own, "seq", onward)
        blocks += [own, swap(own)]
        if k < chips // 2:
            other = lax.ppermute(other, "seq", onward)
            blocks += [other, swap(other)]
    return blocks


def local(volume, cotangent, weights, pairs, valid):
    peers = lax.axis_size("seq")
    owners = lax.axis_size("dp")
    vol, cot = volume[0], cotangent[0]
    toks, width = vol.shape
    w_rows = weights.shape[0]
    half = toks // 2

    blocks = gather(vol)
    me = lax.axis_index("seq").reshape(1)

    column = lax.axis_index("seq") * HD
    mine = lax.dynamic_slice_in_dim(weights, column, HD, axis=2)
    mine = jnp.stack([mine[:, 1], mine[:, 2], mine[:, 0]], axis=1).reshape(-1, BLOCK)
    sent = jnp.broadcast_to(mine[None], (owners, *mine.shape))
    w = lax.all_to_all(sent, "dp", split_axis=0, concat_axis=0, tiled=True)
    w = w.reshape(owners * w_rows, 3 * HD)
    w = jnp.pad(w, ((0, 0), (0, HD)))

    cot = cot.reshape(2, half, peers, HD).transpose(2, 1, 0, 3).reshape(peers, half, 2 * HD)
    cot = lax.all_to_all(cot, "seq", split_axis=0, concat_axis=0, tiled=True)

    att, wg = head_call(me, pairs[0, 0], valid[0, 0], w, cot, blocks, owners)

    wg = lax.all_to_all(wg, "dp", split_axis=0, concat_axis=0, tiled=True)
    att = lax.all_to_all(att, "seq", split_axis=0, concat_axis=0, tiled=True)
    att = att.reshape(peers, half, 2, HD).transpose(2, 1, 0, 3).reshape(1, toks, peers * HD)
    total = jnp.sum(wg.astype(jnp.float32), axis=0)
    kv = total[:w_rows].reshape(w_rows, 2, HD)
    q = total[w_rows:].reshape(w_rows // 2, 2, HD).transpose(1, 0, 2).reshape(w_rows, 1, HD)
    return att, jnp.concatenate([q, kv], axis=1)


def solution(mesh):
    return jax.shard_map(
        local,
        mesh=mesh,
        in_specs=(
            P("dp", "seq", None),
            P("dp", "seq", None),
            P("dp", None, None),
            P("dp", "seq", None, None),
            P("dp", "seq", None, None),
        ),
        out_specs=(P("dp", "seq", None), P("dp", None, "seq")),
        check_vma=False,
    )
```

time: 155 us -> 148 us (0.955)
  starting transfers between devices: 34.1 us -> 73.2 us
  waiting for transfers between devices: 50.3 us -> 15.6 us
  Pallas kernels: 27.3 us -> 14.1 us
  between operations: 14.2 us -> 1.04 us
  local copies, waits for them, and re-layouts: 10.2 us -> 21.2 us
  blocking collectives: 18.7 us -> 21.6 us
    ppermute x0 -> x15, starting transfers between devices: none -> 47.1 us  [the longest x8 20.4 us: swap(): return lax.ppermute(x, 'seq', twin)]
    all_to_all x1, waiting for transfers between devices: 17.7 us -> 0.01 us  [local(): cot = lax.all_to_all(cot, 'seq', split_axis=0, concat_axis=0, tiled=True)]
    pallas_call x1, Pallas kernels: 27.3 us -> 14.1 us  [head_call(): pl.pallas_call(head_kernel, out_shape=(jax.ShapeDtypeStruct(cot.shape, jn...]
    all_gather x1 -> x0, waiting for transfers between devices: 10.2 us -> none  [local(): gathered = lax.all_gather(vol, 'seq', axis=0, tiled=True)]
    all_to_all x1, waiting for transfers between devices: 9.05 us -> 0.01 us  [local(): w = lax.all_to_all(sent, 'dp', split_axis=0, concat_axis=0, tiled=True)]
    all_to_all x1, starting transfers between devices: 14.2 us -> 6.88 us  [local(): cot = lax.all_to_all(cot, 'seq', split_axis=0, concat_axis=0, tiled=True)]
    ppermute x0 -> x15, waiting for transfers between devices: none -> 2.94 us  [the longest x4 2.92 us: gather(): own = lax.ppermute(own, 'seq', onward)]
    all_to_all x1, blocking collectives: 18.7 us -> 21.6 us  [local(): att = lax.all_to_all(att, 'seq', split_axis=0, concat_axis=0, tiled=True)]
  transfers between devices with their start and end apart: 4 -> 18, of which waited for: 4 -> 2; matrix products, arithmetic and copies ran while one was open for 4% -> 10% of each run, Pallas kernels for 0% -> 0%
where the time goes in v2:
time: 148 us; the launch traced here: 147 us
  starting transfers between devices  73.2 us (49%)
  blocking collectives  21.6 us (15%)
  local copies, waits for them, and re-layouts  21.2 us (14%)
  waiting for transfers between devices  15.6 us (11%)
  Pallas kernels  14.1 us (10%)
    all_to_all x1, blocking collectives, local(): att = lax.all_to_all(att, 'seq', split_axis=0, concat_axis=0, tiled=True)  21.6 us
    ppermute x8, starting transfers between devices, swap(): return lax.ppermute(x, 'seq', twin)  20.4 us
    ppermute x4, starting transfers between devices, gather(): own = lax.ppermute(own, 'seq', onward)  20.4 us
    pallas_call x1, Pallas kernels, head_call(): pl.pallas_call(head_kernel, out_shape=(jax.ShapeDtypeStruct(cot.shape, jn...  14.1 us
    all_to_all x1, waiting for transfers between devices, local(): wg = lax.all_to_all(wg, 'dp', split_axis=0, concat_axis=0, tiled=True)  12.7 us
    all_to_all x1, starting transfers between devices, local(): w = lax.all_to_all(sent, 'dp', split_axis=0, concat_axis=0, tiled=True)  9.67 us
    all_to_all x1, starting transfers between devices, local(): wg = lax.all_to_all(wg, 'dp', split_axis=0, concat_axis=0, tiled=True)  9.5 us
    unnamed x26, local copies, waits for them, and re-layouts  9.39 us
  transfers between devices with their start and end apart: 18, of which 2 were waited for; matrix products, arithmetic and copies ran while one was open for 10% of the time, Pallas kernels for 0%

profile of v2, /device:TPU:1, one launch (start us, length us, event | category | flops | bytes accessed | tf_op | source)
XLA Modules:
  0.0 146.8 jit_solution(10544456452570148654)
XLA Ops:
  0.6 11.6 %collective-permute-start.1 = (bf16[192,1024]{1,0:T(8,128)(2,1)}, bf16[192,1024]{1,0:T(8,128)(2,1)S(1)}, u32[]{:S(2)}, u32[]{:S(2)}) collective-permute-start(bf16[192,1024]{1,0:T(8,128)(2,1)} %bitcast.17), channel_id=1, source_target_pairs={{0,2},{1,15},{2,4},{3,1},{4,6},{5,3},{6,8},{7,5},{8,10},{9,7},{10,... | collective-permute-start | bytes 1179656 | tf_op jit(solution)/shard_map/ppermute | solution.py:189
  12.3 1.9 %collective-permute-start = (bf16[192,1024]{1,0:T(8,128)(2,1)}, bf16[192,1024]{1,0:T(8,128)(2,1)S(1)}, u32[]{:S(2)}, u32[]{:S(2)}) collective-permute-start(bf16[192,1024]{1,0:T(8,128)(2,1)} %bitcast.18), channel_id=1, source_target_pairs={{0,1},{1,0},{2,3},{3,2},{4,5},{5,4},{6,7},{7,6},{8,9},{9,8},{10,11... | collective-permute-start | bytes 1179656 | tf_op jit(solution)/shard_map/ppermute | solution.py:184
  14.4 2.9 %collective-permute-done.1.refs_7_ = bf16[192,1024]{1,0:T(8,128)(2,1)S(1)} collective-permute-done((bf16[192,1024]{1,0:T(8,128)(2,1)}, bf16[192,1024]{1,0:T(8,128)(2,1)S(1)}, u32[]{:S(2)}, u32[]{:S(2)}) %collective-permute-start.1) | collective-permute-done | bytes 393248 | tf_op jit(solution)/shard_map/ppermute | solution.py:189
  17.3 4.9 %collective-permute-start.5 = (bf16[192,1024]{1,0:T(8,128)(2,1)S(1)}, bf16[192,1024]{1,0:T(8,128)(2,1)S(1)}, u32[]{:S(2)}, u32[]{:S(2)}) collective-permute-start(bf16[192,1024]{1,0:T(8,128)(2,1)S(1)} %collective-permute-done.1.refs_7_), channel_id=1, source_target_pairs={{0,2},{1,15},{2,4},{3,1},{4,6},{5,3},{6,8},{7,5},{8,10},{9,7},{10,... | collective-permute-start | bytes 1179656 | tf_op jit(solution)/shard_map/ppermute | solution.py:189
  22.2 1.9 %collective-permute-start.3 = (bf16[192,1024]{1,0:T(8,128)(2,1)S(1)}, bf16[192,1024]{1,0:T(8,128)(2,1)S(1)}, u32[]{:S(2)}, u32[]{:S(2)}) collective-permute-start(bf16[192,1024]{1,0:T(8,128)(2,1)S(1)} %collective-permute-done.refs_6_), channel_id=1, source_target_pairs={{0,2},{1,15},{2,4},{3,1},{4,6},{5,3},{6,8},{7,5},{8,10},{9,7},{10,... | collective-permute-start | bytes 1179656 | tf_op jit(solution)/shard_map/ppermute | solution.py:192
  24.3 0.8 broadcast_in_dim.8
  25.1 9.7 %all-to-all-start = ((bf16[32,48,128]{2,1,0:T(8,128)(2,1)}), bf16[32,48,128]{2,1,0:T(8,128)(2,1)S(1)}, u32[]{:S(2)}, u32[]{:S(2)}) async-start(bf16[32,48,128]{2,1,0:T(8,128)(2,1)} %broadcast_in_dim.8), calls=%async_computation | async-start | bytes 786432 | tf_op jit(solution)/shard_map/all_to_all | solution.py:212
  34.8 1.9 %collective-permute-start.9 = (bf16[192,1024]{1,0:T(8,128)(2,1)S(1)}, bf16[192,1024]{1,0:T(8,128)(2,1)S(1)}, u32[]{:S(2)}, u32[]{:S(2)}) collective-permute-start(bf16[192,1024]{1,0:T(8,128)(2,1)S(1)} %collective-permute-done.5.refs_11_), channel_id=1, source_target_pairs={{0,2},{1,15},{2,4},{3,1},{4,6},{5,3},{6,8},{7,5},{8,10},{9,7},{10,... | collective-permute-start | bytes 1179656 | tf_op jit(solution)/shard_map/ppermute | solution.py:189
  36.7 1.9 %collective-permute-start.7 = (bf16[192,1024]{1,0:T(8,128)(2,1)S(1)}, bf16[192,1024]{1,0:T(8,128)(2,1)}, u32[]{:S(2)}, u32[]{:S(2)}) collective-permute-start(bf16[192,1024]{1,0:T(8,128)(2,1)S(1)} %collective-permute-done.3.refs_9_), channel_id=1, source_target_pairs={{0,2},{1,15},{2,4},{3,1},{4,6},{5,3},{6,8},{7,5},{8,10},{9,7},{10,... | collective-permute-start | bytes 1179656 | tf_op jit(solution)/shard_map/ppermute | solution.py:192
  38.6 5.9 %collective-permute-start.2 = (bf16[192,1024]{1,0:T(8,128)(2,1)S(1)}, bf16[192,1024]{1,0:T(8,128)(2,1)S(1)}, u32[]{:S(2)}, u32[]{:S(2)}) collective-permute-start(bf16[192,1024]{1,0:T(8,128)(2,1)S(1)} %collective-permute-done.1.refs_7_), channel_id=1, source_target_pairs={{0,1},{1,0},{2,3},{3,2},{4,5},{5,4},{6,7},{7,6},{8,9},{9,8},{10,11... | collective-permute-start | bytes 1179656 | tf_op jit(solution)/shard_map/ppermute | solution.py:184
  44.6 1.9 %collective-permute-start.6 = (bf16[192,1024]{1,0:T(8,128)(2,1)S(1)}, bf16[192,1024]{1,0:T(8,128)(2,1)S(1)}, u32[]{:S(2)}, u32[]{:S(2)}) collective-permute-start(bf16[192,1024]{1,0:T(8,128)(2,1)S(1)} %collective-permute-done.5.refs_11_), channel_id=1, source_target_pairs={{0,1},{1,0},{2,3},{3,2},{4,5},{5,4},{6,7},{7,6},{8,9},{9,8},{10,11... | collective-permute-start | bytes 1179656 | tf_op jit(solution)/shard_map/ppermute | solution.py:184
  46.5 1.9 %collective-permute-start.13 = (bf16[192,1024]{1,0:T(8,128)(2,1)S(1)}, bf16[192,1024]{1,0:T(8,128)(2,1)}, u32[]{:S(2)}, u32[]{:S(2)}) collective-permute-start(bf16[192,1024]{1,0:T(8,128)(2,1)S(1)} %collective-permute-done.9.refs_15_), channel_id=1, source_target_pairs={{0,2},{1,15},{2,4},{3,1},{4,6},{5,3},{6,8},{7,5},{8,10},{9,7},{10,... | collective-permute-start | bytes 1179656 | tf_op jit(solution)/shard_map/ppermute | solution.py:189
  48.5 2.5 %collective-permute-start.11 = (bf16[192,1024]{1,0:T(8,128)(2,1)}, bf16[192,1024]{1,0:T(8,128)(2,1)}, u32[]{:S(2)}, u32[]{:S(2)}) collective-permute-start(bf16[192,1024]{1,0:T(8,128)(2,1)} %collective-permute-done.7.refs_13_), channel_id=1, source_target_pairs={{0,2},{1,15},{2,4},{3,1},{4,6},{5,3},{6,8},{7,5},{8,10},{9,7},{10,... | collective-permute-start | bytes 1179656 | tf_op jit(solution)/shard_map/ppermute | solution.py:192
  50.9 2.0 %copy.22 = bf16[1,192,1024]{1,2,0:T(8,128)(2,1)} copy(bf16[1,192,1024]{2,1,0:T(8,128)(2,1)} %param.6) | data formatting | bytes 786432 | tf_op args[1]
  53.0 2.1 %reshape_squeeze.3 = bf16[2,96,16,64]{1,0,3,2:T(2,128)(2,1)} reshape(bf16[1,192,1024]{1,2,0:T(8,128)(2,1)} %copy.22) | data formatting | bytes 786432 | tf_op jit(solution)/shard_map/reshape;squeeze | solution.py:216
  55.1 2.0 %copy.23 = bf16[16,96,2,64]{1,3,2,0:T(8,128)(2,1)} copy(bf16[16,96,2,64]{1,2,3,0:T(2,128)(2,1)} %bitcast.22) | data formatting | bytes 786432 | tf_op jit(solution)/shard_map/transpose | solution.py:216
  57.1 2.0 %copy.24 = bf16[16,96,128]{2,1,0:T(8,128)(2,1)} copy(bf16[16,96,128]{1,2,0:T(8,128)(2,1)} %bitcast.20) | data formatting | bytes 786432 | tf_op jit(solution)/shard_map/reshape | solution.py:216
  59.8 6.9 %all-to-all-start.1 = ((bf16[16,96,128]{2,1,0:T(8,128)(2,1)}), bf16[16,96,128]{2,1,0:T(8,128)(2,1)S(1)}, u32[]{:S(2)}, u32[]{:S(2)}) async-start(bf16[16,96,128]{2,1,0:T(8,128)(2,1)} %copy.24), calls=%async_computation.1 | async-start | bytes 786432 | tf_op jit(solution)/shard_map/all_to_all | solution.py:217
  66.7 2.0 %collective-permute-start.4 = (bf16[192,1024]{1,0:T(8,128)(2,1)S(1)}, bf16[192,1024]{1,0:T(8,128)(2,1)}, u32[]{:S(2)}, u32[]{:S(2)}) collective-permute-start(bf16[192,1024]{1,0:T(8,128)(2,1)S(1)} %collective-permute-done.3.refs_9_), channel_id=1, source_target_pairs={{0,1},{1,0},{2,3},{3,2},{4,5},{5,4},{6,7},{7,6},{8,9},{9,8},{10,11... | collective-permute-start | bytes 1179656 | tf_op jit(solution)/shard_map/ppermute | solution.py:184
  69.4 2.3 %collective-permute-start.10 = (bf16[192,1024]{1,0:T(8,128)(2,1)S(1)}, bf16[192,1024]{1,0:T(8,128)(2,1)}, u32[]{:S(2)}, u32[]{:S(2)}) collective-permute-start(bf16[192,1024]{1,0:T(8,128)(2,1)S(1)} %collective-permute-done.9.refs_15_), channel_id=1, source_target_pairs={{0,1},{1,0},{2,3},{3,2},{4,5},{5,4},{6,7},{7,6},{8,9},{9,8},{10,11... | collective-permute-start | bytes 1179656 | tf_op jit(solution)/shard_map/ppermute | solution.py:184
  72.5 2.0 %collective-permute-start.8 = (bf16[192,1024]{1,0:T(8,128)(2,1)}, bf16[192,1024]{1,0:T(8,128)(2,1)}, u32[]{:S(2)}, u32[]{:S(2)}) collective-permute-start(bf16[192,1024]{1,0:T(8,128)(2,1)} %collective-permute-done.7.refs_13_), channel_id=1, source_target_pairs={{0,1},{1,0},{2,3},{3,2},{4,5},{5,4},{6,7},{7,6},{8,9},{9,8},{10,11... | collective-permute-start | bytes 1179656 | tf_op jit(solution)/shard_map/ppermute | solution.py:184
  74.5 2.3 %collective-permute-start.14 = (bf16[192,1024]{1,0:T(8,128)(2,1)}, bf16[192,1024]{1,0:T(8,128)(2,1)}, u32[]{:S(2)}, u32[]{:S(2)}) collective-permute-start(bf16[192,1024]{1,0:T(8,128)(2,1)} %collective-permute-done.13.refs_19_), channel_id=1, source_target_pairs={{0,1},{1,0},{2,3},{3,2},{4,5},{5,4},{6,7},{7,6},{8,9},{9,8},{10,11... | collective-permute-start | bytes 1179656 | tf_op jit(solution)/shard_map/ppermute | solution.py:184
  76.9 2.0 %collective-permute-start.12 = (bf16[192,1024]{1,0:T(8,128)(2,1)}, bf16[192,1024]{1,0:T(8,128)(2,1)}, u32[]{:S(2)}, u32[]{:S(2)}) collective-permute-start(bf16[192,1024]{1,0:T(8,128)(2,1)} %collective-permute-done.11.refs_17_), channel_id=1, source_target_pairs={{0,1},{1,0},{2,3},{3,2},{4,5},{5,4},{6,7},{7,6},{8,9},{9,8},{10,11... | collective-permute-start | bytes 1179656 | tf_op jit(solution)/shard_map/ppermute | solution.py:184
  79.1 2.1 %reshape.30 = bf16[1024,192]{1,0:T(8,128)(2,1)} reshape(bf16[32,48,128]{2,1,0:T(8,128)(2,1)} %copy-done.7) | data formatting | bytes 786432 | tf_op jit(solution)/shard_map/reshape | solution.py:213
  81.2 1.2 pad.4.refs_3_
  82.5 1.0 copy-done.3
  83.5 1.0 copy-done.5
  84.5 14.1 %head.1 = (bf16[16,96,128]{2,1,0:T(8,128)(2,1)S(1)}, bf16[32,48,128]{2,1,0:T(8,128)(2,1)S(1)}) custom-call(s32[1]{0:T(128)} %bitcast.refs_0_, s32[24,4]{1,0:T(8,128)S(1)} %copy.25.refs_1_, s32[24,4]{1,0:T(8,128)S(1)} %copy.26.refs_2_, bf16[1024,256]{1,0:T(8,128)(2,1)S(1)} %pad.4.refs_3_, bf16[16,96,128]{2,1,0:T(8,128)(2,1)S(1)} %all-to-all-done.1.refs_4_, ...), custom_call_target="tpu_custom_call" | custom-call | tf_op jit(solution)/shard_map/head/pallas_call | solution.py:150
  98.6 21.6 %all_to_all.20 = bf16[16,96,128]{2,1,0:T(8,128)(2,1)S(1)} all-to-all(bf16[16,96,128]{2,1,0:T(8,128)(2,1)S(1)} %get-tuple-element.4), channel_id=1, replica_groups=mesh['dp'=32,'seq'=16] {'seq'}, dimensions={0} | all-to-all | bytes 786432 | tf_op jit(solution)/shard_map/all_to_all | solution.py:222
  120.2 9.5 %all-to-all-start.3 = ((bf16[32,48,128]{2,1,0:T(8,128)(2,1)}), bf16[32,48,128]{2,1,0:T(8,128)(2,1)S(1)}, u32[]{:S(2)}, u32[]{:S(2)}) async-start(bf16[32,48,128]{2,1,0:T(8,128)(2,1)} %copy-done.6), calls=%async_computation.3 | async-start | bytes 786432 | tf_op jit(solution)/shard_map/all_to_all | solution.py:221
  130.6 1.3 reshape.37
  131.9 12.7 %all-to-all-done.3 = bf16[32,48,128]{2,1,0:T(8,128)(2,1)S(1)} async-done(((bf16[32,48,128]{2,1,0:T(8,128)(2,1)}), bf16[32,48,128]{2,1,0:T(8,128)(2,1)S(1)}, u32[]{:S(2)}, u32[]{:S(2)}) %all-to-all-start.3) | async-done | bytes 393248 | tf_op jit(solution)/shard_map/all_to_all | solution.py:221
  (54 shorter events, 5.9 us)
Async XLA Ops:
  0.6 13.6 %copy-start = (bf16[32,3,1024]{2,0,1:T(8,128)(2,1)S(1)}, bf16[32,3,1024]{2,0,1:T(8,128)(2,1)}, u32[]{:S(2)}) copy-start(bf16[32,3,1024]{2,0,1:T(8,128)(2,1)} %param.7) | copy-start | bytes 589828
  0.6 16.7 %collective-permute-start.1 = (bf16[192,1024]{1,0:T(8,128)(2,1)}, bf16[192,1024]{1,0:T(8,128)(2,1)S(1)}, u32[]{:S(2)}, u32[]{:S(2)}) collective-permute-start(bf16[192,1024]{1,0:T(8,128)(2,1)} %bitcast.17), channel_id=1, source_target_pairs={{0,2},{1,15},{2,4},{3,1},{4,6},{5,3},{6,8},{7,5},{8,10},{9,7},{10,... | collective-permute-start | bytes 1179656 | tf_op jit(solution)/shard_map/ppermute | solution.py:189
  12.3 9.9 %collective-permute-start = (bf16[192,1024]{1,0:T(8,128)(2,1)}, bf16[192,1024]{1,0:T(8,128)(2,1)S(1)}, u32[]{:S(2)}, u32[]{:S(2)}) collective-permute-start(bf16[192,1024]{1,0:T(8,128)(2,1)} %bitcast.18), channel_id=1, source_target_pairs={{0,1},{1,0},{2,3},{3,2},{4,5},{5,4},{6,7},{7,6},{8,9},{9,8},{10,11... | collective-permute-start | bytes 1179656 | tf_op jit(solution)/shard_map/ppermute | solution.py:184
  17.3 17.5 %collective-permute-start.5 = (bf16[192,1024]{1,0:T(8,128)(2,1)S(1)}, bf16[192,1024]{1,0:T(8,128)(2,1)S(1)}, u32[]{:S(2)}, u32[]{:S(2)}) collective-permute-start(bf16[192,1024]{1,0:T(8,128)(2,1)S(1)} %collective-permute-done.1.refs_7_), channel_id=1, source_target_pairs={{0,2},{1,15},{2,4},{3,1},{4,6},{5,3},{6,8},{7,5},{8,10},{9,7},{10,... | collective-permute-start | bytes 1179656 | tf_op jit(solution)/shard_map/ppermute | solution.py:189
  22.2 14.5 %collective-permute-start.3 = (bf16[192,1024]{1,0:T(8,128)(2,1)S(1)}, bf16[192,1024]{1,0:T(8,128)(2,1)S(1)}, u32[]{:S(2)}, u32[]{:S(2)}) collective-permute-start(bf16[192,1024]{1,0:T(8,128)(2,1)S(1)} %collective-permute-done.refs_6_), channel_id=1, source_target_pairs={{0,2},{1,15},{2,4},{3,1},{4,6},{5,3},{6,8},{7,5},{8,10},{9,7},{10,... | collective-permute-start | bytes 1179656 | tf_op jit(solution)/shard_map/ppermute | solution.py:192
  25.1 33.9 %all-to-all-start = ((bf16[32,48,128]{2,1,0:T(8,128)(2,1)}), bf16[32,48,128]{2,1,0:T(8,128)(2,1)S(1)}, u32[]{:S(2)}, u32[]{:S(2)}) async-start(bf16[32,48,128]{2,1,0:T(8,128)(2,1)} %broadcast_in_dim.8), calls=%async_computation | async-start | bytes 786432 | tf_op jit(solution)/shard_map/all_to_all | solution.py:212
  34.8 11.7 %collective-permute-start.9 = (bf16[192,1024]{1,0:T(8,128)(2,1)S(1)}, bf16[192,1024]{1,0:T(8,128)(2,1)S(1)}, u32[]{:S(2)}, u32[]{:S(2)}) collective-permute-start(bf16[192,1024]{1,0:T(8,128)(2,1)S(1)} %collective-permute-done.5.refs_11_), channel_id=1, source_target_pairs={{0,2},{1,15},{2,4},{3,1},{4,6},{5,3},{6,8},{7,5},{8,10},{9,7},{10,... | collective-permute-start | bytes 1179656 | tf_op jit(solution)/shard_map/ppermute | solution.py:189
  36.7 11.7 %collective-permute-start.7 = (bf16[192,1024]{1,0:T(8,128)(2,1)S(1)}, bf16[192,1024]{1,0:T(8,128)(2,1)}, u32[]{:S(2)}, u32[]{:S(2)}) collective-permute-start(bf16[192,1024]{1,0:T(8,128)(2,1)S(1)} %collective-permute-done.3.refs_9_), channel_id=1, source_target_pairs={{0,2},{1,15},{2,4},{3,1},{4,6},{5,3},{6,8},{7,5},{8,10},{9,7},{10,... | collective-permute-start | bytes 1179656 | tf_op jit(solution)/shard_map/ppermute | solution.py:192
  38.6 30.0 %collective-permute-start.2 = (bf16[192,1024]{1,0:T(8,128)(2,1)S(1)}, bf16[192,1024]{1,0:T(8,128)(2,1)S(1)}, u32[]{:S(2)}, u32[]{:S(2)}) collective-permute-start(bf16[192,1024]{1,0:T(8,128)(2,1)S(1)} %collective-permute-done.1.refs_7_), channel_id=1, source_target_pairs={{0,1},{1,0},{2,3},{3,2},{4,5},{5,4},{6,7},{7,6},{8,9},{9,8},{10,11... | collective-permute-start | bytes 1179656 | tf_op jit(solution)/shard_map/ppermute | solution.py:184
  44.6 27.2 %collective-permute-start.6 = (bf16[192,1024]{1,0:T(8,128)(2,1)S(1)}, bf16[192,1024]{1,0:T(8,128)(2,1)S(1)}, u32[]{:S(2)}, u32[]{:S(2)}) collective-permute-start(bf16[192,1024]{1,0:T(8,128)(2,1)S(1)} %collective-permute-done.5.refs_11_), channel_id=1, source_target_pairs={{0,1},{1,0},{2,3},{3,2},{4,5},{5,4},{6,7},{7,6},{8,9},{9,8},{10,11... | collective-permute-start | bytes 1179656 | tf_op jit(solution)/shard_map/ppermute | solution.py:184
  46.5 28.0 %collective-permute-start.13 = (bf16[192,1024]{1,0:T(8,128)(2,1)S(1)}, bf16[192,1024]{1,0:T(8,128)(2,1)}, u32[]{:S(2)}, u32[]{:S(2)}) collective-permute-start(bf16[192,1024]{1,0:T(8,128)(2,1)S(1)} %collective-permute-done.9.refs_15_), channel_id=1, source_target_pairs={{0,2},{1,15},{2,4},{3,1},{4,6},{5,3},{6,8},{7,5},{8,10},{9,7},{10,... | collective-permute-start | bytes 1179656 | tf_op jit(solution)/shard_map/ppermute | solution.py:189
  48.5 28.4 %collective-permute-start.11 = (bf16[192,1024]{1,0:T(8,128)(2,1)}, bf16[192,1024]{1,0:T(8,128)(2,1)}, u32[]{:S(2)}, u32[]{:S(2)}) collective-permute-start(bf16[192,1024]{1,0:T(8,128)(2,1)} %collective-permute-done.7.refs_13_), channel_id=1, source_target_pairs={{0,2},{1,15},{2,4},{3,1},{4,6},{5,3},{6,8},{7,5},{8,10},{9,7},{10,... | collective-permute-start | bytes 1179656 | tf_op jit(solution)/shard_map/ppermute | solution.py:192
  59.0 0.7 copy-start.7
  59.0 19.9 %copy-start.9 = (s32[1,1,24,4]{2,3,1,0:T(4,128)S(1)}, s32[1,1,24,4]{2,3,1,0:T(4,128)}, u32[]{:S(2)}) copy-start(s32[1,1,24,4]{2,3,1,0:T(4,128)} %param.8) | copy-start | bytes 1156
  59.0 20.0 %copy-start.10 = (s32[1,1,24,4]{2,3,1,0:T(4,128)S(1)}, s32[1,1,24,4]{2,3,1,0:T(4,128)}, u32[]{:S(2)}) copy-start(s32[1,1,24,4]{2,3,1,0:T(4,128)} %param.9) | copy-start | bytes 1156
  59.8 22.6 %all-to-all-start.1 = ((bf16[16,96,128]{2,1,0:T(8,128)(2,1)}), bf16[16,96,128]{2,1,0:T(8,128)(2,1)S(1)}, u32[]{:S(2)}, u32[]{:S(2)}) async-start(bf16[16,96,128]{2,1,0:T(8,128)(2,1)} %copy.24), calls=%async_computation.1 | async-start | bytes 786432 | tf_op jit(solution)/shard_map/all_to_all | solution.py:217
  66.7 15.8 %collective-permute-start.4 = (bf16[192,1024]{1,0:T(8,128)(2,1)S(1)}, bf16[192,1024]{1,0:T(8,128)(2,1)}, u32[]{:S(2)}, u32[]{:S(2)}) collective-permute-start(bf16[192,1024]{1,0:T(8,128)(2,1)S(1)} %collective-permute-done.3.refs_9_), channel_id=1, source_target_pairs={{0,1},{1,0},{2,3},{3,2},{4,5},{5,4},{6,7},{7,6},{8,9},{9,8},{10,11... | collective-permute-start | bytes 1179656 | tf_op jit(solution)/shard_map/ppermute | solution.py:184
  68.7 0.7 copy-start.2
  69.4 13.0 %collective-permute-start.10 = (bf16[192,1024]{1,0:T(8,128)(2,1)S(1)}, bf16[192,1024]{1,0:T(8,128)(2,1)}, u32[]{:S(2)}, u32[]{:S(2)}) collective-permute-start(bf16[192,1024]{1,0:T(8,128)(2,1)S(1)} %collective-permute-done.9.refs_15_), channel_id=1, source_target_pairs={{0,1},{1,0},{2,3},{3,2},{4,5},{5,4},{6,7},{7,6},{8,9},{9,8},{10,11... | collective-permute-start | bytes 1179656 | tf_op jit(solution)/shard_map/ppermute | solution.py:184
  71.8 0.8 copy-start.4
  72.5 9.9 %collective-permute-start.8 = (bf16[192,1024]{1,0:T(8,128)(2,1)}, bf16[192,1024]{1,0:T(8,128)(2,1)}, u32[]{:S(2)}, u32[]{:S(2)}) collective-permute-start(bf16[192,1024]{1,0:T(8,128)(2,1)} %collective-permute-done.7.refs_13_), channel_id=1, source_target_pairs={{0,1},{1,0},{2,3},{3,2},{4,5},{5,4},{6,7},{7,6},{8,9},{9,8},{10,11... | collective-permute-start | bytes 1179656 | tf_op jit(solution)/shard_map/ppermute | solution.py:184
  74.5 7.9 %collective-permute-start.14 = (bf16[192,1024]{1,0:T(8,128)(2,1)}, bf16[192,1024]{1,0:T(8,128)(2,1)}, u32[]{:S(2)}, u32[]{:S(2)}) collective-permute-start(bf16[192,1024]{1,0:T(8,128)(2,1)} %collective-permute-done.13.refs_19_), channel_id=1, source_target_pairs={{0,1},{1,0},{2,3},{3,2},{4,5},{5,4},{6,7},{7,6},{8,9},{9,8},{10,11... | collective-permute-start | bytes 1179656 | tf_op jit(solution)/shard_map/ppermute | solution.py:184
  76.9 5.6 %collective-permute-start.12 = (bf16[192,1024]{1,0:T(8,128)(2,1)}, bf16[192,1024]{1,0:T(8,128)(2,1)}, u32[]{:S(2)}, u32[]{:S(2)}) collective-permute-start(bf16[192,1024]{1,0:T(8,128)(2,1)} %collective-permute-done.11.refs_17_), channel_id=1, source_target_pairs={{0,1},{1,0},{2,3},{3,2},{4,5},{5,4},{6,7},{7,6},{8,9},{9,8},{10,11... | collective-permute-start | bytes 1179656 | tf_op jit(solution)/shard_map/ppermute | solution.py:184
  81.2 1.3 copy-start.1
  82.5 1.0 copy-start.3
  83.5 1.0 copy-start.5
  98.6 21.6 %copy-start.6 = (bf16[32,48,128]{2,1,0:T(8,128)(2,1)}, bf16[32,48,128]{2,1,0:T(8,128)(2,1)S(1)}, u32[]{:S(2)}) copy-start(bf16[32,48,128]{2,1,0:T(8,128)(2,1)S(1)} %get-tuple-element.5) | copy-start | bytes 1179652
  120.2 24.4 %all-to-all-start.3 = ((bf16[32,48,128]{2,1,0:T(8,128)(2,1)}), bf16[32,48,128]{2,1,0:T(8,128)(2,1)S(1)}, u32[]{:S(2)}, u32[]{:S(2)}) async-start(bf16[32,48,128]{2,1,0:T(8,128)(2,1)} %copy-done.6), calls=%async_computation.3 | async-start | bytes 786432 | tf_op jit(solution)/shard_map/all_to_all | solution.py:221
  144.7 0.6 copy-start.8
  145.4 0.7 slice-start

commit v3 on v2

--- a/solution.py
+++ b/solution.py
@@ -11,6 +11,7 @@
 BLOCK = 128
 LOG2E = 1.4426950408889634
 UNROLL = 4
+CHUNKS = 8
 
 NN = (((1,), (0,)), ((), ()))
 NT = (((1,), (1,)), ((), ()))
@@ -55,7 +56,8 @@
             kvt = jnp.concatenate([kvt_ref[n] for n in some], axis=1)
             mixed = mm(kvt, pair)
             dt_ref[BLOCK:, row(b)] = (mixed[:HD, :BLOCK] * scale).astype(jnp.bfloat16)
-            o_ref[row(b), :] = mixed[HD:, BLOCK:].T.astype(jnp.bfloat16)
+            out = mixed[HD:, BLOCK:]
+            o_ref[row(b), :] = jnp.concatenate([out, out], axis=0).T.astype(jnp.bfloat16)
         for some, pair, r in zip(names, sent, rhs):
             back = mm(pair, r)
             for j in range(slots):
@@ -68,32 +70,23 @@
     lax.fori_loop(0, n_blocks // UNROLL, body, 0)
 
 
-def block_places(me, peers):
-    core = lax.rem(me, 2)
-    chip = lax.div(me, 2)
-    chips = peers // 2
-    ahead = 1 - 2 * core
-    places = [me, me + ahead]
-    for k in range(1, chips // 2 + 1):
-        back = lax.rem(chip - k * ahead + chips, chips)
-        forth = lax.rem(chip + k * ahead + chips, chips)
-        places += [2 * back + core, 2 * forth + 1 - core]
-        if k < chips // 2:
-            places += [2 * back + 1 - core, 2 * forth + core]
-    return places
-
-
-def head_kernel(*refs):
-    me_ref, pairs_ref, valid_ref, w_ref, cot_ref = refs[:5]
-    (
-        att_ref, wg_ref, vol_ref, kv_ref, kvt_ref, q_ref, do_ref, acc_ref, dt_ref, o_ref,
-    ) = refs[-10:]
-    blocks = refs[5:-10]
+def head_kernel(
+    me_ref, pairs_ref, valid_ref, w_ref, cot_ref, vol_hbm, mine_ref, give_ref, wg_ref,
+    vol_ref, kv_ref, kvt_ref, q_ref, do_ref, acc_ref, dt_ref, o_ref, sems,
+):
     rows, width = vol_ref.shape
-    toks = blocks[0].shape[0]
     n_blocks, slots = pairs_ref.shape
     peers, half, _ = cot_ref.shape
     scale = HD ** -0.5
+    chunk = rows // CHUNKS
+    copies = [
+        pltpu.make_async_copy(
+            vol_hbm.at[pl.ds(c * chunk, chunk)], vol_ref.at[pl.ds(c * chunk, chunk)], sems.at[c]
+        )
+        for c in range(CHUNKS)
+    ]
+    for copy in copies:
+        copy.start()
 
     acc_ref[...] = jnp.zeros_like(acc_ref)
     blank = jnp.zeros((half, HD), jnp.bfloat16)
@@ -102,10 +95,10 @@
         do_ref[pl.ds(2 * half * s, half), :] = jnp.concatenate([blank, both[:, :HD]], axis=1)
         do_ref[pl.ds(2 * half * s + half, half), :] = jnp.concatenate([blank, both[:, HD:]], axis=1)
 
-    for place, block_ref in zip(block_places(me_ref[0], peers), blocks):
-        at = pl.ds(pl.multiple_of(place * toks, HD), toks)
-        vol_ref[at, :] = block_ref[...]
-        got = mm(block_ref[...], w_ref[...])
+    for c in range(CHUNKS):
+        copies[c].wait()
+        at = pl.ds(c * chunk, chunk)
+        got = mm(vol_ref[at, :], w_ref[...])
         q_ref[at, :] = got[:, BLOCK:].astype(jnp.bfloat16)
         kv_ref[at, :] = got[:, :BLOCK].astype(jnp.bfloat16)
     for b in range(n_blocks):
@@ -113,14 +106,14 @@
 
     attend(n_blocks, slots, pairs_ref, valid_ref, kv_ref, kvt_ref, q_ref, do_ref, acc_ref, dt_ref, o_ref)
 
-    for s in range(peers):
-        att_ref[s] = jnp.concatenate(
-            [
-                o_ref[pl.ds(2 * half * s, half), :],
-                o_ref[pl.ds(2 * half * s + half, half), :],
-            ],
-            axis=1,
-        )
+    core = lax.rem(me_ref[0], 2)
+    chip = lax.div(me_ref[0], 2)
+    chips = peers // 2
+    for k in range(chips):
+        to = 2 * lax.rem(chip + k, chips)
+        for ref, side in ((mine_ref, core), (give_ref, 1 - core)):
+            one = o_ref[pl.ds(pl.multiple_of((to + side) * (2 * half), HD), 2 * half), :]
+            ref[k] = one
     lane = lax.broadcasted_iota(jnp.int32, (BLOCK, BLOCK), 1)
     factor = jnp.where(lane < HD, scale, 1.0)
     for b in range(n_blocks):
@@ -140,21 +133,23 @@
             wg_ref[owner, mine:] = jnp.concatenate([q_rows[:mine // 2], q_rows[mine // 2:]], axis=1)
 
 
-def head_call(me, pairs, valid, w, cot, blocks, owners):
-    toks, width = blocks[0].shape
-    rows = toks * len(blocks)
+def head_call(me, pairs, valid, w, cot, vol, owners):
+    rows, width = vol.shape
+    peers, half, _ = cot.shape
     n_blocks = rows // BLOCK
     mine = width // owners
     vmem = pl.BlockSpec(memory_space=pltpu.VMEM)
     smem = pl.BlockSpec(memory_space=pltpu.SMEM)
+    piece = jax.ShapeDtypeStruct((peers // 2, 2 * half, BLOCK), jnp.bfloat16)
     return pl.pallas_call(
         head_kernel,
         out_shape=(
-            jax.ShapeDtypeStruct(cot.shape, jnp.bfloat16),
+            piece,
+            piece,
             jax.ShapeDtypeStruct((owners, mine + mine // 2, BLOCK), jnp.bfloat16),
         ),
-        in_specs=[smem] * 3 + [vmem] * (2 + len(blocks)),
-        out_specs=(vmem, vmem),
+        in_specs=[smem] * 3 + [vmem] * 2 + [pl.BlockSpec(memory_space=pl.ANY)],
+        out_specs=(vmem, vmem, vmem),
         scratch_shapes=[
             pltpu.VMEM((rows, width), jnp.bfloat16),
             pltpu.VMEM((rows, BLOCK), jnp.bfloat16),
@@ -163,35 +158,67 @@
             pltpu.VMEM((rows, BLOCK), jnp.bfloat16),
             pltpu.VMEM((n_blocks, BLOCK, BLOCK), jnp.float32),
             pltpu.VMEM((BLOCK + HD, rows), jnp.bfloat16),
-            pltpu.VMEM((rows, HD), jnp.bfloat16),
+            pltpu.VMEM((rows, BLOCK), jnp.bfloat16),
+            pltpu.SemaphoreType.DMA((CHUNKS,)),
         ],
-        compiler_params=pltpu.CompilerParams(vmem_limit_bytes=32 * 2**20),
+        compiler_params=pltpu.CompilerParams(vmem_limit_bytes=56 * 2**20),
         name="head",
-    )(me, pairs, valid, w, cot, *blocks)
-
-
-def gather(vol):
+    )(me, pairs, valid, w, cot, vol)
+
+
+def merge_kernel(me_ref, mine_ref, got_ref, *out_refs):
+    core = lax.rem(me_ref[0], 2)
+    toks = mine_ref.shape[1]
+    lane = lax.broadcasted_iota(jnp.int32, (toks, BLOCK), 1)
+    own = lax.div(lane, HD) == core
+    for k, out_ref in enumerate(out_refs):
+        out_ref[...] = jnp.where(own, mine_ref[k], got_ref[k])
+
+
+def merge_call(me, mine, got):
+    vmem = pl.BlockSpec(memory_space=pltpu.VMEM)
+    return pl.pallas_call(
+        merge_kernel,
+        out_shape=[jax.ShapeDtypeStruct(mine.shape[1:], mine.dtype)] * mine.shape[0],
+        in_specs=[pl.BlockSpec(memory_space=pltpu.SMEM), vmem, vmem],
+        out_specs=[vmem] * mine.shape[0],
+        compiler_params=pltpu.CompilerParams(vmem_limit_bytes=8 * 2**20),
+        name="merge",
+    )(me, mine, got)
+
+
+def place_kernel(me_ref, *refs):
+    out_ref = refs[-1]
+    chips = len(refs) - 1
+    chip = lax.div(me_ref[0], 2)
+    for k, ref in enumerate(refs[:-1]):
+        at = pl.multiple_of(lax.rem(chip - k + chips, chips) * BLOCK, BLOCK)
+        out_ref[:, pl.ds(at, BLOCK)] = ref[...]
+
+
+def place_call(me, parts):
+    toks = parts[0].shape[0]
+    vmem = pl.BlockSpec(memory_space=pltpu.VMEM)
+    return pl.pallas_call(
+        place_kernel,
+        out_shape=jax.ShapeDtypeStruct((toks, len(parts) * BLOCK), parts[0].dtype),
+        in_specs=[pl.BlockSpec(memory_space=pltpu.SMEM)] + [vmem] * len(parts),
+        out_specs=vmem,
+        compiler_params=pltpu.CompilerParams(vmem_limit_bytes=8 * 2**20),
+        name="place",
+    )(me, *parts)
+
+
+def return_heads(me, mine, give):
     peers = lax.axis_size("seq")
     chips = peers // 2
-    onward = [
-        (2 * z + c, 2 * ((z + 1) % chips) if c == 0 else 2 * ((z - 1) % chips) + 1)
-        for z in range(chips)
-        for c in range(2)
+    got = lax.ppermute(give, "seq", [(i, i ^ 1) for i in range(peers)])
+    parts = merge_call(me, mine, got)
+    here = [parts[0]] + [
+        lax.ppermute(parts[k], "seq", [(i, (i + 2 * k) % peers) for i in range(peers)])
+        for k in range(1, chips)
     ]
-    twin = [(i, i ^ 1) for i in range(peers)]
-
-    def swap(x):
-        return lax.ppermute(x, "seq", twin)
-
-    own, other = vol, swap(vol)
-    blocks = [own, other]
-    for k in range(1, chips // 2 + 1):
-        own = lax.ppermute(own, "seq", onward)
-        blocks += [own, swap(own)]
-        if k < chips // 2:
-            other = lax.ppermute(other, "seq", onward)
-            blocks += [other, swap(other)]
-    return blocks
+    return place_call(me, here)
 
 
 def local(volume, cotangent, weights, pairs, valid):
@@ -202,25 +229,25 @@
     w_rows = weights.shape[0]
     half = toks // 2
 
-    blocks = gather(vol)
     me = lax.axis_index("seq").reshape(1)
+    gathered = lax.all_gather(vol, "seq", axis=0, tiled=True)
+
+    cot = cot.reshape(2, half, peers, HD).transpose(2, 1, 0, 3).reshape(peers, half, 2 * HD)
+    cot = lax.all_to_all(cot, "seq", split_axis=0, concat_axis=0, tiled=True)
+    weights, cot = lax.optimization_barrier((weights, cot))
 
     column = lax.axis_index("seq") * HD
-    mine = lax.dynamic_slice_in_dim(weights, column, HD, axis=2)
-    mine = jnp.stack([mine[:, 1], mine[:, 2], mine[:, 0]], axis=1).reshape(-1, BLOCK)
-    sent = jnp.broadcast_to(mine[None], (owners, *mine.shape))
+    part = lax.dynamic_slice_in_dim(weights, column, HD, axis=2)
+    part = jnp.stack([part[:, 1], part[:, 2], part[:, 0]], axis=1).reshape(-1, BLOCK)
+    sent = jnp.broadcast_to(part[None], (owners, *part.shape))
     w = lax.all_to_all(sent, "dp", split_axis=0, concat_axis=0, tiled=True)
     w = w.reshape(owners * w_rows, 3 * HD)
     w = jnp.pad(w, ((0, 0), (0, HD)))
 
-    cot = cot.reshape(2, half, peers, HD).transpose(2, 1, 0, 3).reshape(peers, half, 2 * HD)
-    cot = lax.all_to_all(cot, "seq", split_axis=0, concat_axis=0, tiled=True)
-
-    att, wg = head_call(me, pairs[0, 0], valid[0, 0], w, cot, blocks, owners)
+    mine, give, wg = head_call(me, pairs[0, 0], valid[0, 0], w, cot, gathered, owners)
 
     wg = lax.all_to_all(wg, "dp", split_axis=0, concat_axis=0, tiled=True)
-    att = lax.all_to_all(att, "seq", split_axis=0, concat_axis=0, tiled=True)
-    att = att.reshape(peers, half, 2, HD).transpose(2, 1, 0, 3).reshape(1, toks, peers * HD)
+    att = return_heads(me, mine, give)[None]
     total = jnp.sum(wg.astype(jnp.float32), axis=0)
     kv = total[:w_rows].reshape(w_rows, 2, HD)
     q = total[w_rows:].reshape(w_rows // 2, 2, HD).transpose(1, 0, 2).reshape(w_rows, 1, HD)

time: 148 us -> 138 us (0.932); the launches traced: 147 us -> 135 us
  blocking collectives: 21.6 us -> 0 us
  waiting for transfers between devices: 15.6 us -> 35 us
  starting transfers between devices: 73.2 us -> 59.7 us
  between operations: 1.04 us -> 14.3 us
  local copies, waits for them, and re-layouts: 21.2 us -> 8.04 us
  Pallas kernels: 14.1 us -> 18.2 us
    all_to_all x1 -> x0, blocking collectives: 21.6 us -> none  [local(): att = lax.all_to_all(att, 'seq', split_axis=0, concat_axis=0, tiled=True)]
    ppermute x15 -> x8, starting transfers between devices: 47.1 us -> 28.3 us  [the longest x7 25.8 us: return_heads(): lax.ppermute(parts[k], 'seq', [(i, (i + 2 * k) % peers) for i in range(pe...]
    all_to_all x1, waiting for transfers between devices: 0.01 us -> 14 us  [local(): cot = lax.all_to_all(cot, 'seq', split_axis=0, concat_axis=0, tiled=True)]
    all_to_all x1, waiting for transfers between devices: 0.01 us -> 13 us  [local(): w = lax.all_to_all(sent, 'dp', split_axis=0, concat_axis=0, tiled=True)]
    all_to_all x1, waiting for transfers between devices: 12.7 us -> 0.01 us  [local(): wg = lax.all_to_all(wg, 'dp', split_axis=0, concat_axis=0, tiled=True)]
    unnamed x26 -> x12, local copies, waits for them, and re-layouts: 9.39 us -> 2.84 us
    all_to_all x1, starting transfers between devices: 6.88 us -> 11.8 us  [local(): cot = lax.all_to_all(cot, 'seq', split_axis=0, concat_axis=0, tiled=True)]
    pallas_call x1 -> x3, Pallas kernels: 14.1 us -> 18.2 us  [the longest x1 17.2 us: head_call(): pl.pallas_call(head_kernel, out_shape=(piece, piece, jax.ShapeDtypeStruct...]
  transfers between devices with their start and end apart: 18 -> 12, of which waited for: 2 -> 5; matrix products, arithmetic and copies ran while one was open for 10% -> 5% of each run, Pallas kernels for 0% -> 1%
where the time goes in v3:
time: 138 us; the launch traced here: 135 us
  starting transfers between devices  59.7 us (43%)
  waiting for transfers between devices  35 us (25%)
  Pallas kernels  18.2 us (13%)
  between operations  14.3 us (10%)
  local copies, waits for them, and re-layouts  8.04 us (6%)
    ppermute x7, starting transfers between devices, return_heads(): lax.ppermute(parts[k], 'seq', [(i, (i + 2 * k) % peers) for i in range(pe...  25.8 us
    pallas_call x1, Pallas kernels, head_call(): pl.pallas_call(head_kernel, out_shape=(piece, piece, jax.ShapeDtypeStruct...  17.2 us
    all_to_all x1, waiting for transfers between devices, local(): cot = lax.all_to_all(cot, 'seq', split_axis=0, concat_axis=0, tiled=True)  14 us
    all_to_all x1, waiting for transfers between devices, local(): w = lax.all_to_all(sent, 'dp', split_axis=0, concat_axis=0, tiled=True)  13 us
    all_to_all x1, starting transfers between devices, local(): cot = lax.all_to_all(cot, 'seq', split_axis=0, concat_axis=0, tiled=True)  11.8 us
    all_to_all x1, starting transfers between devices, local(): w = lax.all_to_all(sent, 'dp', split_axis=0, concat_axis=0, tiled=True)  10.1 us
    all_to_all x1, starting transfers between devices, local(): wg = lax.all_to_all(wg, 'dp', split_axis=0, concat_axis=0, tiled=True)  9.51 us
    all_gather x1, waiting for transfers between devices, local(): gathered = lax.all_gather(vol, 'seq', axis=0, tiled=True)  3.12 us
  transfers between devices with their start and end apart: 12, of which 5 were waited for; matrix products, arithmetic and copies ran while one was open for 5% of the time, Pallas kernels for 1%

profile of v3, /device:TPU:1, one launch (start us, length us, event | category | flops | bytes accessed | tf_op | source)
XLA Modules:
  0.0 135.3 jit_solution(2329478947791147830)
XLA Ops:
  7.2 0.7 all-gather.3.cloned.1.call-update
  7.9 1.2 copy.17
  9.1 0.3 reshape_squeeze.3
  9.4 0.1 copy.18
  9.6 1.0 copy.19
  10.5 11.8 %all-to-all-start = ((bf16[16,96,128]{2,1,0:T(8,128)(2,1)}), bf16[16,96,128]{2,1,0:T(8,128)(2,1)S(1)}, u32[]{:S(2)}, u32[]{:S(2)}) async-start(bf16[16,96,128]{2,1,0:T(8,128)(2,1)} %copy.19), calls=%async_computation | async-start | bytes 786432 | tf_op jit(solution)/shard_map/all_to_all | solution.py:236
  22.3 14.0 %all-to-all-done.cot_ref = bf16[16,96,128]{2,1,0:T(8,128)(2,1)S(1)} async-done(((bf16[16,96,128]{2,1,0:T(8,128)(2,1)}), bf16[16,96,128]{2,1,0:T(8,128)(2,1)S(1)}, u32[]{:S(2)}, u32[]{:S(2)}) %all-to-all-start) | async-done | bytes 393248 | tf_op jit(solution)/shard_map/all_to_all | solution.py:236
  36.6 0.1 broadcast_in_dim.10
  36.7 0.8 broadcast_in_dim.11
  37.5 10.1 %all-to-all-start.1 = ((bf16[32,48,128]{2,1,0:T(8,128)(2,1)}), bf16[32,48,128]{2,1,0:T(8,128)(2,1)S(1)}, u32[]{:S(2)}, u32[]{:S(2)}) async-start(bf16[32,48,128]{2,1,0:T(8,128)(2,1)} %broadcast_in_dim.11), calls=%async_computation.1 | async-start | bytes 786432 | tf_op jit(solution)/shard_map/all_to_all | solution.py:243
  47.5 0.7 copy.21.pairs_ref
  48.2 0.7 copy.22.valid_ref
  48.9 13.0 %all-to-all-done.1 = bf16[32,48,128]{2,1,0:T(8,128)(2,1)S(1)} async-done(((bf16[32,48,128]{2,1,0:T(8,128)(2,1)}), bf16[32,48,128]{2,1,0:T(8,128)(2,1)S(1)}, u32[]{:S(2)}, u32[]{:S(2)}) %all-to-all-start.1) | async-done | bytes 393248 | tf_op jit(solution)/shard_map/all_to_all | solution.py:243
  61.9 0.3 reshape.25
  62.3 0.9 pad.4.w_ref
  63.2 3.1 %all-gather.3.cloned.1.call-done = bf16[1,3072,1024]{2,1,0:T(8,128)(2,1)} async-done(((bf16[1,192,1024]{2,1,0:T(8,128)(2,1)}), bf16[1,3072,1024]{2,1,0:T(8,128)(2,1)}) %all-gather.3.cloned.1.call-update) | async-done | bytes 6291472 | tf_op jit(solution)/shard_map/all_gather | solution.py:233
  66.3 17.2 %head.1 = (bf16[8,192,128]{2,1,0:T(8,128)(2,1)}, bf16[8,192,128]{2,1,0:T(8,128)(2,1)}, bf16[32,48,128]{2,1,0:T(8,128)(2,1)}) custom-call(s32[1]{0:T(128)} %bitcast.me_ref, s32[24,4]{1,0:T(8,128)} %copy.21.pairs_ref, s32[24,4]{1,0:T(8,128)} %copy.22.valid_ref, bf16[1024,256]{1,0:T(8,128)(2,1)} %pad.4.w_ref, bf16[16,96,128]{2,1,0:T(8,128)(2,1)} %copy-done.2, ...), custom_call_target="tpu_custom_call" | custom-call | tf_op jit(solution)/shard_map/head/pallas_call | solution.py:144
  83.5 9.5 %all-to-all-start.2 = ((bf16[32,48,128]{2,1,0:T(8,128)(2,1)}), bf16[32,48,128]{2,1,0:T(8,128)(2,1)S(1)}, u32[]{:S(2)}, u32[]{:S(2)}) async-start(bf16[32,48,128]{2,1,0:T(8,128)(2,1)} %get-tuple-element.27), calls=%async_computation.2 | async-start | bytes 786432 | tf_op jit(solution)/shard_map/all_to_all | solution.py:249
  93.0 2.4 %collective-permute-start = (bf16[8,192,128]{2,1,0:T(8,128)(2,1)}, bf16[8,192,128]{2,1,0:T(8,128)(2,1)S(1)}, u32[]{:S(2)}, u32[]{:S(2)}) collective-permute-start(bf16[8,192,128]{2,1,0:T(8,128)(2,1)} %get-tuple-element.18), channel_id=1, source_target_pairs={{0,1},{1,0},{2,3},{3,2},{4,5},{5,4},{6,7},{7,6},{8,9},{9,8},{10,11... | collective-permute-start | bytes 1179656 | tf_op jit(solution)/shard_map/ppermute | solution.py:215
  95.5 1.5 %collective-permute-done.got_ref = bf16[8,192,128]{2,1,0:T(8,128)(2,1)S(1)} collective-permute-done((bf16[8,192,128]{2,1,0:T(8,128)(2,1)}, bf16[8,192,128]{2,1,0:T(8,128)(2,1)S(1)}, u32[]{:S(2)}, u32[]{:S(2)}) %collective-permute-start) | collective-permute-done | bytes 393248 | tf_op jit(solution)/shard_map/ppermute | solution.py:215
  97.0 1.0 copy-done.1
  98.0 0.1 merge.1
  98.1 2.5 %collective-permute-start.1 = (bf16[192,128]{1,0:T(8,128)(2,1)S(1)}, bf16[192,128]{1,0:T(8,128)(2,1)S(1)}, u32[]{:S(2)}, u32[]{:S(2)}) collective-permute-start(bf16[192,128]{1,0:T(8,128)(2,1)S(1)} %get-tuple-element.20), channel_id=1, source_target_pairs={{0,2},{1,3},{2,4},{3,5},{4,6},{5,7},{6,8},{7,9},{8,10},{9,11},{10,... | collective-permute-start | bytes 147464 | tf_op jit(solution)/shard_map/ppermute | solution.py:218
  100.6 4.5 %collective-permute-start.2 = (bf16[192,128]{1,0:T(8,128)(2,1)S(1)}, bf16[192,128]{1,0:T(8,128)(2,1)S(1)}, u32[]{:S(2)}, u32[]{:S(2)}) collective-permute-start(bf16[192,128]{1,0:T(8,128)(2,1)S(1)} %get-tuple-element.21), channel_id=1, source_target_pairs={{0,4},{1,5},{2,6},{3,7},{4,8},{5,9},{6,10},{7,11},{8,12},{9,13},{1... | collective-permute-start | bytes 147464 | tf_op jit(solution)/shard_map/ppermute | solution.py:218
  105.1 3.2 %collective-permute-start.3 = (bf16[192,128]{1,0:T(8,128)(2,1)S(1)}, bf16[192,128]{1,0:T(8,128)(2,1)S(1)}, u32[]{:S(2)}, u32[]{:S(2)}) collective-permute-start(bf16[192,128]{1,0:T(8,128)(2,1)S(1)} %get-tuple-element.22), channel_id=1, source_target_pairs={{0,6},{1,7},{2,8},{3,9},{4,10},{5,11},{6,12},{7,13},{8,14},{9,15},... | collective-permute-start | bytes 147464 | tf_op jit(solution)/shard_map/ppermute | solution.py:218
  108.3 4.8 %collective-permute-start.4 = (bf16[192,128]{1,0:T(8,128)(2,1)S(1)}, bf16[192,128]{1,0:T(8,128)(2,1)S(1)}, u32[]{:S(2)}, u32[]{:S(2)}) collective-permute-start(bf16[192,128]{1,0:T(8,128)(2,1)S(1)} %get-tuple-element.23), channel_id=1, source_target_pairs={{0,8},{1,9},{2,10},{3,11},{4,12},{5,13},{6,14},{7,15},{8,0},{9,1},... | collective-permute-start | bytes 147464 | tf_op jit(solution)/shard_map/ppermute | solution.py:218
  113.1 4.0 %collective-permute-start.5 = (bf16[192,128]{1,0:T(8,128)(2,1)S(1)}, bf16[192,128]{1,0:T(8,128)(2,1)S(1)}, u32[]{:S(2)}, u32[]{:S(2)}) collective-permute-start(bf16[192,128]{1,0:T(8,128)(2,1)S(1)} %get-tuple-element.24), channel_id=1, source_target_pairs={{0,10},{1,11},{2,12},{3,13},{4,14},{5,15},{6,0},{7,1},{8,2},{9,3},... | collective-permute-start | bytes 147464 | tf_op jit(solution)/shard_map/ppermute | solution.py:218
  117.1 4.7 %collective-permute-start.6 = (bf16[192,128]{1,0:T(8,128)(2,1)S(1)}, bf16[192,128]{1,0:T(8,128)(2,1)S(1)}, u32[]{:S(2)}, u32[]{:S(2)}) collective-permute-start(bf16[192,128]{1,0:T(8,128)(2,1)S(1)} %get-tuple-element.25), channel_id=1, source_target_pairs={{0,12},{1,13},{2,14},{3,15},{4,0},{5,1},{6,2},{7,3},{8,4},{9,5},{1... | collective-permute-start | bytes 147464 | tf_op jit(solution)/shard_map/ppermute | solution.py:218
  121.8 2.2 %collective-permute-start.7 = (bf16[192,128]{1,0:T(8,128)(2,1)S(1)}, bf16[192,128]{1,0:T(8,128)(2,1)S(1)}, u32[]{:S(2)}, u32[]{:S(2)}) collective-permute-start(bf16[192,128]{1,0:T(8,128)(2,1)S(1)} %get-tuple-element.26), channel_id=1, source_target_pairs={{0,14},{1,15},{2,0},{3,1},{4,2},{5,3},{6,4},{7,5},{8,6},{9,7},{10,... | collective-permute-start | bytes 147464 | tf_op jit(solution)/shard_map/ppermute | solution.py:218
  124.1 2.6 %collective-permute-done.7.refs_7_ = bf16[192,128]{1,0:T(8,128)(2,1)S(1)} collective-permute-done((bf16[192,128]{1,0:T(8,128)(2,1)S(1)}, bf16[192,128]{1,0:T(8,128)(2,1)S(1)}, u32[]{:S(2)}, u32[]{:S(2)}) %collective-permute-start.7) | collective-permute-done | bytes 49184 | tf_op jit(solution)/shard_map/ppermute | solution.py:218
  126.7 0.9 place.1
  127.9 0.6 copy.25
  (28 shorter events, 0.6 us)
Async XLA Ops:
  7.2 29.2 %copy-start = (bf16[32,3,1024]{2,0,1:T(8,128)(2,1)S(1)}, bf16[32,3,1024]{2,0,1:T(8,128)(2,1)}, u32[]{:S(2)}) copy-start(bf16[32,3,1024]{2,0,1:T(8,128)(2,1)} %param.7) | copy-start | bytes 589828
  7.2 40.4 %copy-start.3 = (s32[1,1,24,4]{2,3,1,0:T(4,128)S(1)}, s32[1,1,24,4]{2,3,1,0:T(4,128)}, u32[]{:S(2)}) copy-start(s32[1,1,24,4]{2,3,1,0:T(4,128)} %param.8) | copy-start | bytes 1156
  7.2 41.0 %copy-start.4 = (s32[1,1,24,4]{2,3,1,0:T(4,128)S(1)}, s32[1,1,24,4]{2,3,1,0:T(4,128)}, u32[]{:S(2)}) copy-start(s32[1,1,24,4]{2,3,1,0:T(4,128)} %param.9) | copy-start | bytes 1156
  7.2 59.1 %all-gather.3.cloned.1.call-start = ((), (), s32[]{:S(2)}) async-start(), calls=%async_computation.3 | async-start | bytes 6684672 | tf_op jit(solution)/shard_map/all_gather | solution.py:233
  10.5 25.9 %all-to-all-start = ((bf16[16,96,128]{2,1,0:T(8,128)(2,1)}), bf16[16,96,128]{2,1,0:T(8,128)(2,1)S(1)}, u32[]{:S(2)}, u32[]{:S(2)}) async-start(bf16[16,96,128]{2,1,0:T(8,128)(2,1)} %copy.19), calls=%async_computation | async-start | bytes 786432 | tf_op jit(solution)/shard_map/all_to_all | solution.py:236
  36.4 29.9 %copy-start.2 = (bf16[16,96,128]{2,1,0:T(8,128)(2,1)}, bf16[16,96,128]{2,1,0:T(8,128)(2,1)S(1)}, u32[]{:S(2)}) copy-start(bf16[16,96,128]{2,1,0:T(8,128)(2,1)S(1)} %all-to-all-done.cot_ref) | copy-start | bytes 1179652
  37.5 24.5 %all-to-all-start.1 = ((bf16[32,48,128]{2,1,0:T(8,128)(2,1)}), bf16[32,48,128]{2,1,0:T(8,128)(2,1)S(1)}, u32[]{:S(2)}, u32[]{:S(2)}) async-start(bf16[32,48,128]{2,1,0:T(8,128)(2,1)} %broadcast_in_dim.11), calls=%async_computation.1 | async-start | bytes 786432 | tf_op jit(solution)/shard_map/all_to_all | solution.py:243
  83.5 44.0 %all-to-all-start.2 = ((bf16[32,48,128]{2,1,0:T(8,128)(2,1)}), bf16[32,48,128]{2,1,0:T(8,128)(2,1)S(1)}, u32[]{:S(2)}, u32[]{:S(2)}) async-start(bf16[32,48,128]{2,1,0:T(8,128)(2,1)} %get-tuple-element.27), calls=%async_computation.2 | async-start | bytes 786432 | tf_op jit(solution)/shard_map/all_to_all | solution.py:249
  93.0 4.0 %collective-permute-start = (bf16[8,192,128]{2,1,0:T(8,128)(2,1)}, bf16[8,192,128]{2,1,0:T(8,128)(2,1)S(1)}, u32[]{:S(2)}, u32[]{:S(2)}) collective-permute-start(bf16[8,192,128]{2,1,0:T(8,128)(2,1)} %get-tuple-element.18), channel_id=1, source_target_pairs={{0,1},{1,0},{2,3},{3,2},{4,5},{5,4},{6,7},{7,6},{8,9},{9,8},{10,11... | collective-permute-start | bytes 1179656 | tf_op jit(solution)/shard_map/ppermute | solution.py:215
  97.0 1.0 copy-start.1
  98.1 18.9 %collective-permute-start.1 = (bf16[192,128]{1,0:T(8,128)(2,1)S(1)}, bf16[192,128]{1,0:T(8,128)(2,1)S(1)}, u32[]{:S(2)}, u32[]{:S(2)}) collective-permute-start(bf16[192,128]{1,0:T(8,128)(2,1)S(1)} %get-tuple-element.20), channel_id=1, source_target_pairs={{0,2},{1,3},{2,4},{3,5},{4,6},{5,7},{6,8},{7,9},{8,10},{9,11},{10,... | collective-permute-start | bytes 147464 | tf_op jit(solution)/shard_map/ppermute | solution.py:218
  100.6 21.2 %collective-permute-start.2 = (bf16[192,128]{1,0:T(8,128)(2,1)S(1)}, bf16[192,128]{1,0:T(8,128)(2,1)S(1)}, u32[]{:S(2)}, u32[]{:S(2)}) collective-permute-start(bf16[192,128]{1,0:T(8,128)(2,1)S(1)} %get-tuple-element.21), channel_id=1, source_target_pairs={{0,4},{1,5},{2,6},{3,7},{4,8},{5,9},{6,10},{7,11},{8,12},{9,13},{1... | collective-permute-start | bytes 147464 | tf_op jit(solution)/shard_map/ppermute | solution.py:218
  105.1 18.9 %collective-permute-start.3 = (bf16[192,128]{1,0:T(8,128)(2,1)S(1)}, bf16[192,128]{1,0:T(8,128)(2,1)S(1)}, u32[]{:S(2)}, u32[]{:S(2)}) collective-permute-start(bf16[192,128]{1,0:T(8,128)(2,1)S(1)} %get-tuple-element.22), channel_id=1, source_target_pairs={{0,6},{1,7},{2,8},{3,9},{4,10},{5,11},{6,12},{7,13},{8,14},{9,15},... | collective-permute-start | bytes 147464 | tf_op jit(solution)/shard_map/ppermute | solution.py:218
  108.3 15.7 %collective-permute-start.4 = (bf16[192,128]{1,0:T(8,128)(2,1)S(1)}, bf16[192,128]{1,0:T(8,128)(2,1)S(1)}, u32[]{:S(2)}, u32[]{:S(2)}) collective-permute-start(bf16[192,128]{1,0:T(8,128)(2,1)S(1)} %get-tuple-element.23), channel_id=1, source_target_pairs={{0,8},{1,9},{2,10},{3,11},{4,12},{5,13},{6,14},{7,15},{8,0},{9,1},... | collective-permute-start | bytes 147464 | tf_op jit(solution)/shard_map/ppermute | solution.py:218
  113.1 11.0 %collective-permute-start.5 = (bf16[192,128]{1,0:T(8,128)(2,1)S(1)}, bf16[192,128]{1,0:T(8,128)(2,1)S(1)}, u32[]{:S(2)}, u32[]{:S(2)}) collective-permute-start(bf16[192,128]{1,0:T(8,128)(2,1)S(1)} %get-tuple-element.24), channel_id=1, source_target_pairs={{0,10},{1,11},{2,12},{3,13},{4,14},{5,15},{6,0},{7,1},{8,2},{9,3},... | collective-permute-start | bytes 147464 | tf_op jit(solution)/shard_map/ppermute | solution.py:218
  117.1 7.0 %collective-permute-start.6 = (bf16[192,128]{1,0:T(8,128)(2,1)S(1)}, bf16[192,128]{1,0:T(8,128)(2,1)S(1)}, u32[]{:S(2)}, u32[]{:S(2)}) collective-permute-start(bf16[192,128]{1,0:T(8,128)(2,1)S(1)} %get-tuple-element.25), channel_id=1, source_target_pairs={{0,12},{1,13},{2,14},{3,15},{4,0},{5,1},{6,2},{7,3},{8,4},{9,5},{1... | collective-permute-start | bytes 147464 | tf_op jit(solution)/shard_map/ppermute | solution.py:218
  121.8 4.8 %collective-permute-start.7 = (bf16[192,128]{1,0:T(8,128)(2,1)S(1)}, bf16[192,128]{1,0:T(8,128)(2,1)S(1)}, u32[]{:S(2)}, u32[]{:S(2)}) collective-permute-start(bf16[192,128]{1,0:T(8,128)(2,1)S(1)} %get-tuple-element.26), channel_id=1, source_target_pairs={{0,14},{1,15},{2,0},{3,1},{4,2},{5,3},{6,4},{7,5},{8,6},{9,7},{10,... | collective-permute-start | bytes 147464 | tf_op jit(solution)/shard_map/ppermute | solution.py:218
Sparse Core Ops, SparseCore 0:
  10.2 56.1 all-gather.2

commit v4 on v1

v4 whole, which is shorter than its diff:
```python
import functools

import jax
import jax.numpy as jnp
from jax import lax
from jax.experimental import pallas as pl
from jax.experimental.pallas import tpu as pltpu
from jax.sharding import PartitionSpec as P

HD = 64
BLOCK = 128
LOG2E = 1.4426950408889634
UNROLL = 6
AHEAD = 6
CHUNKS = 8

NN = (((1,), (0,)), ((), ()))
NT = (((1,), (1,)), ((), ()))


def mm(a, b, dims=NN):
    return lax.dot_general(a, b, dims, preferred_element_type=jnp.float32)


def row(b):
    return pl.ds(pl.multiple_of(b * BLOCK, BLOCK), BLOCK)


def softmax(scores, live):
    parts = [scores[j * BLOCK:(j + 1) * BLOCK] * (HD ** -0.5 * LOG2E) for j in range(len(live))]
    tops = [
        jnp.where(ok, jnp.max(part, axis=0, keepdims=True), -jnp.inf)
        for ok, part in zip(live, parts)
    ]
    top = functools.reduce(jnp.maximum, tops)
    exponent = jnp.concatenate(
        [jnp.exp2(part - jnp.where(ok, top, jnp.inf)) for ok, part in zip(live, parts)], axis=0
    )
    return exponent * (1.0 / jnp.sum(exponent, axis=0, keepdims=True))


def forward_kernel(
    pairs_ref, valid_ref, w_ref, vol_hbm, att_ref, kv_ref, kvt_ref, q_ref, vol_ref, o_ref, sems,
):
    rows = vol_ref.shape[0]
    n_blocks, slots = pairs_ref.shape
    peers, half, _ = att_ref.shape
    chunk = rows // CHUNKS
    copies = [
        pltpu.make_async_copy(
            vol_hbm.at[pl.ds(c * chunk, chunk)], vol_ref.at[pl.ds(c * chunk, chunk)], sems.at[c]
        )
        for c in range(CHUNKS)
    ]
    for copy in copies:
        copy.start()
    for c in range(CHUNKS):
        copies[c].wait()
        at = pl.ds(c * chunk, chunk)
        got = mm(vol_ref[at, :], w_ref[...])
        q_ref[at, :] = got[:, BLOCK:].astype(jnp.bfloat16)
        kv = got[:, :BLOCK].astype(jnp.bfloat16)
        kv_ref[at, :] = kv
        for b in range(chunk // BLOCK):
            kvt_ref[c * (chunk // BLOCK) + b] = kv[b * BLOCK:(b + 1) * BLOCK].T

    def body(i, carry):
        blocks = [i * AHEAD + u for u in range(AHEAD)]
        names = [[pairs_ref[b, j] for j in range(slots)] for b in blocks]
        scores = [
            mm(jnp.concatenate([kv_ref[row(n), :] for n in some], axis=0), q_ref[row(b), :], NT)
            for b, some in zip(blocks, names)
        ]
        probs = [
            softmax(s, [valid_ref[b, j] > 0 for j in range(slots)]).astype(jnp.bfloat16)
            for b, s in zip(blocks, scores)
        ]
        for b, some, p in zip(blocks, names, probs):
            values = jnp.concatenate([kvt_ref[n, HD:] for n in some], axis=1)
            o_ref[row(b), :] = mm(values, p).T.astype(jnp.bfloat16)
        return carry

    lax.fori_loop(0, n_blocks // AHEAD, body, 0)

    for s in range(peers):
        att_ref[s] = jnp.concatenate(
            [
                o_ref[pl.ds(2 * half * s, half), :],
                o_ref[pl.ds(2 * half * s + half, half), :],
            ],
            axis=1,
        )


def forward_call(pairs, valid, w, vol, peers):
    rows, width = vol.shape
    n_blocks = rows // BLOCK
    vmem = pl.BlockSpec(memory_space=pltpu.VMEM)
    smem = pl.BlockSpec(memory_space=pltpu.SMEM)
    return pl.pallas_call(
        forward_kernel,
        out_shape=(
            jax.ShapeDtypeStruct((peers, rows // peers // 2, BLOCK), jnp.bfloat16),
            jax.ShapeDtypeStruct((rows, BLOCK), jnp.bfloat16),
            jax.ShapeDtypeStruct((n_blocks, BLOCK, BLOCK), jnp.bfloat16),
            jax.ShapeDtypeStruct((rows, BLOCK), jnp.bfloat16),
        ),
        in_specs=[smem] * 2 + [vmem, pl.BlockSpec(memory_space=pl.ANY)],
        out_specs=(vmem,) * 4,
        scratch_shapes=[
            pltpu.VMEM((rows, width), jnp.bfloat16),
            pltpu.VMEM((rows, HD), jnp.bfloat16),
            pltpu.SemaphoreType.DMA((CHUNKS,)),
        ],
        compiler_params=pltpu.CompilerParams(vmem_limit_bytes=56 * 2**20),
        name="forward",
    )(pairs, valid, w, vol)


def backward_kernel(
    pairs_ref, valid_ref, cot_ref, kv_ref, kvt_ref, q_ref, vol_hbm, wg_ref,
    vol_ref, do_ref, acc_ref, dt_ref, sem,
):
    rows, width = vol_ref.shape
    n_blocks, slots = pairs_ref.shape
    peers, half, _ = cot_ref.shape
    scale = HD ** -0.5
    copy = pltpu.make_async_copy(vol_hbm, vol_ref, sem)
    copy.start()

    acc_ref[...] = jnp.zeros_like(acc_ref)
    blank = jnp.zeros((half, HD), jnp.bfloat16)
    for s in range(peers):
        both = cot_ref[s]
        do_ref[pl.ds(2 * half * s, half), :] = jnp.concatenate([blank, both[:, :HD]], axis=1)
        do_ref[pl.ds(2 * half * s + half, half), :] = jnp.concatenate([blank, both[:, HD:]], axis=1)

    def body(i, carry):
        blocks = [i * UNROLL + u for u in range(UNROLL)]
        names = [[pairs_ref[b, j] for j in range(slots)] for b in blocks]
        rhs = [jnp.concatenate([q_ref[row(b), :], do_ref[row(b), :]], axis=0) for b in blocks]
        both = [
            mm(jnp.concatenate([kv_ref[row(n), :] for n in some], axis=0), r, NT)
            for some, r in zip(names, rhs)
        ]
        sent = []
        for b, pair in zip(blocks, both):
            probs = softmax(pair[:, :BLOCK], [valid_ref[b, j] > 0 for j in range(slots)])
            weighted = probs * pair[:, BLOCK:]
            row_dot = jnp.sum(weighted, axis=0, keepdims=True)
            score_grad = (weighted - probs * row_dot).astype(jnp.bfloat16)
            sent.append((score_grad, probs.astype(jnp.bfloat16)))
        for b, some, pair in zip(blocks, names, sent):
            keys = jnp.concatenate([kvt_ref[n, :HD] for n in some], axis=1)
            dt_ref[BLOCK:, row(b)] = (mm(keys, pair[0]) * scale).astype(jnp.bfloat16)
        for some, pair, r in zip(names, sent, rhs):
            back = mm(jnp.concatenate(pair, axis=1), r)
            for j in range(slots):
                acc_ref[some[j]] += back[j * BLOCK:(j + 1) * BLOCK]
        return carry

    lax.fori_loop(0, n_blocks // UNROLL, body, 0)

    lane = lax.broadcasted_iota(jnp.int32, (BLOCK, BLOCK), 1)
    factor = jnp.where(lane < HD, scale, 1.0)
    for b in range(n_blocks):
        dt_ref[:BLOCK, b * BLOCK:(b + 1) * BLOCK] = (acc_ref[b] * factor).T.astype(jnp.bfloat16)

    copy.wait()
    owners = wg_ref.shape[0]
    mine = width // owners
    part = 256
    for n in range(width // part):
        got = mm(dt_ref[...], vol_ref[:, n * part:(n + 1) * part])
        kv_part = got[:BLOCK].T.astype(jnp.bfloat16)
        q_part = got[BLOCK:].T.astype(jnp.bfloat16)
        for k in range(part // mine):
            owner = n * (part // mine) + k
            wg_ref[owner, :mine] = kv_part[k * mine:(k + 1) * mine]
            q_rows = q_part[k * mine:(k + 1) * mine]
            wg_ref[owner, mine:] = jnp.concatenate([q_rows[:mine // 2], q_rows[mine // 2:]], axis=1)


def backward_call(pairs, valid, cot, kv, kvt, q, vol, owners):
    rows, width = vol.shape
    n_blocks = rows // BLOCK
    mine = width // owners
    vmem = pl.BlockSpec(memory_space=pltpu.VMEM)
    smem = pl.BlockSpec(memory_space=pltpu.SMEM)
    return pl.pallas_call(
        backward_kernel,
        out_shape=jax.ShapeDtypeStruct((owners, mine + mine // 2, BLOCK), jnp.bfloat16),
        in_specs=[smem] * 2 + [vmem] * 4 + [pl.BlockSpec(memory_space=pl.ANY)],
        out_specs=vmem,
        scratch_shapes=[
            pltpu.VMEM((rows, width), jnp.bfloat16),
            pltpu.VMEM((rows, BLOCK), jnp.bfloat16),
            pltpu.VMEM((n_blocks, BLOCK, BLOCK), jnp.float32),
            pltpu.VMEM((BLOCK + HD, rows), jnp.bfloat16),
            pltpu.SemaphoreType.DMA,
        ],
        compiler_params=pltpu.CompilerParams(vmem_limit_bytes=56 * 2**20),
        cost_estimate=pl.CostEstimate(
            flops=12 * 10**9, bytes_accessed=20 * 2**20, transcendentals=n_blocks * 2**16
        ),
        name="backward",
    )(pairs, valid, cot, kv, kvt, q, vol)


def place_kernel(got_ref, out_ref):
    peers, half, _ = got_ref.shape
    for p in range(peers // 2):
        one, two = got_ref[2 * p], got_ref[2 * p + 1]
        at = pl.ds(p * BLOCK, BLOCK)
        out_ref[:half, at] = jnp.concatenate([one[:, :HD], two[:, :HD]], axis=1)
        out_ref[half:, at] = jnp.concatenate([one[:, HD:], two[:, HD:]], axis=1)


def place_call(got):
    peers, half, _ = got.shape
    vmem = pl.BlockSpec(memory_space=pltpu.VMEM)
    return pl.pallas_call(
        place_kernel,
        out_shape=jax.ShapeDtypeStruct((2 * half, peers * HD), got.dtype),
        in_specs=[vmem],
        out_specs=vmem,
        compiler_params=pltpu.CompilerParams(vmem_limit_bytes=8 * 2**20),
        name="place",
    )(got)


def total_kernel(got_ref, out_ref):
    mine = out_ref.shape[1]
    total = got_ref[0].astype(jnp.float32)
    for i in range(1, got_ref.shape[0]):
        total += got_ref[i].astype(jnp.float32)
    out_ref[0, :mine // 2] = total[mine:, :HD]
    out_ref[0, mine // 2:] = total[mine:, HD:]
    out_ref[1] = total[:mine, :HD]
    out_ref[2] = total[:mine, HD:]


def total_call(got, mine):
    vmem = pl.BlockSpec(memory_space=pltpu.VMEM)
    return pl.pallas_call(
        total_kernel,
        out_shape=jax.ShapeDtypeStruct((3, mine, HD), jnp.float32),
        in_specs=[vmem],
        out_specs=vmem,
        compiler_params=pltpu.CompilerParams(vmem_limit_bytes=8 * 2**20),
        name="total",
    )(got)


def local(volume, cotangent, weights, pairs, valid):
    peers = lax.axis_size("seq")
    owners = lax.axis_size("dp")
    vol, cot = volume[0], cotangent[0]
    toks, width = vol.shape
    w_rows = weights.shape[0]
    half = toks // 2

    gathered = lax.all_gather(vol, "seq", axis=0, tiled=True)

    cot = cot.reshape(2, half, peers, HD).transpose(2, 1, 0, 3).reshape(peers, half, 2 * HD)
    cot = lax.all_to_all(cot, "seq", split_axis=0, concat_axis=0, tiled=True)
    weights, cot = lax.optimization_barrier((weights, cot))

    column = lax.axis_index("seq") * HD
    part = lax.dynamic_slice_in_dim(weights, column, HD, axis=2)
    part = jnp.stack([part[:, 1], part[:, 2], part[:, 0]], axis=1).reshape(-1, BLOCK)
    sent = jnp.broadcast_to(part[None], (owners, *part.shape))
    w = lax.all_to_all(sent, "dp", split_axis=0, concat_axis=0, tiled=True)
    w = w.reshape(owners * w_rows, 3 * HD)
    w = jnp.pad(w, ((0, 0), (0, HD)))

    pairs, valid = pairs[0, 0], valid[0, 0]
    att, kv, kvt, q = forward_call(pairs, valid, w, gathered, peers)
    att = lax.all_to_all(att, "seq", split_axis=0, concat_axis=0, tiled=True)
    wg = backward_call(pairs, valid, cot, kv, kvt, q, gathered, owners)
    att = place_call(att)
    wg, att = lax.optimization_barrier((wg, att))
    wg = lax.all_to_all(wg, "dp", split_axis=0, concat_axis=0, tiled=True)
    return att[None], total_call(wg, w_rows).transpose(1, 0, 2)


def solution(mesh):
    return jax.shard_map(
        local,
        mesh=mesh,
        in_specs=(
            P("dp", "seq", None),
            P("dp", "seq", None),
            P("dp", None, None),
            P("dp", "seq", None, None),
            P("dp", "seq", None, None),
        ),
        out_specs=(P("dp", "seq", None), P("dp", None, "seq")),
        check_vma=False,
    )
```

time: 155 us -> 131 us (0.85)
  waiting for transfers between devices: 50.3 us -> 33.7 us
  starting transfers between devices: 34.1 us -> 26.6 us
  blocking collectives: 18.7 us -> 24.6 us
  local copies, waits for them, and re-layouts: 10.2 us -> 6.32 us
  Pallas kernels: 27.3 us -> 25.5 us
    all_to_all x1, waiting for transfers between devices: 12.7 us -> 2.9 us  [local(): att = lax.all_to_all(att, 'seq', split_axis=0, concat_axis=0, tiled=True)]
    all_gather x1, waiting for transfers between devices: 10.2 us -> 3.05 us  [local(): gathered = lax.all_gather(vol, 'seq', axis=0, tiled=True)]
    all_to_all x1, blocking collectives: 18.7 us -> 24.6 us  [local(): wg = lax.all_to_all(wg, 'dp', split_axis=0, concat_axis=0, tiled=True)]
    unnamed x12 -> x9, local copies, waits for them, and re-layouts: 6.69 us -> 1.22 us
    all_to_all x1, starting transfers between devices: 9.35 us -> 4.63 us  [local(): att = lax.all_to_all(att, 'seq', split_axis=0, concat_axis=0, tiled=True)]
    all_to_all x1, waiting for transfers between devices: 9.05 us -> 13 us  [local(): w = lax.all_to_all(sent, 'dp', split_axis=0, concat_axis=0, tiled=True)]
    all_to_all x1, waiting for transfers between devices: 17.7 us -> 14 us  [local(): cot = lax.all_to_all(cot, 'seq', split_axis=0, concat_axis=0, tiled=True)]
    all_to_all x1, starting transfers between devices: 14.2 us -> 11.8 us  [local(): cot = lax.all_to_all(cot, 'seq', split_axis=0, concat_axis=0, tiled=True)]
  transfers between devices with their start and end apart: 4 -> 4, of which waited for: 4 -> 4; matrix products, arithmetic and copies ran while one was open for 4% -> 5% of each run, Pallas kernels for 0% -> 9%
where the time goes in v4:
time: 131 us
  waiting for transfers between devices  33.7 us (26%)
  starting transfers between devices  26.6 us (20%)
  Pallas kernels  25.5 us (19%)
  blocking collectives  24.6 us (19%)
  between operations  14.1 us (11%)
  local copies, waits for them, and re-layouts  6.32 us (5%)
    all_to_all x1, blocking collectives, local(): wg = lax.all_to_all(wg, 'dp', split_axis=0, concat_axis=0, tiled=True)  24.6 us
    all_to_all x1, waiting for transfers between devices, local(): cot = lax.all_to_all(cot, 'seq', split_axis=0, concat_axis=0, tiled=True)  14 us
    all_to_all x1, waiting for transfers between devices, local(): w = lax.all_to_all(sent, 'dp', split_axis=0, concat_axis=0, tiled=True)  13 us
    pallas_call x1, Pallas kernels, forward_call(): pl.pallas_call(forward_kernel, out_shape=(jax.ShapeDtypeStruct((peers, ro...  12.2 us
    all_to_all x1, starting transfers between devices, local(): cot = lax.all_to_all(cot, 'seq', split_axis=0, concat_axis=0, tiled=True)  11.8 us
    pallas_call x1, Pallas kernels, backward_call(): pl.pallas_call(backward_kernel, out_shape=jax.ShapeDtypeStruct((owners, m...  11.6 us
    all_to_all x1, starting transfers between devices, local(): w = lax.all_to_all(sent, 'dp', split_axis=0, concat_axis=0, tiled=True)  10.1 us
    all_to_all x1, starting transfers between devices, local(): att = lax.all_to_all(att, 'seq', split_axis=0, concat_axis=0, tiled=True)  4.63 us
  transfers between devices with their start and end apart: 4, of which 4 were waited for; matrix products, arithmetic and copies ran while one was open for 5% of the time, Pallas kernels for 9%

profile of v4, /device:TPU:1, one launch (start us, length us, event | category | flops | bytes accessed | tf_op | source)
XLA Modules:
  0.0 130.8 jit_solution(18426728628840268543)
XLA Ops:
  7.2 0.0 copy-start
  7.2 0.0 copy-start.2
  7.2 0.0 copy-start.3
  7.2 0.0 all-gather.3.cloned.1.call-start
  7.2 0.7 all-gather.3.cloned.1.call-update
  7.9 1.2 copy.12
  9.1 0.3 reshape_squeeze.3
  9.4 0.1 copy.13
  9.6 1.0 copy.14
  10.5 11.8 %all-to-all-start = ((bf16[16,96,128]{2,1,0:T(8,128)(2,1)}), bf16[16,96,128]{2,1,0:T(8,128)(2,1)S(1)}, u32[]{:S(2)}, u32[]{:S(2)}) async-start(bf16[16,96,128]{2,1,0:T(8,128)(2,1)} %copy.14), calls=%async_computation | async-start | bytes 786432 | tf_op jit(solution)/shard_map/all_to_all | solution.py:266
  22.3 14.0 %all-to-all-done.cot_ref = bf16[16,96,128]{2,1,0:T(8,128)(2,1)S(1)} async-done(((bf16[16,96,128]{2,1,0:T(8,128)(2,1)}), bf16[16,96,128]{2,1,0:T(8,128)(2,1)S(1)}, u32[]{:S(2)}, u32[]{:S(2)}) %all-to-all-start) | async-done | bytes 393248 | tf_op jit(solution)/shard_map/all_to_all | solution.py:266
  36.4 0.0 copy-done
  36.4 0.1 constant_dynamic-slice_fusion.1
  36.4 0.1 constant_dynamic-slice_fusion
  36.6 0.1 broadcast_in_dim.10
  36.7 0.8 broadcast_in_dim.11
  37.5 10.1 %all-to-all-start.1 = ((bf16[32,48,128]{2,1,0:T(8,128)(2,1)}), bf16[32,48,128]{2,1,0:T(8,128)(2,1)S(1)}, u32[]{:S(2)}, u32[]{:S(2)}) async-start(bf16[32,48,128]{2,1,0:T(8,128)(2,1)} %broadcast_in_dim.11), calls=%async_computation.1 | async-start | bytes 786432 | tf_op jit(solution)/shard_map/all_to_all | solution.py:273
  47.5 0.0 copy-done.2
  47.5 0.7 copy.18.pairs_ref
  48.2 0.7 copy.19.valid_ref
  48.9 13.0 %all-to-all-done.1 = bf16[32,48,128]{2,1,0:T(8,128)(2,1)S(1)} async-done(((bf16[32,48,128]{2,1,0:T(8,128)(2,1)}), bf16[32,48,128]{2,1,0:T(8,128)(2,1)S(1)}, u32[]{:S(2)}, u32[]{:S(2)}) %all-to-all-start.1) | async-done | bytes 393248 | tf_op jit(solution)/shard_map/all_to_all | solution.py:273
  61.9 0.3 reshape.12
  62.3 1.0 pad.4.w_ref
  63.3 3.0 %all-gather.3.cloned.1.call-done = bf16[1,3072,1024]{2,1,0:T(8,128)(2,1)} async-done(((bf16[1,192,1024]{2,1,0:T(8,128)(2,1)}), bf16[1,3072,1024]{2,1,0:T(8,128)(2,1)}) %all-gather.3.cloned.1.call-update) | async-done | bytes 6291472 | tf_op jit(solution)/shard_map/all_gather | solution.py:263
  66.3 12.2 %forward.1 = (bf16[16,96,128]{2,1,0:T(8,128)(2,1)}, bf16[3072,128]{1,0:T(8,128)(2,1)}, bf16[24,128,128]{2,1,0:T(8,128)(2,1)}, bf16[3072,128]{1,0:T(8,128)(2,1)}) custom-call(s32[24,4]{1,0:T(8,128)} %copy.18.pairs_ref, s32[24,4]{1,0:T(8,128)} %copy.19.valid_ref, bf16[1024,256]{1,0:T(8,128)(2,1)} %pad.4.w_ref, bf16[3072,1024]{1,0:T(8,128)(2,1)} %bitcast.9), custom_call_target="tpu_custom_call" | custom-call | tf_op jit(solution)/shard_map/forward/pallas_call | solution.py:100
  78.5 4.6 %all-to-all-start.2 = ((bf16[16,96,128]{2,1,0:T(8,128)(2,1)}), bf16[16,96,128]{2,1,0:T(8,128)(2,1)S(1)}, u32[]{:S(2)}, u32[]{:S(2)}) async-start(bf16[16,96,128]{2,1,0:T(8,128)(2,1)} %get-tuple-element.15), calls=%async_computation.2 | async-start | bytes 786432 | tf_op jit(solution)/shard_map/all_to_all | solution.py:279
  83.1 0.0 copy-done.1
  83.1 11.6 %backward.1 = bf16[32,48,128]{2,1,0:T(8,128)(2,1)} custom-call(s32[24,4]{1,0:T(8,128)} %copy.18.pairs_ref, s32[24,4]{1,0:T(8,128)} %copy.19.valid_ref, bf16[16,96,128]{2,1,0:T(8,128)(2,1)} %copy-done.1, bf16[3072,128]{1,0:T(8,128)(2,1)} %get-tuple-element.12.kv_ref, bf16[24,128,128]{2,1,0:T(8,128)(2,1)} %get-tuple-element.13.kvt_ref, ...), custom_call_target="tpu_custom_call" | custom-call | flops 12000000000 | bytes 20971520 | tf_op jit(solution)/shard_map/backward/pallas_call | solution.py:190
  94.8 2.9 %all-to-all-done.2.got_ref = bf16[16,96,128]{2,1,0:T(8,128)(2,1)S(1)} async-done(((bf16[16,96,128]{2,1,0:T(8,128)(2,1)}), bf16[16,96,128]{2,1,0:T(8,128)(2,1)S(1)}, u32[]{:S(2)}, u32[]{:S(2)}) %all-to-all-start.2) | async-done | bytes 393248 | tf_op jit(solution)/shard_map/all_to_all | solution.py:279
  97.7 0.9 place.1
  98.6 24.6 %all_to_all.20.got_ref = bf16[32,48,128]{2,1,0:T(8,128)(2,1)S(1)} all-to-all(bf16[32,48,128]{2,1,0:T(8,128)(2,1)} %backward.1), channel_id=1, replica_groups=mesh['dp'=32,'seq'=16] {'dp'}, dimensions={0} | all-to-all | bytes 786432 | tf_op jit(solution)/shard_map/all_to_all | solution.py:283
  123.2 0.8 total.1
  (4 shorter events, 0.0 us)
Async XLA Ops:
  7.2 29.2 %copy-start = (bf16[32,3,1024]{2,0,1:T(8,128)(2,1)S(1)}, bf16[32,3,1024]{2,0,1:T(8,128)(2,1)}, u32[]{:S(2)}) copy-start(bf16[32,3,1024]{2,0,1:T(8,128)(2,1)} %param.7) | copy-start | bytes 589828
  7.2 40.4 %copy-start.2 = (s32[1,1,24,4]{2,3,1,0:T(4,128)S(1)}, s32[1,1,24,4]{2,3,1,0:T(4,128)}, u32[]{:S(2)}) copy-start(s32[1,1,24,4]{2,3,1,0:T(4,128)} %param.8) | copy-start | bytes 1156
  7.2 41.0 %copy-start.3 = (s32[1,1,24,4]{2,3,1,0:T(4,128)S(1)}, s32[1,1,24,4]{2,3,1,0:T(4,128)}, u32[]{:S(2)}) copy-start(s32[1,1,24,4]{2,3,1,0:T(4,128)} %param.9) | copy-start | bytes 1156
  7.2 59.1 %all-gather.3.cloned.1.call-start = ((), (), s32[]{:S(2)}) async-start(), calls=%async_computation.4 | async-start | bytes 6684672 | tf_op jit(solution)/shard_map/all_gather | solution.py:263
  10.5 25.9 %all-to-all-start = ((bf16[16,96,128]{2,1,0:T(8,128)(2,1)}), bf16[16,96,128]{2,1,0:T(8,128)(2,1)S(1)}, u32[]{:S(2)}, u32[]{:S(2)}) async-start(bf16[16,96,128]{2,1,0:T(8,128)(2,1)} %copy.14), calls=%async_computation | async-start | bytes 786432 | tf_op jit(solution)/shard_map/all_to_all | solution.py:266
  36.4 46.7 %copy-start.1 = (bf16[16,96,128]{2,1,0:T(8,128)(2,1)}, bf16[16,96,128]{2,1,0:T(8,128)(2,1)S(1)}, u32[]{:S(2)}) copy-start(bf16[16,96,128]{2,1,0:T(8,128)(2,1)S(1)} %all-to-all-done.cot_ref) | copy-start | bytes 1179652
  37.5 24.5 %all-to-all-start.1 = ((bf16[32,48,128]{2,1,0:T(8,128)(2,1)}), bf16[32,48,128]{2,1,0:T(8,128)(2,1)S(1)}, u32[]{:S(2)}, u32[]{:S(2)}) async-start(bf16[32,48,128]{2,1,0:T(8,128)(2,1)} %broadcast_in_dim.11), calls=%async_computation.1 | async-start | bytes 786432 | tf_op jit(solution)/shard_map/all_to_all | solution.py:273
  78.5 19.2 %all-to-all-start.2 = ((bf16[16,96,128]{2,1,0:T(8,128)(2,1)}), bf16[16,96,128]{2,1,0:T(8,128)(2,1)S(1)}, u32[]{:S(2)}, u32[]{:S(2)}) async-start(bf16[16,96,128]{2,1,0:T(8,128)(2,1)} %get-tuple-element.15), calls=%async_computation.2 | async-start | bytes 786432 | tf_op jit(solution)/shard_map/all_to_all | solution.py:279
Sparse Core Ops, SparseCore 0:
  10.2 56.1 all-gather.2

commit v5 on v4

--- a/solution.py
+++ b/solution.py
@@ -12,7 +12,6 @@
 LOG2E = 1.4426950408889634
 UNROLL = 6
 AHEAD = 6
-CHUNKS = 8
 
 NN = (((1,), (0,)), ((), ()))
 NT = (((1,), (1,)), ((), ()))
@@ -39,30 +38,45 @@
     return exponent * (1.0 / jnp.sum(exponent, axis=0, keepdims=True))
 
 
-def forward_kernel(
-    pairs_ref, valid_ref, w_ref, vol_hbm, att_ref, kv_ref, kvt_ref, q_ref, vol_ref, o_ref, sems,
-):
-    rows = vol_ref.shape[0]
-    n_blocks, slots = pairs_ref.shape
-    peers, half, _ = att_ref.shape
-    chunk = rows // CHUNKS
+def block_places(me, peers):
+    core = lax.rem(me, 2)
+    chip = lax.div(me, 2)
+    chips = peers // 2
+    ahead = 1 - 2 * core
+    places = [me, me + ahead]
+    for k in range(1, chips // 2 + 1):
+        back = lax.rem(chip - k * ahead + chips, chips)
+        forth = lax.rem(chip + k * ahead + chips, chips)
+        places += [2 * back + core, 2 * forth + 1 - core]
+        if k < chips // 2:
+            places += [2 * back + 1 - core, 2 * forth + core]
+    return places
+
+
+def forward_kernel(*refs):
+    me_ref, pairs_ref, valid_ref, got_ref = refs[:4]
+    att_ref, kv_ref, kvt_ref, q_ref, held_ref, w_ref, o_ref, sems = refs[-8:]
+    blocks = refs[4:-8]
+    toks = blocks[0].shape[0]
     copies = [
-        pltpu.make_async_copy(
-            vol_hbm.at[pl.ds(c * chunk, chunk)], vol_ref.at[pl.ds(c * chunk, chunk)], sems.at[c]
-        )
-        for c in range(CHUNKS)
+        pltpu.make_async_copy(block_ref, held_ref.at[c], sems.at[c])
+        for c, block_ref in enumerate(blocks)
     ]
     for copy in copies:
         copy.start()
-    for c in range(CHUNKS):
+    n_blocks, slots = pairs_ref.shape
+    peers, half, _ = att_ref.shape
+    depth = got_ref.shape[1] // 2
+    for s in range(got_ref.shape[0]):
+        w_ref[pl.ds(s * depth, depth), :] = jnp.concatenate([got_ref[s, :depth], got_ref[s, depth:]], axis=1)
+    for c, place in enumerate(block_places(me_ref[0], peers)):
+        at = pl.ds(pl.multiple_of(place * toks, HD), toks)
         copies[c].wait()
-        at = pl.ds(c * chunk, chunk)
-        got = mm(vol_ref[at, :], w_ref[...])
+        got = mm(held_ref[c], w_ref[...])
         q_ref[at, :] = got[:, BLOCK:].astype(jnp.bfloat16)
-        kv = got[:, :BLOCK].astype(jnp.bfloat16)
-        kv_ref[at, :] = kv
-        for b in range(chunk // BLOCK):
-            kvt_ref[c * (chunk // BLOCK) + b] = kv[b * BLOCK:(b + 1) * BLOCK].T
+        kv_ref[at, :] = got[:, :BLOCK].astype(jnp.bfloat16)
+    for b in range(n_blocks):
+        kvt_ref[b] = kv_ref[b * BLOCK:(b + 1) * BLOCK, :].T
 
     def body(i, carry):
         blocks = [i * AHEAD + u for u in range(AHEAD)]
@@ -92,41 +106,52 @@
         )
 
 
-def forward_call(pairs, valid, w, vol, peers):
-    rows, width = vol.shape
+def forward_call(me, pairs, valid, w, blocks):
+    peers = len(blocks)
+    toks, width = blocks[0].shape
+    rows = toks * peers
     n_blocks = rows // BLOCK
     vmem = pl.BlockSpec(memory_space=pltpu.VMEM)
     smem = pl.BlockSpec(memory_space=pltpu.SMEM)
     return pl.pallas_call(
         forward_kernel,
         out_shape=(
-            jax.ShapeDtypeStruct((peers, rows // peers // 2, BLOCK), jnp.bfloat16),
+            jax.ShapeDtypeStruct((peers, toks // 2, BLOCK), jnp.bfloat16),
             jax.ShapeDtypeStruct((rows, BLOCK), jnp.bfloat16),
             jax.ShapeDtypeStruct((n_blocks, BLOCK, BLOCK), jnp.bfloat16),
             jax.ShapeDtypeStruct((rows, BLOCK), jnp.bfloat16),
         ),
-        in_specs=[smem] * 2 + [vmem, pl.BlockSpec(memory_space=pl.ANY)],
+        in_specs=[smem] * 3 + [vmem] + [pl.BlockSpec(memory_space=pl.ANY)] * peers,
         out_specs=(vmem,) * 4,
         scratch_shapes=[
-            pltpu.VMEM((rows, width), jnp.bfloat16),
+            pltpu.VMEM((peers, toks, width), jnp.bfloat16),
+            pltpu.VMEM((width, 2 * BLOCK), jnp.bfloat16),
             pltpu.VMEM((rows, HD), jnp.bfloat16),
-            pltpu.SemaphoreType.DMA((CHUNKS,)),
+            pltpu.SemaphoreType.DMA((peers,)),
         ],
         compiler_params=pltpu.CompilerParams(vmem_limit_bytes=56 * 2**20),
         name="forward",
-    )(pairs, valid, w, vol)
-
-
-def backward_kernel(
-    pairs_ref, valid_ref, cot_ref, kv_ref, kvt_ref, q_ref, vol_hbm, wg_ref,
-    vol_ref, do_ref, acc_ref, dt_ref, sem,
-):
-    rows, width = vol_ref.shape
+    )(me, pairs, valid, w, *blocks)
+
+
+def backward_kernel(*refs):
+    me_ref, pairs_ref, valid_ref, cot_ref, kv_ref, kvt_ref, q_ref = refs[:7]
+    wg_ref, vol_ref, do_ref, acc_ref, dt_ref, sems = refs[-6:]
+    blocks = refs[7:-6]
+    width = vol_ref.shape[1]
     n_blocks, slots = pairs_ref.shape
     peers, half, _ = cot_ref.shape
     scale = HD ** -0.5
-    copy = pltpu.make_async_copy(vol_hbm, vol_ref, sem)
-    copy.start()
+    copies = [
+        pltpu.make_async_copy(
+            block_ref,
+            vol_ref.at[pl.ds(pl.multiple_of(place * (2 * half), HD), 2 * half)],
+            sems.at[c],
+        )
+        for c, (place, block_ref) in enumerate(zip(block_places(me_ref[0], peers), blocks))
+    ]
+    for copy in copies:
+        copy.start()
 
     acc_ref[...] = jnp.zeros_like(acc_ref)
     blank = jnp.zeros((half, HD), jnp.bfloat16)
@@ -166,7 +191,8 @@
     for b in range(n_blocks):
         dt_ref[:BLOCK, b * BLOCK:(b + 1) * BLOCK] = (acc_ref[b] * factor).T.astype(jnp.bfloat16)
 
-    copy.wait()
+    for copy in copies:
+        copy.wait()
     owners = wg_ref.shape[0]
     mine = width // owners
     part = 256
@@ -181,8 +207,9 @@
             wg_ref[owner, mine:] = jnp.concatenate([q_rows[:mine // 2], q_rows[mine // 2:]], axis=1)
 
 
-def backward_call(pairs, valid, cot, kv, kvt, q, vol, owners):
-    rows, width = vol.shape
+def backward_call(me, pairs, valid, cot, kv, kvt, q, blocks, owners):
+    toks, width = blocks[0].shape
+    rows = toks * len(blocks)
     n_blocks = rows // BLOCK
     mine = width // owners
     vmem = pl.BlockSpec(memory_space=pltpu.VMEM)
@@ -190,21 +217,21 @@
     return pl.pallas_call(
         backward_kernel,
         out_shape=jax.ShapeDtypeStruct((owners, mine + mine // 2, BLOCK), jnp.bfloat16),
-        in_specs=[smem] * 2 + [vmem] * 4 + [pl.BlockSpec(memory_space=pl.ANY)],
+        in_specs=[smem] * 3 + [vmem] * 4 + [pl.BlockSpec(memory_space=pl.ANY)] * len(blocks),
         out_specs=vmem,
         scratch_shapes=[
             pltpu.VMEM((rows, width), jnp.bfloat16),
             pltpu.VMEM((rows, BLOCK), jnp.bfloat16),
             pltpu.VMEM((n_blocks, BLOCK, BLOCK), jnp.float32),
             pltpu.VMEM((BLOCK + HD, rows), jnp.bfloat16),
-            pltpu.SemaphoreType.DMA,
+            pltpu.SemaphoreType.DMA((len(blocks),)),
         ],
         compiler_params=pltpu.CompilerParams(vmem_limit_bytes=56 * 2**20),
         cost_estimate=pl.CostEstimate(
             flops=12 * 10**9, bytes_accessed=20 * 2**20, transcendentals=n_blocks * 2**16
         ),
         name="backward",
-    )(pairs, valid, cot, kv, kvt, q, vol)
+    )(me, pairs, valid, cot, kv, kvt, q, *blocks)
 
 
 def place_kernel(got_ref, out_ref):
@@ -252,32 +279,104 @@
     )(got)
 
 
+def pack_weights_kernel(me_ref, weights_ref, out_ref):
+    core = lax.rem(me_ref[0], 2)
+    at = pl.ds(pl.multiple_of(lax.div(me_ref[0], 2) * BLOCK, BLOCK), BLOCK)
+    depth = weights_ref.shape[1]
+    q, k, v = (weights_ref[t, :, at] for t in range(3))
+    blank = jnp.zeros((depth, HD), q.dtype)
+
+    def side(half):
+        kv = jnp.concatenate([half(k), half(v)], axis=1)
+        return jnp.concatenate([kv, jnp.concatenate([half(q), blank], axis=1)], axis=0)
+
+    one = jnp.where(core == 0, side(lambda x: x[:, :HD]), side(lambda x: x[:, HD:]))
+    for i in range(out_ref.shape[0]):
+        out_ref[i] = one
+
+
+def pack_weights(me, weights, owners):
+    depth = weights.shape[0]
+    vmem = pl.BlockSpec(memory_space=pltpu.VMEM)
+    return pl.pallas_call(
+        pack_weights_kernel,
+        out_shape=jax.ShapeDtypeStruct((owners, 2 * depth, BLOCK), weights.dtype),
+        in_specs=[pl.BlockSpec(memory_space=pltpu.SMEM), vmem],
+        out_specs=vmem,
+        compiler_params=pltpu.CompilerParams(vmem_limit_bytes=8 * 2**20),
+        name="pack_weights",
+    )(me, weights.transpose(1, 0, 2))
+
+
+def pack_cotangent_kernel(cot_ref, out_ref):
+    peers, half, _ = out_ref.shape
+    for p in range(peers // 2):
+        at = pl.ds(p * BLOCK, BLOCK)
+        first, second = cot_ref[:half, at], cot_ref[half:, at]
+        out_ref[2 * p] = jnp.concatenate([first[:, :HD], second[:, :HD]], axis=1)
+        out_ref[2 * p + 1] = jnp.concatenate([first[:, HD:], second[:, HD:]], axis=1)
+
+
+def pack_cotangent(cot, peers):
+    toks = cot.shape[0]
+    vmem = pl.BlockSpec(memory_space=pltpu.VMEM)
+    return pl.pallas_call(
+        pack_cotangent_kernel,
+        out_shape=jax.ShapeDtypeStruct((peers, toks // 2, BLOCK), cot.dtype),
+        in_specs=[vmem],
+        out_specs=vmem,
+        compiler_params=pltpu.CompilerParams(vmem_limit_bytes=8 * 2**20),
+        name="pack_cotangent",
+    )(cot)
+
+
+def gather(vol):
+    peers = lax.axis_size("seq")
+    chips = peers // 2
+    onward = [
+        (2 * z + c, 2 * ((z + 1) % chips) if c == 0 else 2 * ((z - 1) % chips) + 1)
+        for z in range(chips)
+        for c in range(2)
+    ]
+    twin = [(i, i ^ 1) for i in range(peers)]
+
+    def swap(x):
+        return lax.ppermute(x, "seq", twin)
+
+    own, other = vol, swap(vol)
+    blocks = [own, other]
+    last = chips // 2
+    for k in range(1, last + 1):
+        if k >= 3:
+            n = 4 * (k - 2) + 1
+            own, other, blocks[n], blocks[n - 2] = lax.optimization_barrier(
+                (own, other, blocks[n], blocks[n - 2])
+            )
+        own = lax.ppermute(own, "seq", onward)
+        if k < last:
+            other = lax.ppermute(other, "seq", onward)
+        blocks += [own, swap(own)]
+        if k < last:
+            blocks += [other, swap(other)]
+    return blocks
+
+
 def local(volume, cotangent, weights, pairs, valid):
     peers = lax.axis_size("seq")
     owners = lax.axis_size("dp")
     vol, cot = volume[0], cotangent[0]
-    toks, width = vol.shape
+    me = lax.axis_index("seq").reshape(1)
     w_rows = weights.shape[0]
-    half = toks // 2
-
-    gathered = lax.all_gather(vol, "seq", axis=0, tiled=True)
-
-    cot = cot.reshape(2, half, peers, HD).transpose(2, 1, 0, 3).reshape(peers, half, 2 * HD)
-    cot = lax.all_to_all(cot, "seq", split_axis=0, concat_axis=0, tiled=True)
-    weights, cot = lax.optimization_barrier((weights, cot))
-
-    column = lax.axis_index("seq") * HD
-    part = lax.dynamic_slice_in_dim(weights, column, HD, axis=2)
-    part = jnp.stack([part[:, 1], part[:, 2], part[:, 0]], axis=1).reshape(-1, BLOCK)
-    sent = jnp.broadcast_to(part[None], (owners, *part.shape))
-    w = lax.all_to_all(sent, "dp", split_axis=0, concat_axis=0, tiled=True)
-    w = w.reshape(owners * w_rows, 3 * HD)
-    w = jnp.pad(w, ((0, 0), (0, HD)))
+
+    w = lax.all_to_all(pack_weights(me, weights, owners), "dp", split_axis=0, concat_axis=0, tiled=True)
+    cot, w = lax.optimization_barrier((cot, w))
+    cot = lax.all_to_all(pack_cotangent(cot, peers), "seq", split_axis=0, concat_axis=0, tiled=True)
+    blocks = gather(vol)
 
     pairs, valid = pairs[0, 0], valid[0, 0]
-    att, kv, kvt, q = forward_call(pairs, valid, w, gathered, peers)
+    att, kv, kvt, q = forward_call(me, pairs, valid, w, blocks)
     att = lax.all_to_all(att, "seq", split_axis=0, concat_axis=0, tiled=True)
-    wg = backward_call(pairs, valid, cot, kv, kvt, q, gathered, owners)
+    wg = backward_call(me, pairs, valid, cot, kv, kvt, q, blocks, owners)
     att = place_call(att)
     wg, att = lax.optimization_barrier((wg, att))
     wg = lax.all_to_all(wg, "dp", split_axis=0, concat_axis=0, tiled=True)

time: 131 us -> 141 us (1.076)
  starting transfers between devices: 26.6 us -> 73.7 us
  waiting for transfers between devices: 33.7 us -> 7.53 us
  between operations: 14.1 us -> 1.02 us
  Pallas kernels: 25.5 us -> 28.5 us
    ppermute x0 -> x15, starting transfers between devices: none -> 48.6 us  [the longest x8 27.2 us: swap(): return lax.ppermute(x, 'seq', twin)]
    all_to_all x2, waiting for transfers between devices: 27 us -> 0.01 us  [the longest x1 0.01 us: local(): lax.all_to_all(pack_weights(me, weights, owners), 'dp', split_axis=0, con...]
    ppermute x0 -> x15, waiting for transfers between devices: none -> 4.75 us  [the longest x3 4.2 us: gather(): other = lax.ppermute(other, 'seq', onward)]
    all_to_all x2, starting transfers between devices: 21.9 us -> 17.9 us  [the longest x1 9.8 us: local(): lax.all_to_all(pack_weights(me, weights, owners), 'dp', split_axis=0, con...]
    all_gather x1 -> x0, waiting for transfers between devices: 3.05 us -> none  [local(): gathered = lax.all_gather(vol, 'seq', axis=0, tiled=True)]
    pallas_call x1 -> x3, Pallas kernels: 12.2 us -> 15 us  [the longest x1 13.2 us: forward_call(): pl.pallas_call(forward_kernel, out_shape=(jax.ShapeDtypeStruct((peers, to...]
    all_to_all x1, starting transfers between devices: 4.63 us -> 7.28 us  [local(): att = lax.all_to_all(att, 'seq', split_axis=0, concat_axis=0, tiled=True)]
    unnamed x9 -> x40, local copies, waits for them, and re-layouts: 1.22 us -> 3.63 us
  transfers between devices with their start and end apart: 4 -> 18, of which waited for: 4 -> 4; matrix products, arithmetic and copies ran while one was open for 5% -> 1% of each run, Pallas kernels for 9% -> 19%
where the time goes in v5:
time: 141 us; the launch traced here: 140 us
  starting transfers between devices  73.7 us (52%)
  Pallas kernels  28.5 us (20%)
  blocking collectives  24.2 us (17%)
  waiting for transfers between devices  7.53 us (5%)
  local copies, waits for them, and re-layouts  5 us (4%)
    ppermute x8, starting transfers between devices, swap(): return lax.ppermute(x, 'seq', twin)  27.2 us
    all_to_all x1, blocking collectives, local(): wg = lax.all_to_all(wg, 'dp', split_axis=0, concat_axis=0, tiled=True)  24.2 us
    ppermute x4, starting transfers between devices, gather(): own = lax.ppermute(own, 'seq', onward)  15.1 us
    pallas_call x1, Pallas kernels, forward_call(): pl.pallas_call(forward_kernel, out_shape=(jax.ShapeDtypeStruct((peers, to...  13.2 us
    pallas_call x1, Pallas kernels, backward_call(): pl.pallas_call(backward_kernel, out_shape=jax.ShapeDtypeStruct((owners, m...  11.8 us
    all_to_all x1, starting transfers between devices, local(): lax.all_to_all(pack_weights(me, weights, owners), 'dp', split_axis=0, con...  9.8 us
    all_to_all x1, starting transfers between devices, local(): lax.all_to_all(pack_cotangent(cot, peers), 'seq', split_axis=0, concat_ax...  8.07 us
    all_to_all x1, starting transfers between devices, local(): att = lax.all_to_all(att, 'seq', split_axis=0, concat_axis=0, tiled=True)  7.28 us
  transfers between devices with their start and end apart: 18, of which 4 were waited for; matrix products, arithmetic and copies ran while one was open for 1% of the time, Pallas kernels for 19%

profile of v5, /device:TPU:1, one launch (start us, length us, event | category | flops | bytes accessed | tf_op | source)
XLA Modules:
  0.0 140.0 jit_solution(10410910351306227869)
XLA Ops:
  0.6 8.8 %collective-permute-start = (bf16[192,1024]{1,0:T(8,128)(2,1)}, bf16[192,1024]{1,0:T(8,128)(2,1)S(1)}, u32[]{:S(2)}, u32[]{:S(2)}) collective-permute-start(bf16[192,1024]{1,0:T(8,128)(2,1)} %bitcast.11), channel_id=1, source_target_pairs={{0,1},{1,0},{2,3},{3,2},{4,5},{5,4},{6,7},{7,6},{8,9},{9,8},{10,11... | collective-permute-start | bytes 1179656 | tf_op jit(solution)/shard_map/ppermute | solution.py:344
  9.4 5.3 %collective-permute-start.1 = (bf16[192,1024]{1,0:T(8,128)(2,1)}, bf16[192,1024]{1,0:T(8,128)(2,1)S(1)}, u32[]{:S(2)}, u32[]{:S(2)}) collective-permute-start(bf16[192,1024]{1,0:T(8,128)(2,1)} %bitcast.12), channel_id=1, source_target_pairs={{0,2},{1,15},{2,4},{3,1},{4,6},{5,3},{6,8},{7,5},{8,10},{9,7},{10,... | collective-permute-start | bytes 1179656 | tf_op jit(solution)/shard_map/ppermute | solution.py:355
  14.8 2.2 %collective-permute-start.3 = (bf16[192,1024]{1,0:T(8,128)(2,1)S(1)}, bf16[192,1024]{1,0:T(8,128)(2,1)S(1)}, u32[]{:S(2)}, u32[]{:S(2)}) collective-permute-start(bf16[192,1024]{1,0:T(8,128)(2,1)S(1)} %collective-permute-done.refs_5_.refs_8_), channel_id=1, source_target_pairs={{0,2},{1,15},{2,4},{3,1},{4,6},{5,3},{6,8},{7,5},{8,10},{9,7},{10,... | collective-permute-start | bytes 1179656 | tf_op jit(solution)/shard_map/ppermute | solution.py:357
  17.0 0.9 copy-done.1
  17.9 0.9 pack_weights.1
  18.8 9.8 %all-to-all-start = ((bf16[32,64,128]{2,1,0:T(8,128)(2,1)}), bf16[32,64,128]{2,1,0:T(8,128)(2,1)S(1)}, u32[]{:S(2)}, u32[]{:S(2)}) async-start(bf16[32,64,128]{2,1,0:T(8,128)(2,1)} %pack_weights.1), calls=%async_computation | async-start | bytes 1048576 | tf_op jit(solution)/shard_map/all_to_all | solution.py:371
  28.6 2.2 %collective-permute-start.2 = (bf16[192,1024]{1,0:T(8,128)(2,1)S(1)}, bf16[192,1024]{1,0:T(8,128)(2,1)S(1)}, u32[]{:S(2)}, u32[]{:S(2)}) collective-permute-start(bf16[192,1024]{1,0:T(8,128)(2,1)S(1)} %collective-permute-done.1.refs_6_.refs_9_), channel_id=1, source_target_pairs={{0,2},{1,15},{2,4},{3,1},{4,6},{5,3},{6,8},{7,5},{8,10},{9,7},{10,... | collective-permute-start | bytes 1179656 | tf_op jit(solution)/shard_map/ppermute | solution.py:355
  30.8 1.9 %collective-permute-start.6 = (bf16[192,1024]{1,0:T(8,128)(2,1)S(1)}, bf16[192,1024]{1,0:T(8,128)(2,1)S(1)}, u32[]{:S(2)}, u32[]{:S(2)}) collective-permute-start(bf16[192,1024]{1,0:T(8,128)(2,1)S(1)} %collective-permute-done.1.refs_6_.refs_9_), channel_id=1, source_target_pairs={{0,1},{1,0},{2,3},{3,2},{4,5},{5,4},{6,7},{7,6},{8,9},{9,8},{10,11... | collective-permute-start | bytes 1179656 | tf_op jit(solution)/shard_map/ppermute | solution.py:344
  32.8 2.2 %collective-permute-start.4 = (bf16[192,1024]{1,0:T(8,128)(2,1)S(1)}, bf16[192,1024]{1,0:T(8,128)(2,1)S(1)}, u32[]{:S(2)}, u32[]{:S(2)}) collective-permute-start(bf16[192,1024]{1,0:T(8,128)(2,1)S(1)} %collective-permute-done.3.refs_8_.refs_11_), channel_id=1, source_target_pairs={{0,2},{1,15},{2,4},{3,1},{4,6},{5,3},{6,8},{7,5},{8,10},{9,7},{10,... | collective-permute-start | bytes 1179656 | tf_op jit(solution)/shard_map/ppermute | solution.py:357
  35.0 3.6 %collective-permute-start.5 = (bf16[192,1024]{1,0:T(8,128)(2,1)S(1)}, bf16[192,1024]{1,0:T(8,128)(2,1)S(1)}, u32[]{:S(2)}, u32[]{:S(2)}) collective-permute-start(bf16[192,1024]{1,0:T(8,128)(2,1)S(1)} %collective-permute-done.3.refs_8_.refs_11_), channel_id=1, source_target_pairs={{0,1},{1,0},{2,3},{3,2},{4,5},{5,4},{6,7},{7,6},{8,9},{9,8},{10,11... | collective-permute-start | bytes 1179656 | tf_op jit(solution)/shard_map/ppermute | solution.py:344
  38.6 1.9 %collective-permute-start.10 = (bf16[192,1024]{1,0:T(8,128)(2,1)S(1)}, bf16[192,1024]{1,0:T(8,128)(2,1)S(1)}, u32[]{:S(2)}, u32[]{:S(2)}) collective-permute-start(bf16[192,1024]{1,0:T(8,128)(2,1)S(1)} %collective-permute-done.2.refs_10_.refs_13_), channel_id=1, source_target_pairs={{0,1},{1,0},{2,3},{3,2},{4,5},{5,4},{6,7},{7,6},{8,9},{9,8},{10,11... | collective-permute-start | bytes 1179656 | tf_op jit(solution)/shard_map/ppermute | solution.py:344
  40.5 1.1 collective-permute-done.4.refs_12_.refs_15_
  41.7 3.4 %collective-permute-start.7 = (bf16[192,1024]{1,0:T(8,128)(2,1)S(1)}, bf16[192,1024]{1,0:T(8,128)(2,1)}, u32[]{:S(2)}, u32[]{:S(2)}) collective-permute-start(bf16[192,1024]{1,0:T(8,128)(2,1)S(1)} %collective-permute-done.2.refs_10_.refs_13_), channel_id=1, source_target_pairs={{0,2},{1,15},{2,4},{3,1},{4,6},{5,3},{6,8},{7,5},{8,10},{9,7},{10,... | collective-permute-start | bytes 1179656 | tf_op jit(solution)/shard_map/ppermute | solution.py:355
  45.1 1.9 %collective-permute-start.8 = (bf16[192,1024]{1,0:T(8,128)(2,1)S(1)}, bf16[192,1024]{1,0:T(8,128)(2,1)S(1)}, u32[]{:S(2)}, u32[]{:S(2)}) collective-permute-start(bf16[192,1024]{1,0:T(8,128)(2,1)S(1)} %collective-permute-done.4.refs_12_.refs_15_), channel_id=1, source_target_pairs={{0,2},{1,15},{2,4},{3,1},{4,6},{5,3},{6,8},{7,5},{8,10},{9,7},{10,... | collective-permute-start | bytes 1179656 | tf_op jit(solution)/shard_map/ppermute | solution.py:357
  47.0 4.6 %collective-permute-start.9 = (bf16[192,1024]{1,0:T(8,128)(2,1)S(1)}, bf16[192,1024]{1,0:T(8,128)(2,1)S(1)}, u32[]{:S(2)}, u32[]{:S(2)}) collective-permute-start(bf16[192,1024]{1,0:T(8,128)(2,1)S(1)} %collective-permute-done.4.refs_12_.refs_15_), channel_id=1, source_target_pairs={{0,1},{1,0},{2,3},{3,2},{4,5},{5,4},{6,7},{7,6},{8,9},{9,8},{10,11... | collective-permute-start | bytes 1179656 | tf_op jit(solution)/shard_map/ppermute | solution.py:344
  51.7 3.1 %collective-permute-done.8.refs_16_.refs_19_ = bf16[192,1024]{1,0:T(8,128)(2,1)S(1)} collective-permute-done((bf16[192,1024]{1,0:T(8,128)(2,1)S(1)}, bf16[192,1024]{1,0:T(8,128)(2,1)S(1)}, u32[]{:S(2)}, u32[]{:S(2)}) %collective-permute-start.8) | collective-permute-done | bytes 393248 | tf_op jit(solution)/shard_map/ppermute | solution.py:357
  54.8 0.7 copy-done.13
  55.5 0.8 copy-done.15
  56.3 4.2 %collective-permute-start.13 = (bf16[192,1024]{1,0:T(8,128)(2,1)}, bf16[192,1024]{1,0:T(8,128)(2,1)}, u32[]{:S(2)}, u32[]{:S(2)}) collective-permute-start(bf16[192,1024]{1,0:T(8,128)(2,1)} %collective-permute-done.7.refs_14_.refs_17_), channel_id=1, source_target_pairs={{0,2},{1,15},{2,4},{3,1},{4,6},{5,3},{6,8},{7,5},{8,10},{9,7},{10,... | collective-permute-start | bytes 1179656 | tf_op jit(solution)/shard_map/ppermute | solution.py:355
  60.5 1.0 pack_cotangent.1
  61.5 8.1 %all-to-all-start.1 = ((bf16[16,96,128]{2,1,0:T(8,128)(2,1)}), bf16[16,96,128]{2,1,0:T(8,128)(2,1)S(1)}, u32[]{:S(2)}, u32[]{:S(2)}) async-start(bf16[16,96,128]{2,1,0:T(8,128)(2,1)} %pack_cotangent.1), calls=%async_computation.1 | async-start | bytes 786432 | tf_op jit(solution)/shard_map/all_to_all | solution.py:373
  69.6 2.0 %collective-permute-start.11 = (bf16[192,1024]{1,0:T(8,128)(2,1)}, bf16[192,1024]{1,0:T(8,128)(2,1)S(1)}, u32[]{:S(2)}, u32[]{:S(2)}) collective-permute-start(bf16[192,1024]{1,0:T(8,128)(2,1)} %collective-permute-done.7.refs_14_.refs_17_), channel_id=1, source_target_pairs={{0,1},{1,0},{2,3},{3,2},{4,5},{5,4},{6,7},{7,6},{8,9},{9,8},{10,11... | collective-permute-start | bytes 1179656 | tf_op jit(solution)/shard_map/ppermute | solution.py:344
  71.6 2.3 %collective-permute-start.12 = (bf16[192,1024]{1,0:T(8,128)(2,1)S(1)}, bf16[192,1024]{1,0:T(8,128)(2,1)S(1)}, u32[]{:S(2)}, u32[]{:S(2)}) collective-permute-start(bf16[192,1024]{1,0:T(8,128)(2,1)S(1)} %copy-done.14), channel_id=1, source_target_pairs={{0,1},{1,0},{2,3},{3,2},{4,5},{5,4},{6,7},{7,6},{8,9},{9,8},{10,11... | collective-permute-start | bytes 1179656 | tf_op jit(solution)/shard_map/ppermute | solution.py:344
  74.0 2.0 %collective-permute-start.14 = (bf16[192,1024]{1,0:T(8,128)(2,1)}, bf16[192,1024]{1,0:T(8,128)(2,1)}, u32[]{:S(2)}, u32[]{:S(2)}) collective-permute-start(bf16[192,1024]{1,0:T(8,128)(2,1)} %collective-permute-done.13.refs_18_.refs_21_), channel_id=1, source_target_pairs={{0,1},{1,0},{2,3},{3,2},{4,5},{5,4},{6,7},{7,6},{8,9},{9,8},{10,11... | collective-permute-start | bytes 1179656 | tf_op jit(solution)/shard_map/ppermute | solution.py:344
  78.3 13.2 %forward.1 = (bf16[16,96,128]{2,1,0:T(8,128)(2,1)}, bf16[3072,128]{1,0:T(8,128)(2,1)}, bf16[24,128,128]{2,1,0:T(8,128)(2,1)}, bf16[3072,128]{1,0:T(8,128)(2,1)}) custom-call(s32[1]{0:T(128)} %bitcast.me_ref.refs_0_, s32[24,4]{1,0:T(8,128)} %copy.9.refs_1_, s32[24,4]{1,0:T(8,128)} %copy.10.refs_2_, bf16[32,64,128]{2,1,0:T(8,128)(2,1)} %copy-done.2, ...), custom_call_target="tpu_custom_call" | custom-call | tf_op jit(solution)/shard_map/forward/pallas_call | solution.py:116
  91.5 0.7 copy-done.3
  92.3 7.3 %all-to-all-start.2 = ((bf16[16,96,128]{2,1,0:T(8,128)(2,1)}), bf16[16,96,128]{2,1,0:T(8,128)(2,1)S(1)}, u32[]{:S(2)}, u32[]{:S(2)}) async-start(bf16[16,96,128]{2,1,0:T(8,128)(2,1)} %get-tuple-element.29), calls=%async_computation.2 | async-start | bytes 786432 | tf_op jit(solution)/shard_map/all_to_all | solution.py:378
  99.5 11.8 %backward.1 = bf16[32,48,128]{2,1,0:T(8,128)(2,1)} custom-call(s32[1]{0:T(128)} %bitcast.me_ref.refs_0_, s32[24,4]{1,0:T(8,128)} %copy.9.refs_1_, s32[24,4]{1,0:T(8,128)} %copy.10.refs_2_, bf16[16,96,128]{2,1,0:T(8,128)(2,1)} %copy-done.3, bf16[3072,128]{1,0:T(8,128)(2,1)} %get-tuple-element.26.refs_4_, bf16[24,128,128]{2,1,0:T(8,128)(2,1)} %get-tuple-element.27.refs_5_, ...), custom_call_target="tpu_custom_call" | custom-call | flops 12000000000 | bytes 20971520 | tf_op jit(solution)/shard_map/backward/pallas_call | solution.py:217
  111.3 2.8 %all-to-all-done.2.got_ref = bf16[16,96,128]{2,1,0:T(8,128)(2,1)S(1)} async-done(((bf16[16,96,128]{2,1,0:T(8,128)(2,1)}), bf16[16,96,128]{2,1,0:T(8,128)(2,1)S(1)}, u32[]{:S(2)}, u32[]{:S(2)}) %all-to-all-start.2) | async-done | bytes 393248 | tf_op jit(solution)/shard_map/all_to_all | solution.py:378
  114.1 0.9 place.1
  115.0 24.2 %all_to_all.20.got_ref = bf16[32,48,128]{2,1,0:T(8,128)(2,1)S(1)} all-to-all(bf16[32,48,128]{2,1,0:T(8,128)(2,1)S(1)} %copy-done.4), channel_id=1, replica_groups=mesh['dp'=32,'seq'=16] {'dp'}, dimensions={0} | all-to-all | bytes 786432 | tf_op jit(solution)/shard_map/all_to_all | solution.py:382
  139.2 0.8 total.1
  (53 shorter events, 2.4 us)
Async XLA Ops:
  0.6 14.1 %collective-permute-start = (bf16[192,1024]{1,0:T(8,128)(2,1)}, bf16[192,1024]{1,0:T(8,128)(2,1)S(1)}, u32[]{:S(2)}, u32[]{:S(2)}) collective-permute-start(bf16[192,1024]{1,0:T(8,128)(2,1)} %bitcast.11), channel_id=1, source_target_pairs={{0,1},{1,0},{2,3},{3,2},{4,5},{5,4},{6,7},{7,6},{8,9},{9,8},{10,11... | collective-permute-start | bytes 1179656 | tf_op jit(solution)/shard_map/ppermute | solution.py:344
  9.4 19.2 %collective-permute-start.1 = (bf16[192,1024]{1,0:T(8,128)(2,1)}, bf16[192,1024]{1,0:T(8,128)(2,1)S(1)}, u32[]{:S(2)}, u32[]{:S(2)}) collective-permute-start(bf16[192,1024]{1,0:T(8,128)(2,1)} %bitcast.12), channel_id=1, source_target_pairs={{0,2},{1,15},{2,4},{3,1},{4,6},{5,3},{6,8},{7,5},{8,10},{9,7},{10,... | collective-permute-start | bytes 1179656 | tf_op jit(solution)/shard_map/ppermute | solution.py:355
  14.7 4.1 %copy-start.5 = (bf16[192,1024]{1,0:T(8,128)(2,1)}, bf16[192,1024]{1,0:T(8,128)(2,1)S(1)}, u32[]{:S(2)}) copy-start(bf16[192,1024]{1,0:T(8,128)(2,1)S(1)} %collective-permute-done.refs_5_.refs_8_) | copy-start | bytes 1179652
  14.8 18.0 %collective-permute-start.3 = (bf16[192,1024]{1,0:T(8,128)(2,1)S(1)}, bf16[192,1024]{1,0:T(8,128)(2,1)S(1)}, u32[]{:S(2)}, u32[]{:S(2)}) collective-permute-start(bf16[192,1024]{1,0:T(8,128)(2,1)S(1)} %collective-permute-done.refs_5_.refs_8_), channel_id=1, source_target_pairs={{0,2},{1,15},{2,4},{3,1},{4,6},{5,3},{6,8},{7,5},{8,10},{9,7},{10,... | collective-permute-start | bytes 1179656 | tf_op jit(solution)/shard_map/ppermute | solution.py:357
  18.8 41.7 %copy-start = (bf16[1,192,1024]{2,1,0:T(8,128)(2,1)S(1)}, bf16[1,192,1024]{2,1,0:T(8,128)(2,1)}, u32[]{:S(2)}) copy-start(bf16[1,192,1024]{2,1,0:T(8,128)(2,1)} %param.6) | copy-start | bytes 1179652
  18.8 41.7 %all-to-all-start = ((bf16[32,64,128]{2,1,0:T(8,128)(2,1)}), bf16[32,64,128]{2,1,0:T(8,128)(2,1)S(1)}, u32[]{:S(2)}, u32[]{:S(2)}) async-start(bf16[32,64,128]{2,1,0:T(8,128)(2,1)} %pack_weights.1), calls=%async_computation | async-start | bytes 1048576 | tf_op jit(solution)/shard_map/all_to_all | solution.py:371
  28.6 32.9 %copy-start.6 = (bf16[192,1024]{1,0:T(8,128)(2,1)}, bf16[192,1024]{1,0:T(8,128)(2,1)S(1)}, u32[]{:S(2)}) copy-start(bf16[192,1024]{1,0:T(8,128)(2,1)S(1)} %collective-permute-done.1.refs_6_.refs_9_) | copy-start | bytes 1179652
  28.6 9.9 %collective-permute-start.2 = (bf16[192,1024]{1,0:T(8,128)(2,1)S(1)}, bf16[192,1024]{1,0:T(8,128)(2,1)S(1)}, u32[]{:S(2)}, u32[]{:S(2)}) collective-permute-start(bf16[192,1024]{1,0:T(8,128)(2,1)S(1)} %collective-permute-done.1.refs_6_.refs_9_), channel_id=1, source_target_pairs={{0,2},{1,15},{2,4},{3,1},{4,6},{5,3},{6,8},{7,5},{8,10},{9,7},{10,... | collective-permute-start | bytes 1179656 | tf_op jit(solution)/shard_map/ppermute | solution.py:355
  30.8 9.7 %collective-permute-start.6 = (bf16[192,1024]{1,0:T(8,128)(2,1)S(1)}, bf16[192,1024]{1,0:T(8,128)(2,1)S(1)}, u32[]{:S(2)}, u32[]{:S(2)}) collective-permute-start(bf16[192,1024]{1,0:T(8,128)(2,1)S(1)} %collective-permute-done.1.refs_6_.refs_9_), channel_id=1, source_target_pairs={{0,1},{1,0},{2,3},{3,2},{4,5},{5,4},{6,7},{7,6},{8,9},{9,8},{10,11... | collective-permute-start | bytes 1179656 | tf_op jit(solution)/shard_map/ppermute | solution.py:344
  32.8 28.8 %copy-start.7 = (bf16[192,1024]{1,0:T(8,128)(2,1)}, bf16[192,1024]{1,0:T(8,128)(2,1)S(1)}, u32[]{:S(2)}) copy-start(bf16[192,1024]{1,0:T(8,128)(2,1)S(1)} %collective-permute-done.3.refs_8_.refs_11_) | copy-start | bytes 1179652
  32.8 8.9 %collective-permute-start.4 = (bf16[192,1024]{1,0:T(8,128)(2,1)S(1)}, bf16[192,1024]{1,0:T(8,128)(2,1)S(1)}, u32[]{:S(2)}, u32[]{:S(2)}) collective-permute-start(bf16[192,1024]{1,0:T(8,128)(2,1)S(1)} %collective-permute-done.3.refs_8_.refs_11_), channel_id=1, source_target_pairs={{0,2},{1,15},{2,4},{3,1},{4,6},{5,3},{6,8},{7,5},{8,10},{9,7},{10,... | collective-permute-start | bytes 1179656 | tf_op jit(solution)/shard_map/ppermute | solution.py:357
  35.0 6.7 %collective-permute-start.5 = (bf16[192,1024]{1,0:T(8,128)(2,1)S(1)}, bf16[192,1024]{1,0:T(8,128)(2,1)S(1)}, u32[]{:S(2)}, u32[]{:S(2)}) collective-permute-start(bf16[192,1024]{1,0:T(8,128)(2,1)S(1)} %collective-permute-done.3.refs_8_.refs_11_), channel_id=1, source_target_pairs={{0,1},{1,0},{2,3},{3,2},{4,5},{5,4},{6,7},{7,6},{8,9},{9,8},{10,11... | collective-permute-start | bytes 1179656 | tf_op jit(solution)/shard_map/ppermute | solution.py:344
  38.6 39.3 %copy-start.8 = (bf16[192,1024]{1,0:T(8,128)(2,1)}, bf16[192,1024]{1,0:T(8,128)(2,1)S(1)}, u32[]{:S(2)}) copy-start(bf16[192,1024]{1,0:T(8,128)(2,1)S(1)} %collective-permute-done.2.refs_10_.refs_13_) | copy-start | bytes 1179652
  38.6 13.0 %collective-permute-start.10 = (bf16[192,1024]{1,0:T(8,128)(2,1)S(1)}, bf16[192,1024]{1,0:T(8,128)(2,1)S(1)}, u32[]{:S(2)}, u32[]{:S(2)}) collective-permute-start(bf16[192,1024]{1,0:T(8,128)(2,1)S(1)} %collective-permute-done.2.refs_10_.refs_13_), channel_id=1, source_target_pairs={{0,1},{1,0},{2,3},{3,2},{4,5},{5,4},{6,7},{7,6},{8,9},{9,8},{10,11... | collective-permute-start | bytes 1179656 | tf_op jit(solution)/shard_map/ppermute | solution.py:344
  40.5 37.4 %copy-start.9 = (bf16[192,1024]{1,0:T(8,128)(2,1)}, bf16[192,1024]{1,0:T(8,128)(2,1)S(1)}, u32[]{:S(2)}) copy-start(bf16[192,1024]{1,0:T(8,128)(2,1)S(1)} %collective-permute-done.6.refs_7_.refs_10_) | copy-start | bytes 1179652
  41.7 36.3 %copy-start.10 = (bf16[192,1024]{1,0:T(8,128)(2,1)}, bf16[192,1024]{1,0:T(8,128)(2,1)S(1)}, u32[]{:S(2)}) copy-start(bf16[192,1024]{1,0:T(8,128)(2,1)S(1)} %collective-permute-done.4.refs_12_.refs_15_) | copy-start | bytes 1179652
  41.7 36.3 %copy-start.11 = (bf16[192,1024]{1,0:T(8,128)(2,1)}, bf16[192,1024]{1,0:T(8,128)(2,1)S(1)}, u32[]{:S(2)}) copy-start(bf16[192,1024]{1,0:T(8,128)(2,1)S(1)} %collective-permute-done.5.refs_9_.refs_12_) | copy-start | bytes 1179652
  41.7 10.0 %collective-permute-start.7 = (bf16[192,1024]{1,0:T(8,128)(2,1)S(1)}, bf16[192,1024]{1,0:T(8,128)(2,1)}, u32[]{:S(2)}, u32[]{:S(2)}) collective-permute-start(bf16[192,1024]{1,0:T(8,128)(2,1)S(1)} %collective-permute-done.2.refs_10_.refs_13_), channel_id=1, source_target_pairs={{0,2},{1,15},{2,4},{3,1},{4,6},{5,3},{6,8},{7,5},{8,10},{9,7},{10,... | collective-permute-start | bytes 1179656 | tf_op jit(solution)/shard_map/ppermute | solution.py:355
  45.1 9.7 %collective-permute-start.8 = (bf16[192,1024]{1,0:T(8,128)(2,1)S(1)}, bf16[192,1024]{1,0:T(8,128)(2,1)S(1)}, u32[]{:S(2)}, u32[]{:S(2)}) collective-permute-start(bf16[192,1024]{1,0:T(8,128)(2,1)S(1)} %collective-permute-done.4.refs_12_.refs_15_), channel_id=1, source_target_pairs={{0,2},{1,15},{2,4},{3,1},{4,6},{5,3},{6,8},{7,5},{8,10},{9,7},{10,... | collective-permute-start | bytes 1179656 | tf_op jit(solution)/shard_map/ppermute | solution.py:357
  47.0 7.8 %collective-permute-start.9 = (bf16[192,1024]{1,0:T(8,128)(2,1)S(1)}, bf16[192,1024]{1,0:T(8,128)(2,1)S(1)}, u32[]{:S(2)}, u32[]{:S(2)}) collective-permute-start(bf16[192,1024]{1,0:T(8,128)(2,1)S(1)} %collective-permute-done.4.refs_12_.refs_15_), channel_id=1, source_target_pairs={{0,1},{1,0},{2,3},{3,2},{4,5},{5,4},{6,7},{7,6},{8,9},{9,8},{10,11... | collective-permute-start | bytes 1179656 | tf_op jit(solution)/shard_map/ppermute | solution.py:344
  51.6 3.1 %copy-start.12 = (bf16[192,1024]{1,0:T(8,128)(2,1)}, bf16[192,1024]{1,0:T(8,128)(2,1)S(1)}, u32[]{:S(2)}) copy-start(bf16[192,1024]{1,0:T(8,128)(2,1)S(1)} %collective-permute-done.10.refs_11_.refs_14_) | copy-start | bytes 1179652
  56.3 17.7 %collective-permute-start.13 = (bf16[192,1024]{1,0:T(8,128)(2,1)}, bf16[192,1024]{1,0:T(8,128)(2,1)}, u32[]{:S(2)}, u32[]{:S(2)}) collective-permute-start(bf16[192,1024]{1,0:T(8,128)(2,1)} %collective-permute-done.7.refs_14_.refs_17_), channel_id=1, source_target_pairs={{0,2},{1,15},{2,4},{3,1},{4,6},{5,3},{6,8},{7,5},{8,10},{9,7},{10,... | collective-permute-start | bytes 1179656 | tf_op jit(solution)/shard_map/ppermute | solution.py:355
  60.5 1.0 copy-start.2
  61.5 10.1 %copy-start.14 = (bf16[192,1024]{1,0:T(8,128)(2,1)S(1)}, bf16[192,1024]{1,0:T(8,128)(2,1)}, u32[]{:S(2)}) copy-start(bf16[192,1024]{1,0:T(8,128)(2,1)} %copy-done.13) | copy-start | bytes 1179652
  61.5 14.5 %copy-start.18 = (s32[1,1,24,4]{2,3,1,0:T(4,128)S(1)}, s32[1,1,24,4]{2,3,1,0:T(4,128)}, u32[]{:S(2)}) copy-start(s32[1,1,24,4]{2,3,1,0:T(4,128)} %param.9) | copy-start | bytes 1156
  61.5 15.2 %copy-start.19 = (s32[1,1,24,4]{2,3,1,0:T(4,128)S(1)}, s32[1,1,24,4]{2,3,1,0:T(4,128)}, u32[]{:S(2)}) copy-start(s32[1,1,24,4]{2,3,1,0:T(4,128)} %param.8) | copy-start | bytes 1156
  61.5 30.0 %all-to-all-start.1 = ((bf16[16,96,128]{2,1,0:T(8,128)(2,1)}), bf16[16,96,128]{2,1,0:T(8,128)(2,1)S(1)}, u32[]{:S(2)}, u32[]{:S(2)}) async-start(bf16[16,96,128]{2,1,0:T(8,128)(2,1)} %pack_cotangent.1), calls=%async_computation.1 | async-start | bytes 786432 | tf_op jit(solution)/shard_map/all_to_all | solution.py:373
  69.6 7.8 %collective-permute-start.11 = (bf16[192,1024]{1,0:T(8,128)(2,1)}, bf16[192,1024]{1,0:T(8,128)(2,1)S(1)}, u32[]{:S(2)}, u32[]{:S(2)}) collective-permute-start(bf16[192,1024]{1,0:T(8,128)(2,1)} %collective-permute-done.7.refs_14_.refs_17_), channel_id=1, source_target_pairs={{0,1},{1,0},{2,3},{3,2},{4,5},{5,4},{6,7},{7,6},{8,9},{9,8},{10,11... | collective-permute-start | bytes 1179656 | tf_op jit(solution)/shard_map/ppermute | solution.py:344
  71.6 5.7 %collective-permute-start.12 = (bf16[192,1024]{1,0:T(8,128)(2,1)S(1)}, bf16[192,1024]{1,0:T(8,128)(2,1)S(1)}, u32[]{:S(2)}, u32[]{:S(2)}) collective-permute-start(bf16[192,1024]{1,0:T(8,128)(2,1)S(1)} %copy-done.14), channel_id=1, source_target_pairs={{0,1},{1,0},{2,3},{3,2},{4,5},{5,4},{6,7},{7,6},{8,9},{9,8},{10,11... | collective-permute-start | bytes 1179656 | tf_op jit(solution)/shard_map/ppermute | solution.py:344
  74.0 4.0 %collective-permute-start.14 = (bf16[192,1024]{1,0:T(8,128)(2,1)}, bf16[192,1024]{1,0:T(8,128)(2,1)}, u32[]{:S(2)}, u32[]{:S(2)}) collective-permute-start(bf16[192,1024]{1,0:T(8,128)(2,1)} %collective-permute-done.13.refs_18_.refs_21_), channel_id=1, source_target_pairs={{0,1},{1,0},{2,3},{3,2},{4,5},{5,4},{6,7},{7,6},{8,9},{9,8},{10,11... | collective-permute-start | bytes 1179656 | tf_op jit(solution)/shard_map/ppermute | solution.py:344
  92.3 21.8 %all-to-all-start.2 = ((bf16[16,96,128]{2,1,0:T(8,128)(2,1)}), bf16[16,96,128]{2,1,0:T(8,128)(2,1)S(1)}, u32[]{:S(2)}, u32[]{:S(2)}) async-start(bf16[16,96,128]{2,1,0:T(8,128)(2,1)} %get-tuple-element.29), calls=%async_computation.2 | async-start | bytes 786432 | tf_op jit(solution)/shard_map/all_to_all | solution.py:378
  111.3 3.7 %copy-start.4 = (bf16[32,48,128]{2,1,0:T(8,128)(2,1)S(1)}, bf16[32,48,128]{2,1,0:T(8,128)(2,1)}, u32[]{:S(2)}) copy-start(bf16[32,48,128]{2,1,0:T(8,128)(2,1)} %backward.1) | copy-start | bytes 1179652
  (6 other events, 4.9 us)

commit v6 on v4

v6 whole, which is shorter than its diff:
```python
import functools

import jax
import jax.numpy as jnp
from jax import lax
from jax.experimental import pallas as pl
from jax.experimental.pallas import tpu as pltpu
from jax.sharding import PartitionSpec as P

HD = 64
BLOCK = 128
LOG2E = 1.4426950408889634
UNROLL = 12
AHEAD = 12
CHUNKS = 6
FLIGHT = 6

NN = (((1,), (0,)), ((), ()))
NT = (((1,), (1,)), ((), ()))


def mm(a, b, dims=NN):
    return lax.dot_general(a, b, dims, preferred_element_type=jnp.float32)


def row(b):
    return pl.ds(pl.multiple_of(b * BLOCK, BLOCK), BLOCK)


def softmax(scores, live):
    parts = [scores[j * BLOCK:(j + 1) * BLOCK] * (HD ** -0.5 * LOG2E) for j in range(len(live))]
    tops = [
        jnp.where(ok, jnp.max(part, axis=0, keepdims=True), -jnp.inf)
        for ok, part in zip(live, parts)
    ]
    top = functools.reduce(jnp.maximum, tops)
    exponent = jnp.concatenate(
        [jnp.exp2(part - jnp.where(ok, top, jnp.inf)) for ok, part in zip(live, parts)], axis=0
    )
    return exponent * (1.0 / jnp.sum(exponent, axis=0, keepdims=True))


def forward_kernel(
    pairs_ref, valid_ref, w_ref, vol_hbm, att_ref, kv_hbm, kvt_hbm, q_hbm,
    vol_ref, kv_ref, kvt_ref, q_ref, in_sems, out_sems,
):
    rows = vol_ref.shape[0]
    n_blocks, slots = pairs_ref.shape
    half = att_ref.shape[1]
    chunk = rows // CHUNKS
    copies = [
        pltpu.make_async_copy(
            vol_hbm.at[pl.ds(c * chunk, chunk)], vol_ref.at[pl.ds(c * chunk, chunk)], in_sems.at[c]
        )
        for c in range(CHUNKS)
    ]
    for copy in copies[:FLIGHT]:
        copy.start()
    for c in range(CHUNKS):
        copies[c].wait()
        if c + FLIGHT < CHUNKS:
            copies[c + FLIGHT].start()
        at = pl.ds(c * chunk, chunk)
        got = mm(vol_ref[at, :], w_ref[...])
        q_ref[at, :] = got[:, BLOCK:].astype(jnp.bfloat16)
        kv = got[:, :BLOCK].astype(jnp.bfloat16)
        kv_ref[at, :] = kv
        for b in range(chunk // BLOCK):
            kvt_ref[c * (chunk // BLOCK) + b] = kv[b * BLOCK:(b + 1) * BLOCK].T
    kept = [
        pltpu.make_async_copy(ref, hbm, out_sems.at[i])
        for i, (ref, hbm) in enumerate(((kv_ref, kv_hbm), (kvt_ref, kvt_hbm), (q_ref, q_hbm)))
    ]
    for copy in kept:
        copy.start()

    def body(i, carry):
        blocks = [i * AHEAD + u for u in range(AHEAD)]
        names = [[pairs_ref[b, j] for j in range(slots)] for b in blocks]
        scores = [
            mm(jnp.concatenate([kv_ref[row(n), :] for n in some], axis=0), q_ref[row(b), :], NT)
            for b, some in zip(blocks, names)
        ]
        probs = [
            softmax(s, [valid_ref[b, j] > 0 for j in range(slots)]).astype(jnp.bfloat16)
            for b, s in zip(blocks, scores)
        ]
        outs = []
        for b, some, p in zip(blocks, names, probs):
            values = jnp.concatenate([kvt_ref[n, HD:] for n in some], axis=1)
            out_t = mm(values, p)
            both = jnp.concatenate([out_t, out_t], axis=0).T.astype(jnp.bfloat16)
            outs.append(both)
        for g in range(AHEAD // 3):
            tokens = jnp.concatenate(outs[3 * g:3 * g + 3], axis=0)
            for h in range(4):
                span = tokens[h * half:(h + 1) * half]
                side = slice(HD * (h % 2), HD * (h % 2) + HD)
                att_ref[(i * (AHEAD // 3) + g) * 2 + h // 2, :, side] = span[:, side]
        return carry

    lax.fori_loop(0, n_blocks // AHEAD, body, 0)
    for copy in kept:
        copy.wait()


def forward_call(pairs, valid, w, vol, peers):
    rows, width = vol.shape
    n_blocks = rows // BLOCK
    vmem = pl.BlockSpec(memory_space=pltpu.VMEM)
    smem = pl.BlockSpec(memory_space=pltpu.SMEM)
    hbm = pl.BlockSpec(memory_space=pl.ANY)
    flat = jax.ShapeDtypeStruct((rows, BLOCK), jnp.bfloat16)
    square = jax.ShapeDtypeStruct((n_blocks, BLOCK, BLOCK), jnp.bfloat16)
    return pl.pallas_call(
        forward_kernel,
        out_shape=(
            jax.ShapeDtypeStruct((peers, rows // peers // 2, BLOCK), jnp.bfloat16),
            flat,
            square,
            flat,
        ),
        in_specs=[smem] * 2 + [vmem, hbm],
        out_specs=(vmem, hbm, hbm, hbm),
        scratch_shapes=[
            pltpu.VMEM((rows, width), jnp.bfloat16),
            pltpu.VMEM(flat.shape, flat.dtype),
            pltpu.VMEM(square.shape, square.dtype),
            pltpu.VMEM(flat.shape, flat.dtype),
            pltpu.SemaphoreType.DMA((CHUNKS,)),
            pltpu.SemaphoreType.DMA((3,)),
        ],
        compiler_params=pltpu.CompilerParams(vmem_limit_bytes=56 * 2**20),
        name="forward",
    )(pairs, valid, w, vol)


def spread_kernel(cot_ref, out_ref):
    peers, half, _ = cot_ref.shape
    blank = jnp.zeros((half, HD), cot_ref.dtype)
    for s in range(peers):
        both = cot_ref[s]
        out_ref[pl.ds(2 * half * s, half), :] = jnp.concatenate([blank, both[:, :HD]], axis=1)
        out_ref[pl.ds(2 * half * s + half, half), :] = jnp.concatenate([blank, both[:, HD:]], axis=1)


def spread_call(cot):
    peers, half, lanes = cot.shape
    vmem = pl.BlockSpec(memory_space=pltpu.VMEM)
    return pl.pallas_call(
        spread_kernel,
        out_shape=jax.ShapeDtypeStruct((2 * half * peers, lanes), cot.dtype),
        in_specs=[vmem],
        out_specs=vmem,
        compiler_params=pltpu.CompilerParams(vmem_limit_bytes=8 * 2**20),
        name="spread",
    )(cot)


def backward_kernel(
    pairs_ref, valid_ref, do_hbm, kv_hbm, kvt_hbm, q_hbm, vol_hbm, wg_ref,
    do_ref, kv_ref, kvt_ref, q_ref, vol_ref, acc_ref, dt_ref, sems,
):
    width = vol_ref.shape[1]
    n_blocks, slots = pairs_ref.shape
    scale = HD ** -0.5
    copies = [
        pltpu.make_async_copy(hbm, ref, sems.at[i])
        for i, (hbm, ref) in enumerate(
            ((kv_hbm, kv_ref), (q_hbm, q_ref), (do_hbm, do_ref), (kvt_hbm, kvt_ref), (vol_hbm, vol_ref))
        )
    ]
    for copy in copies[:-1]:
        copy.start()
    acc_ref[...] = jnp.zeros_like(acc_ref)
    for copy in copies[:-1]:
        copy.wait()
    copies[-1].start()

    def body(i, carry):
        blocks = [i * UNROLL + u for u in range(UNROLL)]
        names = [[pairs_ref[b, j] for j in range(slots)] for b in blocks]
        rhs = [jnp.concatenate([q_ref[row(b), :], do_ref[row(b), :]], axis=0) for b in blocks]
        both = [
            mm(jnp.concatenate([kv_ref[row(n), :] for n in some], axis=0), r, NT)
            for some, r in zip(names, rhs)
        ]
        sent = []
        for b, pair in zip(blocks, both):
            probs = softmax(pair[:, :BLOCK], [valid_ref[b, j] > 0 for j in range(slots)])
            weighted = probs * pair[:, BLOCK:]
            row_dot = jnp.sum(weighted, axis=0, keepdims=True)
            score_grad = (weighted - probs * row_dot).astype(jnp.bfloat16)
            sent.append((score_grad, probs.astype(jnp.bfloat16)))
        for b, some, pair in zip(blocks, names, sent):
            keys = jnp.concatenate([kvt_ref[n, :HD] for n in some], axis=1)
            dt_ref[BLOCK:, row(b)] = (mm(keys, pair[0]) * scale).astype(jnp.bfloat16)
        for some, pair, r in zip(names, sent, rhs):
            back = mm(jnp.concatenate(pair, axis=1), r)
            for j in range(slots):
                acc_ref[some[j]] += back[j * BLOCK:(j + 1) * BLOCK]
        return carry

    lax.fori_loop(0, n_blocks // UNROLL, body, 0)

    lane = lax.broadcasted_iota(jnp.int32, (BLOCK, BLOCK), 1)
    factor = jnp.where(lane < HD, scale, 1.0)
    for b in range(n_blocks):
        dt_ref[:BLOCK, b * BLOCK:(b + 1) * BLOCK] = (acc_ref[b] * factor).astype(jnp.bfloat16).T

    copies[-1].wait()
    owners = wg_ref.shape[0]
    mine = width // owners
    part = 256
    for n in range(width // part):
        got = mm(dt_ref[...], vol_ref[:, n * part:(n + 1) * part]).astype(jnp.bfloat16)
        kv_part = got[:BLOCK].T
        q_part = got[BLOCK:].T
        for k in range(part // mine):
            owner = n * (part // mine) + k
            wg_ref[owner, :mine] = kv_part[k * mine:(k + 1) * mine]
            q_rows = q_part[k * mine:(k + 1) * mine]
            wg_ref[owner, mine:] = jnp.concatenate([q_rows[:mine // 2], q_rows[mine // 2:]], axis=1)


def backward_call(pairs, valid, d_out, kv, kvt, q, vol, owners):
    rows, width = vol.shape
    n_blocks = rows // BLOCK
    mine = width // owners
    vmem = pl.BlockSpec(memory_space=pltpu.VMEM)
    smem = pl.BlockSpec(memory_space=pltpu.SMEM)
    return pl.pallas_call(
        backward_kernel,
        out_shape=jax.ShapeDtypeStruct((owners, mine + mine // 2, BLOCK), jnp.bfloat16),
        in_specs=[smem] * 2 + [pl.BlockSpec(memory_space=pl.ANY)] * 5,
        out_specs=vmem,
        scratch_shapes=[
            pltpu.VMEM((rows, BLOCK), jnp.bfloat16),
            pltpu.VMEM((rows, BLOCK), jnp.bfloat16),
            pltpu.VMEM((n_blocks, BLOCK, BLOCK), jnp.bfloat16),
            pltpu.VMEM((rows, BLOCK), jnp.bfloat16),
            pltpu.VMEM((rows, width), jnp.bfloat16),
            pltpu.VMEM((n_blocks, BLOCK, BLOCK), jnp.float32),
            pltpu.VMEM((BLOCK + HD, rows), jnp.bfloat16),
            pltpu.SemaphoreType.DMA((5,)),
        ],
        compiler_params=pltpu.CompilerParams(vmem_limit_bytes=56 * 2**20),
        cost_estimate=pl.CostEstimate(
            flops=12 * 10**9, bytes_accessed=20 * 2**20, transcendentals=n_blocks * 2**16
        ),
        name="backward",
    )(pairs, valid, d_out, kv, kvt, q, vol)


def finish_kernel(att_ref, wg_ref, out_ref, total_ref):
    mine = total_ref.shape[1]
    total = wg_ref[0].astype(jnp.float32)
    for i in range(1, wg_ref.shape[0]):
        total += wg_ref[i].astype(jnp.float32)
    total_ref[0, :mine // 2] = total[mine:, :HD]
    total_ref[0, mine // 2:] = total[mine:, HD:]
    total_ref[1] = total[:mine, :HD]
    total_ref[2] = total[:mine, HD:]
    peers, half, _ = att_ref.shape
    for p in range(peers // 2):
        one, two = att_ref[2 * p], att_ref[2 * p + 1]
        at = pl.ds(p * BLOCK, BLOCK)
        out_ref[:half, at] = jnp.concatenate([one[:, :HD], two[:, :HD]], axis=1)
        out_ref[half:, at] = jnp.concatenate([one[:, HD:], two[:, HD:]], axis=1)


def finish_call(att, wg, mine):
    peers, half, _ = att.shape
    vmem = pl.BlockSpec(memory_space=pltpu.VMEM)
    return pl.pallas_call(
        finish_kernel,
        out_shape=(
            jax.ShapeDtypeStruct((2 * half, peers * HD), att.dtype),
            jax.ShapeDtypeStruct((3, mine, HD), jnp.float32),
        ),
        in_specs=[vmem] * 2,
        out_specs=(vmem,) * 2,
        compiler_params=pltpu.CompilerParams(vmem_limit_bytes=8 * 2**20),
        name="finish",
    )(att, wg)


def local(volume, cotangent, weights, pairs, valid):
    peers = lax.axis_size("seq")
    owners = lax.axis_size("dp")
    vol, cot = volume[0], cotangent[0]
    toks, width = vol.shape
    w_rows = weights.shape[0]
    half = toks // 2

    gathered = lax.all_gather(vol, "seq", axis=0, tiled=True)

    cot = cot.reshape(2, half, peers, HD).transpose(2, 1, 0, 3).reshape(peers, half, 2 * HD)
    cot = lax.all_to_all(cot, "seq", split_axis=0, concat_axis=0, tiled=True)
    weights, cot = lax.optimization_barrier((weights, cot))
    d_out = spread_call(cot)

    column = lax.axis_index("seq") * HD
    part = lax.dynamic_slice_in_dim(weights, column, HD, axis=2)
    part = jnp.stack([part[:, 1], part[:, 2], part[:, 0]], axis=1).reshape(-1, BLOCK)
    sent = jnp.broadcast_to(part[None], (owners, *part.shape))
    w = lax.all_to_all(sent, "dp", split_axis=0, concat_axis=0, tiled=True)
    w = w.reshape(owners * w_rows, 3 * HD)
    w = jnp.pad(w, ((0, 0), (0, HD)))

    pairs, valid = pairs[0, 0], valid[0, 0]
    att, kv, kvt, q = forward_call(pairs, valid, w, gathered, peers)
    att = lax.all_to_all(att, "seq", split_axis=0, concat_axis=0, tiled=True)
    wg = backward_call(pairs, valid, d_out, kv, kvt, q, gathered, owners)
    wg, att = lax.optimization_barrier((wg, att))
    wg = lax.all_to_all(wg, "dp", split_axis=0, concat_axis=0, tiled=True)
    att, total = finish_call(att, wg, w_rows)
    return att[None], total.transpose(1, 0, 2)


def solution(mesh):
    return jax.shard_map(
        local,
        mesh=mesh,
        in_specs=(
            P("dp", "seq", None),
            P("dp", "seq", None),
            P("dp", None, None),
            P("dp", "seq", None, None),
            P("dp", "seq", None, None),
        ),
        out_specs=(P("dp", "seq", None), P("dp", None, "seq")),
        check_vma=False,
    )
```

time: 131 us -> 129 us (0.985)
  Pallas kernels: 25.5 us -> 23.7 us
    pallas_call x1, Pallas kernels: 12.2 us -> 10.7 us  [forward_call(): pl.pallas_call(forward_kernel, out_shape=(jax.ShapeDtypeStruct((peers, ro...]
where the time goes in v6:
time: 129 us
  waiting for transfers between devices  32.5 us (25%)
  starting transfers between devices  26.6 us (21%)
  blocking collectives  24.6 us (19%)
  Pallas kernels  23.7 us (18%)
  between operations  14.1 us (11%)
  local copies, waits for them, and re-layouts  7.15 us (6%)
    all_to_all x1, blocking collectives, local(): wg = lax.all_to_all(wg, 'dp', split_axis=0, concat_axis=0, tiled=True)  24.6 us
    all_to_all x1, waiting for transfers between devices, local(): cot = lax.all_to_all(cot, 'seq', split_axis=0, concat_axis=0, tiled=True)  14 us
    all_to_all x1, waiting for transfers between devices, local(): w = lax.all_to_all(sent, 'dp', split_axis=0, concat_axis=0, tiled=True)  12 us
    all_to_all x1, starting transfers between devices, local(): cot = lax.all_to_all(cot, 'seq', split_axis=0, concat_axis=0, tiled=True)  11.8 us
    pallas_call x1, Pallas kernels, backward_call(): pl.pallas_call(backward_kernel, out_shape=jax.ShapeDtypeStruct((owners, m...  11.8 us
    pallas_call x1, Pallas kernels, forward_call(): pl.pallas_call(forward_kernel, out_shape=(jax.ShapeDtypeStruct((peers, ro...  10.7 us
    all_to_all x1, starting transfers between devices, local(): w = lax.all_to_all(sent, 'dp', split_axis=0, concat_axis=0, tiled=True)  10.1 us
    all_to_all x1, starting transfers between devices, local(): att = lax.all_to_all(att, 'seq', split_axis=0, concat_axis=0, tiled=True)  4.63 us
  transfers between devices with their start and end apart: 4, of which 4 were waited for; matrix products, arithmetic and copies ran while one was open for 5% of the time, Pallas kernels for 9%

profile of v6, /device:TPU:1, one launch (start us, length us, event | category | flops | bytes accessed | tf_op | source)
XLA Modules:
  0.0 128.6 jit_solution(5549929709053739576)
XLA Ops:
  7.2 0.0 copy-start
  7.2 0.0 copy-start.2
  7.2 0.0 copy-start.3
  7.2 0.0 all-gather.3.cloned.1.call-start
  7.2 0.7 all-gather.3.cloned.1.call-update
  7.9 1.2 copy.12
  9.1 0.3 reshape_squeeze.3
  9.4 0.1 copy.13
  9.6 1.0 copy.14
  10.5 11.8 %all-to-all-start = ((bf16[16,96,128]{2,1,0:T(8,128)(2,1)}), bf16[16,96,128]{2,1,0:T(8,128)(2,1)S(1)}, u32[]{:S(2)}, u32[]{:S(2)}) async-start(bf16[16,96,128]{2,1,0:T(8,128)(2,1)} %copy.14), calls=%async_computation | async-start | bytes 786432 | tf_op jit(solution)/shard_map/all_to_all | solution.py:299
  22.3 14.0 %all-to-all-done.cot_ref = bf16[16,96,128]{2,1,0:T(8,128)(2,1)S(1)} async-done(((bf16[16,96,128]{2,1,0:T(8,128)(2,1)}), bf16[16,96,128]{2,1,0:T(8,128)(2,1)S(1)}, u32[]{:S(2)}, u32[]{:S(2)}) %all-to-all-start) | async-done | bytes 393248 | tf_op jit(solution)/shard_map/all_to_all | solution.py:299
  36.4 0.1 constant_dynamic-slice_fusion.1
  36.4 0.1 constant_dynamic-slice_fusion
  36.6 0.1 broadcast_in_dim.10
  36.7 0.8 broadcast_in_dim.11
  37.5 10.1 %all-to-all-start.1 = ((bf16[32,48,128]{2,1,0:T(8,128)(2,1)}), bf16[32,48,128]{2,1,0:T(8,128)(2,1)S(1)}, u32[]{:S(2)}, u32[]{:S(2)}) async-start(bf16[32,48,128]{2,1,0:T(8,128)(2,1)} %broadcast_in_dim.11), calls=%async_computation.1 | async-start | bytes 786432 | tf_op jit(solution)/shard_map/all_to_all | solution.py:307
  47.5 0.7 copy.18.pairs_ref
  48.2 0.0 copy-done.3
  48.2 0.7 copy.19.valid_ref
  48.9 0.2 spread.1.do_hbm
  49.1 0.0 copy-start.1
  49.1 0.9 copy-done.1
  50.0 12.0 %all-to-all-done.1 = bf16[32,48,128]{2,1,0:T(8,128)(2,1)S(1)} async-done(((bf16[32,48,128]{2,1,0:T(8,128)(2,1)}), bf16[32,48,128]{2,1,0:T(8,128)(2,1)S(1)}, u32[]{:S(2)}, u32[]{:S(2)}) %all-to-all-start.1) | async-done | bytes 393248 | tf_op jit(solution)/shard_map/all_to_all | solution.py:307
  61.9 0.3 reshape.12
  62.3 0.9 pad.4.w_ref
  63.2 3.1 %all-gather.3.cloned.1.call-done = bf16[1,3072,1024]{2,1,0:T(8,128)(2,1)} async-done(((bf16[1,192,1024]{2,1,0:T(8,128)(2,1)}), bf16[1,3072,1024]{2,1,0:T(8,128)(2,1)}) %all-gather.3.cloned.1.call-update) | async-done | bytes 6291472 | tf_op jit(solution)/shard_map/all_gather | solution.py:296
  66.3 10.7 %forward.1 = (bf16[16,96,128]{2,1,0:T(8,128)(2,1)}, bf16[3072,128]{1,0:T(8,128)(2,1)}, bf16[24,128,128]{2,1,0:T(8,128)(2,1)}, bf16[3072,128]{1,0:T(8,128)(2,1)}) custom-call(s32[24,4]{1,0:T(8,128)} %copy.18.pairs_ref, s32[24,4]{1,0:T(8,128)} %copy.19.valid_ref, bf16[1024,256]{1,0:T(8,128)(2,1)} %pad.4.w_ref, bf16[3072,1024]{1,0:T(8,128)(2,1)} %bitcast.9), custom_call_target="tpu_custom_call" | custom-call | tf_op jit(solution)/shard_map/forward/pallas_call | solution.py:115
  77.0 4.6 %all-to-all-start.2 = ((bf16[16,96,128]{2,1,0:T(8,128)(2,1)}), bf16[16,96,128]{2,1,0:T(8,128)(2,1)S(1)}, u32[]{:S(2)}, u32[]{:S(2)}) async-start(bf16[16,96,128]{2,1,0:T(8,128)(2,1)} %get-tuple-element.17), calls=%async_computation.2 | async-start | bytes 786432 | tf_op jit(solution)/shard_map/all_to_all | solution.py:313
  81.7 11.8 %backward.1 = bf16[32,48,128]{2,1,0:T(8,128)(2,1)} custom-call(s32[24,4]{1,0:T(8,128)} %copy.18.pairs_ref, s32[24,4]{1,0:T(8,128)} %copy.19.valid_ref, bf16[3072,128]{1,0:T(8,128)(2,1)} %copy-done.1, bf16[3072,128]{1,0:T(8,128)(2,1)} %get-tuple-element.14.kv_hbm, bf16[24,128,128]{2,1,0:T(8,128)(2,1)} %get-tuple-element.15.kvt_hbm, ...), custom_call_target="tpu_custom_call" | custom-call | flops 12000000000 | bytes 20971520 | tf_op jit(solution)/shard_map/backward/pallas_call | solution.py:232
  93.5 2.7 %all-to-all-done.2.att_ref = bf16[16,96,128]{2,1,0:T(8,128)(2,1)S(1)} async-done(((bf16[16,96,128]{2,1,0:T(8,128)(2,1)}), bf16[16,96,128]{2,1,0:T(8,128)(2,1)S(1)}, u32[]{:S(2)}, u32[]{:S(2)}) %all-to-all-start.2) | async-done | bytes 393248 | tf_op jit(solution)/shard_map/all_to_all | solution.py:313
  96.2 24.6 %all_to_all.20.wg_ref = bf16[32,48,128]{2,1,0:T(8,128)(2,1)S(1)} all-to-all(bf16[32,48,128]{2,1,0:T(8,128)(2,1)} %backward.1), channel_id=1, replica_groups=mesh['dp'=32,'seq'=16] {'dp'}, dimensions={0} | all-to-all | bytes 786432 | tf_op jit(solution)/shard_map/all_to_all | solution.py:316
  120.8 1.0 finish.1
  (4 shorter events, 0.0 us)
Async XLA Ops:
  7.2 29.2 %copy-start = (bf16[32,3,1024]{2,0,1:T(8,128)(2,1)S(1)}, bf16[32,3,1024]{2,0,1:T(8,128)(2,1)}, u32[]{:S(2)}) copy-start(bf16[32,3,1024]{2,0,1:T(8,128)(2,1)} %param.7) | copy-start | bytes 589828
  7.2 40.4 %copy-start.2 = (s32[1,1,24,4]{2,3,1,0:T(4,128)S(1)}, s32[1,1,24,4]{2,3,1,0:T(4,128)}, u32[]{:S(2)}) copy-start(s32[1,1,24,4]{2,3,1,0:T(4,128)} %param.8) | copy-start | bytes 1156
  7.2 41.0 %copy-start.3 = (s32[1,1,24,4]{2,3,1,0:T(4,128)S(1)}, s32[1,1,24,4]{2,3,1,0:T(4,128)}, u32[]{:S(2)}) copy-start(s32[1,1,24,4]{2,3,1,0:T(4,128)} %param.9) | copy-start | bytes 1156
  7.2 59.1 %all-gather.3.cloned.1.call-start = ((), (), s32[]{:S(2)}) async-start(), calls=%async_computation.4 | async-start | bytes 6684672 | tf_op jit(solution)/shard_map/all_gather | solution.py:296
  10.5 25.9 %all-to-all-start = ((bf16[16,96,128]{2,1,0:T(8,128)(2,1)}), bf16[16,96,128]{2,1,0:T(8,128)(2,1)S(1)}, u32[]{:S(2)}, u32[]{:S(2)}) async-start(bf16[16,96,128]{2,1,0:T(8,128)(2,1)} %copy.14), calls=%async_computation | async-start | bytes 786432 | tf_op jit(solution)/shard_map/all_to_all | solution.py:299
  37.5 24.5 %all-to-all-start.1 = ((bf16[32,48,128]{2,1,0:T(8,128)(2,1)}), bf16[32,48,128]{2,1,0:T(8,128)(2,1)S(1)}, u32[]{:S(2)}, u32[]{:S(2)}) async-start(bf16[32,48,128]{2,1,0:T(8,128)(2,1)} %broadcast_in_dim.11), calls=%async_computation.1 | async-start | bytes 786432 | tf_op jit(solution)/shard_map/all_to_all | solution.py:307
  49.1 0.9 copy-start.1
  77.0 19.2 %all-to-all-start.2 = ((bf16[16,96,128]{2,1,0:T(8,128)(2,1)}), bf16[16,96,128]{2,1,0:T(8,128)(2,1)S(1)}, u32[]{:S(2)}, u32[]{:S(2)}) async-start(bf16[16,96,128]{2,1,0:T(8,128)(2,1)} %get-tuple-element.17), calls=%async_computation.2 | async-start | bytes 786432 | tf_op jit(solution)/shard_map/all_to_all | solution.py:313
Sparse Core Ops, SparseCore 0:
  10.2 56.1 all-gather.2

commit v7 on v6

--- a/solution.py
+++ b/solution.py
@@ -12,8 +12,9 @@
 LOG2E = 1.4426950408889634
 UNROLL = 12
 AHEAD = 12
-CHUNKS = 6
-FLIGHT = 6
+CHUNKS = 1
+FLIGHT = 1
+PART = 512
 
 NN = (((1,), (0,)), ((), ()))
 NT = (((1,), (1,)), ((), ()))
@@ -41,8 +42,8 @@
 
 
 def forward_kernel(
-    pairs_ref, valid_ref, w_ref, vol_hbm, att_ref, kv_hbm, kvt_hbm, q_hbm,
-    vol_ref, kv_ref, kvt_ref, q_ref, in_sems, out_sems,
+    pairs_ref, valid_ref, w_ref, vol_hbm, att_ref, kv_hbm, kt_hbm, q_hbm,
+    vol_ref, kv_ref, kt_ref, vt_ref, q_ref, in_sems, out_sems,
 ):
     rows = vol_ref.shape[0]
     n_blocks, slots = pairs_ref.shape
@@ -66,10 +67,12 @@
         kv = got[:, :BLOCK].astype(jnp.bfloat16)
         kv_ref[at, :] = kv
         for b in range(chunk // BLOCK):
-            kvt_ref[c * (chunk // BLOCK) + b] = kv[b * BLOCK:(b + 1) * BLOCK].T
+            turned = kv[b * BLOCK:(b + 1) * BLOCK].T
+            kt_ref[c * (chunk // BLOCK) + b] = turned[:HD]
+            vt_ref[c * (chunk // BLOCK) + b] = turned[HD:]
     kept = [
         pltpu.make_async_copy(ref, hbm, out_sems.at[i])
-        for i, (ref, hbm) in enumerate(((kv_ref, kv_hbm), (kvt_ref, kvt_hbm), (q_ref, q_hbm)))
+        for i, (ref, hbm) in enumerate(((kv_ref, kv_hbm), (kt_ref, kt_hbm), (q_ref, q_hbm)))
     ]
     for copy in kept:
         copy.start()
@@ -87,7 +90,7 @@
         ]
         outs = []
         for b, some, p in zip(blocks, names, probs):
-            values = jnp.concatenate([kvt_ref[n, HD:] for n in some], axis=1)
+            values = jnp.concatenate([vt_ref[n] for n in some], axis=1)
             out_t = mm(values, p)
             both = jnp.concatenate([out_t, out_t], axis=0).T.astype(jnp.bfloat16)
             outs.append(both)
@@ -111,13 +114,13 @@
     smem = pl.BlockSpec(memory_space=pltpu.SMEM)
     hbm = pl.BlockSpec(memory_space=pl.ANY)
     flat = jax.ShapeDtypeStruct((rows, BLOCK), jnp.bfloat16)
-    square = jax.ShapeDtypeStruct((n_blocks, BLOCK, BLOCK), jnp.bfloat16)
+    turned = jax.ShapeDtypeStruct((n_blocks, HD, BLOCK), jnp.bfloat16)
     return pl.pallas_call(
         forward_kernel,
         out_shape=(
             jax.ShapeDtypeStruct((peers, rows // peers // 2, BLOCK), jnp.bfloat16),
             flat,
-            square,
+            turned,
             flat,
         ),
         in_specs=[smem] * 2 + [vmem, hbm],
@@ -125,7 +128,8 @@
         scratch_shapes=[
             pltpu.VMEM((rows, width), jnp.bfloat16),
             pltpu.VMEM(flat.shape, flat.dtype),
-            pltpu.VMEM(square.shape, square.dtype),
+            pltpu.VMEM(turned.shape, turned.dtype),
+            pltpu.VMEM(turned.shape, turned.dtype),
             pltpu.VMEM(flat.shape, flat.dtype),
             pltpu.SemaphoreType.DMA((CHUNKS,)),
             pltpu.SemaphoreType.DMA((3,)),
@@ -158,8 +162,8 @@
 
 
 def backward_kernel(
-    pairs_ref, valid_ref, do_hbm, kv_hbm, kvt_hbm, q_hbm, vol_hbm, wg_ref,
-    do_ref, kv_ref, kvt_ref, q_ref, vol_ref, acc_ref, dt_ref, sems,
+    pairs_ref, valid_ref, do_hbm, kv_hbm, kt_hbm, q_hbm, vol_hbm, wg_ref,
+    do_ref, kv_ref, kt_ref, q_ref, vol_ref, acc_ref, dt_ref, sems,
 ):
     width = vol_ref.shape[1]
     n_blocks, slots = pairs_ref.shape
@@ -167,7 +171,7 @@
     copies = [
         pltpu.make_async_copy(hbm, ref, sems.at[i])
         for i, (hbm, ref) in enumerate(
-            ((kv_hbm, kv_ref), (q_hbm, q_ref), (do_hbm, do_ref), (kvt_hbm, kvt_ref), (vol_hbm, vol_ref))
+            ((kv_hbm, kv_ref), (q_hbm, q_ref), (do_hbm, do_ref), (kt_hbm, kt_ref), (vol_hbm, vol_ref))
         )
     ]
     for copy in copies[:-1]:
@@ -193,7 +197,7 @@
             score_grad = (weighted - probs * row_dot).astype(jnp.bfloat16)
             sent.append((score_grad, probs.astype(jnp.bfloat16)))
         for b, some, pair in zip(blocks, names, sent):
-            keys = jnp.concatenate([kvt_ref[n, :HD] for n in some], axis=1)
+            keys = jnp.concatenate([kt_ref[n] for n in some], axis=1)
             dt_ref[BLOCK:, row(b)] = (mm(keys, pair[0]) * scale).astype(jnp.bfloat16)
         for some, pair, r in zip(names, sent, rhs):
             back = mm(jnp.concatenate(pair, axis=1), r)
@@ -211,7 +215,7 @@
     copies[-1].wait()
     owners = wg_ref.shape[0]
     mine = width // owners
-    part = 256
+    part = PART
     for n in range(width // part):
         got = mm(dt_ref[...], vol_ref[:, n * part:(n + 1) * part]).astype(jnp.bfloat16)
         kv_part = got[:BLOCK].T
@@ -223,7 +227,7 @@
             wg_ref[owner, mine:] = jnp.concatenate([q_rows[:mine // 2], q_rows[mine // 2:]], axis=1)
 
 
-def backward_call(pairs, valid, d_out, kv, kvt, q, vol, owners):
+def backward_call(pairs, valid, d_out, kv, kt, q, vol, owners):
     rows, width = vol.shape
     n_blocks = rows // BLOCK
     mine = width // owners
@@ -237,7 +241,7 @@
         scratch_shapes=[
             pltpu.VMEM((rows, BLOCK), jnp.bfloat16),
             pltpu.VMEM((rows, BLOCK), jnp.bfloat16),
-            pltpu.VMEM((n_blocks, BLOCK, BLOCK), jnp.bfloat16),
+            pltpu.VMEM((n_blocks, HD, BLOCK), jnp.bfloat16),
             pltpu.VMEM((rows, BLOCK), jnp.bfloat16),
             pltpu.VMEM((rows, width), jnp.bfloat16),
             pltpu.VMEM((n_blocks, BLOCK, BLOCK), jnp.float32),
@@ -249,7 +253,7 @@
             flops=12 * 10**9, bytes_accessed=20 * 2**20, transcendentals=n_blocks * 2**16
         ),
         name="backward",
-    )(pairs, valid, d_out, kv, kvt, q, vol)
+    )(pairs, valid, d_out, kv, kt, q, vol)
 
 
 def finish_kernel(att_ref, wg_ref, out_ref, total_ref):
@@ -309,9 +313,9 @@
     w = jnp.pad(w, ((0, 0), (0, HD)))
 
     pairs, valid = pairs[0, 0], valid[0, 0]
-    att, kv, kvt, q = forward_call(pairs, valid, w, gathered, peers)
+    att, kv, kt, q = forward_call(pairs, valid, w, gathered, peers)
     att = lax.all_to_all(att, "seq", split_axis=0, concat_axis=0, tiled=True)
-    wg = backward_call(pairs, valid, d_out, kv, kvt, q, gathered, owners)
+    wg = backward_call(pairs, valid, d_out, kv, kt, q, gathered, owners)
     wg, att = lax.optimization_barrier((wg, att))
     wg = lax.all_to_all(wg, "dp", split_axis=0, concat_axis=0, tiled=True)
     att, total = finish_call(att, wg, w_rows)

time: 129 us -> 128 us (level)
  no operation moved by 1% of the time
where the time goes in v7:
time: 128 us
  waiting for transfers between devices  32.5 us (25%)
  starting transfers between devices  26.6 us (21%)
  blocking collectives  24.6 us (19%)
  Pallas kernels  22.5 us (18%)
  between operations  14.1 us (11%)
  local copies, waits for them, and re-layouts  7.24 us (6%)
    all_to_all x1, blocking collectives, local(): wg = lax.all_to_all(wg, 'dp', split_axis=0, concat_axis=0, tiled=True)  24.6 us
    all_to_all x1, waiting for transfers between devices, local(): cot = lax.all_to_all(cot, 'seq', split_axis=0, concat_axis=0, tiled=True)  14 us
    all_to_all x1, waiting for transfers between devices, local(): w = lax.all_to_all(sent, 'dp', split_axis=0, concat_axis=0, tiled=True)  11.9 us
    all_to_all x1, starting transfers between devices, local(): cot = lax.all_to_all(cot, 'seq', split_axis=0, concat_axis=0, tiled=True)  11.8 us
    pallas_call x1, Pallas kernels, backward_call(): pl.pallas_call(backward_kernel, out_shape=jax.ShapeDtypeStruct((owners, m...  11.7 us
    all_to_all x1, starting transfers between devices, local(): w = lax.all_to_all(sent, 'dp', split_axis=0, concat_axis=0, tiled=True)  10.1 us
    pallas_call x1, Pallas kernels, forward_call(): pl.pallas_call(forward_kernel, out_shape=(jax.ShapeDtypeStruct((peers, ro...  9.62 us
    all_to_all x1, starting transfers between devices, local(): att = lax.all_to_all(att, 'seq', split_axis=0, concat_axis=0, tiled=True)  4.63 us
  transfers between devices with their start and end apart: 4, of which 4 were waited for; matrix products, arithmetic and copies ran while one was open for 5% of the time, Pallas kernels for 9%

profile of v7, /device:TPU:1, one launch (start us, length us, event | category | flops | bytes accessed | tf_op | source)
XLA Modules:
  0.0 127.5 jit_solution(5761671049713675680)
XLA Ops:
  7.2 0.0 copy-start
  7.2 0.0 copy-start.2
  7.2 0.0 copy-start.3
  7.2 0.0 all-gather.3.cloned.1.call-start
  7.2 0.7 all-gather.3.cloned.1.call-update
  7.9 1.2 copy.12
  9.1 0.3 reshape_squeeze.3
  9.4 0.1 copy.13
  9.6 1.0 copy.14
  10.5 11.8 %all-to-all-start = ((bf16[16,96,128]{2,1,0:T(8,128)(2,1)}), bf16[16,96,128]{2,1,0:T(8,128)(2,1)S(1)}, u32[]{:S(2)}, u32[]{:S(2)}) async-start(bf16[16,96,128]{2,1,0:T(8,128)(2,1)} %copy.14), calls=%async_computation | async-start | bytes 786432 | tf_op jit(solution)/shard_map/all_to_all | solution.py:303
  22.3 14.0 %all-to-all-done.cot_ref = bf16[16,96,128]{2,1,0:T(8,128)(2,1)S(1)} async-done(((bf16[16,96,128]{2,1,0:T(8,128)(2,1)}), bf16[16,96,128]{2,1,0:T(8,128)(2,1)S(1)}, u32[]{:S(2)}, u32[]{:S(2)}) %all-to-all-start) | async-done | bytes 393248 | tf_op jit(solution)/shard_map/all_to_all | solution.py:303
  36.4 0.0 copy-done
  36.4 0.1 constant_dynamic-slice_fusion.1
  36.4 0.1 constant_dynamic-slice_fusion
  36.6 0.1 broadcast_in_dim.10
  36.7 0.8 broadcast_in_dim.11
  37.5 10.1 %all-to-all-start.1 = ((bf16[32,48,128]{2,1,0:T(8,128)(2,1)}), bf16[32,48,128]{2,1,0:T(8,128)(2,1)S(1)}, u32[]{:S(2)}, u32[]{:S(2)}) async-start(bf16[32,48,128]{2,1,0:T(8,128)(2,1)} %broadcast_in_dim.11), calls=%async_computation.1 | async-start | bytes 786432 | tf_op jit(solution)/shard_map/all_to_all | solution.py:311
  47.5 0.0 copy-done.2
  47.5 0.7 copy.18.pairs_ref
  48.2 0.7 copy.19.valid_ref
  48.9 0.2 spread.1.do_hbm
  49.1 0.9 copy-done.1
  50.0 11.9 %all-to-all-done.1 = bf16[32,48,128]{2,1,0:T(8,128)(2,1)S(1)} async-done(((bf16[32,48,128]{2,1,0:T(8,128)(2,1)}), bf16[32,48,128]{2,1,0:T(8,128)(2,1)S(1)}, u32[]{:S(2)}, u32[]{:S(2)}) %all-to-all-start.1) | async-done | bytes 393248 | tf_op jit(solution)/shard_map/all_to_all | solution.py:311
  61.9 0.3 reshape.12
  62.3 1.0 pad.4.w_ref
  63.3 3.0 %all-gather.3.cloned.1.call-done = bf16[1,3072,1024]{2,1,0:T(8,128)(2,1)} async-done(((bf16[1,192,1024]{2,1,0:T(8,128)(2,1)}), bf16[1,3072,1024]{2,1,0:T(8,128)(2,1)}) %all-gather.3.cloned.1.call-update) | async-done | bytes 6291472 | tf_op jit(solution)/shard_map/all_gather | solution.py:300
  66.3 9.6 %forward.1 = (bf16[16,96,128]{2,1,0:T(8,128)(2,1)}, bf16[3072,128]{1,0:T(8,128)(2,1)}, bf16[24,64,128]{2,1,0:T(8,128)(2,1)}, bf16[3072,128]{1,0:T(8,128)(2,1)}) custom-call(s32[24,4]{1,0:T(8,128)} %copy.18.pairs_ref, s32[24,4]{1,0:T(8,128)} %copy.19.valid_ref, bf16[1024,256]{1,0:T(8,128)(2,1)} %pad.4.w_ref, bf16[3072,1024]{1,0:T(8,128)(2,1)} %bitcast.9), custom_call_target="tpu_custom_call" | custom-call | tf_op jit(solution)/shard_map/forward/pallas_call | solution.py:118
  75.9 4.6 %all-to-all-start.2 = ((bf16[16,96,128]{2,1,0:T(8,128)(2,1)}), bf16[16,96,128]{2,1,0:T(8,128)(2,1)S(1)}, u32[]{:S(2)}, u32[]{:S(2)}) async-start(bf16[16,96,128]{2,1,0:T(8,128)(2,1)} %get-tuple-element.17), calls=%async_computation.2 | async-start | bytes 786432 | tf_op jit(solution)/shard_map/all_to_all | solution.py:317
  80.6 11.7 %backward.1 = bf16[32,48,128]{2,1,0:T(8,128)(2,1)} custom-call(s32[24,4]{1,0:T(8,128)} %copy.18.pairs_ref, s32[24,4]{1,0:T(8,128)} %copy.19.valid_ref, bf16[3072,128]{1,0:T(8,128)(2,1)} %copy-done.1, bf16[3072,128]{1,0:T(8,128)(2,1)} %get-tuple-element.14.kv_hbm, bf16[24,64,128]{2,1,0:T(8,128)(2,1)} %get-tuple-element.15.kt_hbm, ...), custom_call_target="tpu_custom_call" | custom-call | flops 12000000000 | bytes 20971520 | tf_op jit(solution)/shard_map/backward/pallas_call | solution.py:236
  92.3 2.8 %all-to-all-done.2.att_ref = bf16[16,96,128]{2,1,0:T(8,128)(2,1)S(1)} async-done(((bf16[16,96,128]{2,1,0:T(8,128)(2,1)}), bf16[16,96,128]{2,1,0:T(8,128)(2,1)S(1)}, u32[]{:S(2)}, u32[]{:S(2)}) %all-to-all-start.2) | async-done | bytes 393248 | tf_op jit(solution)/shard_map/all_to_all | solution.py:317
  95.1 24.6 %all_to_all.20.wg_ref = bf16[32,48,128]{2,1,0:T(8,128)(2,1)S(1)} all-to-all(bf16[32,48,128]{2,1,0:T(8,128)(2,1)} %backward.1), channel_id=1, replica_groups=mesh['dp'=32,'seq'=16] {'dp'}, dimensions={0} | all-to-all | bytes 786432 | tf_op jit(solution)/shard_map/all_to_all | solution.py:320
  119.7 1.0 finish.1
  (4 shorter events, 0.0 us)
Async XLA Ops:
  7.2 29.2 %copy-start = (bf16[32,3,1024]{2,0,1:T(8,128)(2,1)S(1)}, bf16[32,3,1024]{2,0,1:T(8,128)(2,1)}, u32[]{:S(2)}) copy-start(bf16[32,3,1024]{2,0,1:T(8,128)(2,1)} %param.7) | copy-start | bytes 589828
  7.2 40.4 %copy-start.2 = (s32[1,1,24,4]{2,3,1,0:T(4,128)S(1)}, s32[1,1,24,4]{2,3,1,0:T(4,128)}, u32[]{:S(2)}) copy-start(s32[1,1,24,4]{2,3,1,0:T(4,128)} %param.8) | copy-start | bytes 1156
  7.2 41.0 %copy-start.3 = (s32[1,1,24,4]{2,3,1,0:T(4,128)S(1)}, s32[1,1,24,4]{2,3,1,0:T(4,128)}, u32[]{:S(2)}) copy-start(s32[1,1,24,4]{2,3,1,0:T(4,128)} %param.9) | copy-start | bytes 1156
  7.2 59.1 %all-gather.3.cloned.1.call-start = ((), (), s32[]{:S(2)}) async-start(), calls=%async_computation.4 | async-start | bytes 6684672 | tf_op jit(solution)/shard_map/all_gather | solution.py:300
  10.5 25.9 %all-to-all-start = ((bf16[16,96,128]{2,1,0:T(8,128)(2,1)}), bf16[16,96,128]{2,1,0:T(8,128)(2,1)S(1)}, u32[]{:S(2)}, u32[]{:S(2)}) async-start(bf16[16,96,128]{2,1,0:T(8,128)(2,1)} %copy.14), calls=%async_computation | async-start | bytes 786432 | tf_op jit(solution)/shard_map/all_to_all | solution.py:303
  37.5 24.5 %all-to-all-start.1 = ((bf16[32,48,128]{2,1,0:T(8,128)(2,1)}), bf16[32,48,128]{2,1,0:T(8,128)(2,1)S(1)}, u32[]{:S(2)}, u32[]{:S(2)}) async-start(bf16[32,48,128]{2,1,0:T(8,128)(2,1)} %broadcast_in_dim.11), calls=%async_computation.1 | async-start | bytes 786432 | tf_op jit(solution)/shard_map/all_to_all | solution.py:311
  49.1 0.9 copy-start.1
  75.9 19.2 %all-to-all-start.2 = ((bf16[16,96,128]{2,1,0:T(8,128)(2,1)}), bf16[16,96,128]{2,1,0:T(8,128)(2,1)S(1)}, u32[]{:S(2)}, u32[]{:S(2)}) async-start(bf16[16,96,128]{2,1,0:T(8,128)(2,1)} %get-tuple-element.17), calls=%async_computation.2 | async-start | bytes 786432 | tf_op jit(solution)/shard_map/all_to_all | solution.py:317
Sparse Core Ops, SparseCore 0:
  10.2 56.1 all-gather.2
